TPU v7x, 32 devices: a whole 2x2x4 slice. The times are simulated.
32 devices in a mesh: section: 2 (over x), dp: 4 (over z), tensor: 4 (over y, core).
Axes of the slice: x: 2, y: 2, z: 4, core: 2. Of those that a mesh axis runs over, the one named last changes fastest.
Arguments:
- hidden: bfloat16 [8, 1024, 768], P('dp', 'tensor'), may hold values from -6 to 6
- cotangent: bfloat16 [8, 1024, 768], P('dp', 'tensor'), may hold values from -6 to 6
- pair_lengths: int32 [8], P('dp'), may hold values from 256 to 1024, as said below
- query_lengths: int32 [8], P('dp'), may hold values from 1 to 256, as said below
- buckets: int32 [2047], replicated, may hold values from 0 to 31
- qkv_weight: bfloat16 [2, 768, 3, 768], P('section', None, None, 'tensor'), may hold values from -0.21875 to 0.21875
- qv_bias: float32 [2, 2, 768], P('section', None, 'tensor'), may hold values from -3 to 3
- out_weight: bfloat16 [2, 768, 768], P('section', 'tensor'), may hold values from -1.25 to 1.25
- up_weight: bfloat16 [2, 768, 3072], P('section', None, 'tensor'), may hold values from -0.21875 to 0.21875
- ffn_bias: float32 [2, 3072], P('section', 'tensor'), may hold values from -3 to 3
- down_weight: bfloat16 [2, 3072, 768], P('section', 'tensor'), may hold values from -0.109375 to 0.109375
- norm_gains: float32 [2, 2, 768], P('section'), may hold values from 0.5 to 1.5
- vectors: float32 [2, 4, 768], P('section'), may hold values from -3 to 3
- bias_table: float32 [2, 12, 64], P('section', 'tensor'), may hold values from -5 to 5
Outputs:
- edges: float32 [2, 8, 1024, 768], P('section', 'dp', 'tensor')
- qkv_weight_grad: float32 [2, 768, 3, 768], P('section', None, None, 'tensor')
- qv_bias_grad: float32 [2, 2, 768], P('section', None, 'tensor')
- out_weight_grad: float32 [2, 768, 768], P('section', 'tensor')
- up_weight_grad: float32 [2, 768, 3072], P('section', None, 'tensor')
- ffn_bias_grad: float32 [2, 3072], P('section', 'tensor')
- down_weight_grad: float32 [2, 3072, 768], P('section', 'tensor')
- gain_grad: float32 [2, 2, 768], P('section', None, 'tensor')
- vector_grad: float32 [2, 4, 768], P('section', None, 'tensor')
- table_grad: float32 [2, 12, 64], P('section', 'tensor')
Inputs may be any that keep to these rules, and one draw needn't show every extreme that they name: `pair_lengths`: in each group of 2 consecutive pairs one, drawn from the seed, has all 1024 tokens live. `query_lengths`: A query is never longer than the shortest pair.
All inputs are finite; a program needn't handle non-finite values.
Results may differ from a plain program's by a relative error of at most 0.019.
Values may be sent and summed in bfloat16 or wider, within the bound.
No kernel may reach another device: no remote copies, remote signals or barrier semaphores. Data moves between devices by JAX's collectives and lax.ppermute only.
A program may use at most 320 MiB of HBM per device.

v0:
```python
import functools

import jax
import jax.numpy as jnp
from jax import lax
from jax.experimental import pallas as pl
from jax.experimental.pallas import tpu as pltpu
from jax.sharding import PartitionSpec as P


f32 = jnp.float32
bf16 = jnp.bfloat16
EPS = 1e-05
HEAD = 64
NEG = -1e30
SWAP_Y = [(0, 2), (2, 0), (1, 3), (3, 1)]
SWAP_C = [(0, 1), (1, 0), (2, 3), (3, 2)]
NT = (((1,), (1,)), ((), ()))
TN = (((0,), (0,)), ((), ()))
NN = (((1,), (0,)), ((), ()))
KEY_BASE = (0, 512, 256, 768)
TILE_BASE = (0, 128, 512, 640)
STRIP = 1664
SPAN = STRIP + 128
MIB = 2**20


def cost(us, flops=0):
    return pl.CostEstimate(flops=flops, bytes_accessed=int(us * 3.4e6), transcendentals=0)


def dotf(a, b, dims=NN):
    return lax.dot_general(a, b, dims, preferred_element_type=f32)


def swap_y(value):
    return lax.ppermute(value, "tensor", SWAP_Y)


def swap_c(value):
    return lax.ppermute(value, "tensor", SWAP_C)


def make_strip(window_ref, h, kind, strip_ref):
    blocks = STRIP // 128
    lane = lax.broadcasted_iota(jnp.int32, (8, 128), 1)
    row = lax.broadcasted_iota(jnp.int32, (8, 128), 0)

    def rolled(first):
        seg = window_ref[0, h, kind : kind + 1, first : first + 128]
        seg = pltpu.roll(jnp.broadcast_to(seg, (8, 128)), 0, 1, stride=1, stride_axis=0)
        return [pltpu.roll(seg, 8 * q, 1) if q else seg for q in range(16)]

    high = rolled(128 * blocks)
    for a in range(blocks):
        low = rolled(128 * (blocks - 1 - a))
        for q in range(16):
            rows = slice(128 * a + 8 * q, 128 * a + 8 * q + 8)
            strip_ref[h, kind, rows, :] = jnp.where(lane >= row + 8 * q, high[q], low[q])
        high = low


def sum_strip(strip_ref, h, kind, held_ref):
    blocks = STRIP // 128
    lane = lax.broadcasted_iota(jnp.int32, (8, 128), 1)
    carry = jnp.zeros((8, 128), f32)
    for a in reversed(range(blocks)):
        low, high = jnp.zeros((8, 128), f32), jnp.zeros((8, 128), f32)
        for q in range(16):
            part = strip_ref[h, kind, 128 * a + 8 * q : 128 * a + 8 * q + 8, :]
            if q:
                part = pltpu.roll(part, 128 - 8 * q, 1)
            stays = lane < 128 - 8 * q
            high += jnp.where(stays, part, 0.0)
            low += jnp.where(stays, 0.0, part)
        first = 128 * (blocks - 1 - a)
        held_ref[0, h, kind, :, first : first + 128] = low + carry
        carry = high
    held_ref[0, h, kind, :, 128 * blocks : 128 * blocks + 128] = carry


def lane_mask(rows, which):
    lane = lax.broadcasted_iota(jnp.int32, (rows, 128), 1)
    return (lane < HEAD) if which == 0 else (lane >= HEAD)


def cross_mask(qlen, core, tile, kb):
    key_low = KEY_BASE[kb] == 0
    row_low = tile < 2
    if not key_low and not row_low:
        return None
    shape = (256, 128)
    if row_low:
        first = 256 * core + 128 * tile
        row_side = first + lax.broadcasted_iota(jnp.int32, shape, 1) < qlen
    if key_low:
        key_side = lax.broadcasted_iota(jnp.int32, shape, 0) < qlen
    if row_low and key_low:
        return row_side != key_side
    return row_side if row_low else key_side


def strip_rows(tile, kb):
    first = KEY_BASE[kb] - TILE_BASE[tile] + 640
    return slice(first, first + 256)


def score_block(info_ref, keys, query, strip_ref, h, ib, kb):
    qlen, core, plen = info_ref[0], info_ref[1], info_ref[2]
    raw = dotf(keys, query, NT)
    parts = []
    for u in (0, 1):
        tile = 2 * ib + u
        rows = strip_rows(tile, kb)
        bias = strip_ref[h, 0, rows, :]
        cross = cross_mask(qlen, core, tile, kb)
        if cross is not None:
            bias = jnp.where(cross, strip_ref[h, 1, rows, :], bias)
        parts.append(raw[:, 128 * u : 128 * u + 128] + bias)
    scores = jnp.concatenate(parts, 1)
    if kb != 0:
        live = KEY_BASE[kb] + lax.broadcasted_iota(jnp.int32, (256, 256), 0) < plen
        scores = jnp.where(live, scores, NEG)
    return scores


def whole(core, own, other):
    return jnp.concatenate([jnp.where(core == 0, own, other), jnp.where(core == 0, other, own)], 0)


def forward_kernel(
    info_ref, q_ref, k_ref, v_ref, ko_ref, vo_ref, win_ref, o_ref, lse_ref, strip_ref
):
    core = info_ref[1]
    for h in range(2):
        for kind in range(2):
            make_strip(win_ref, h, kind, strip_ref)
    keys = whole(core, k_ref[...], ko_ref[...])
    values = whole(core, v_ref[...], vo_ref[...])
    one = jnp.ones_like(values)
    turned = [jnp.where(lane_mask(1024, h), values, one).T for h in range(2)]
    for ib in range(2):
        rows = slice(256 * ib, 256 * ib + 256)
        query = q_ref[rows, :] * jnp.asarray(0.125, bf16)
        outs = []
        for h in range(2):
            one = jnp.where(lane_mask(256, h), query, jnp.zeros_like(query))
            blocks = [
                score_block(
                    info_ref, keys[256 * kb : 256 * kb + 256], one, strip_ref, h, ib, kb
                )
                for kb in range(4)
            ]
            top = functools.reduce(
                jnp.maximum, [jnp.max(s, 0, keepdims=True) for s in blocks]
            )
            mixed = None
            for kb in range(4):
                probs = jnp.exp(blocks[kb] - top).astype(bf16)
                part = dotf(turned[h][:, 256 * kb : 256 * kb + 256], probs)
                mixed = part if mixed is None else mixed + part
            total = mixed[HEAD * (1 - h) : HEAD * (1 - h) + 1, :]
            lse_ref[0, h : h + 1, rows] = top + jnp.log(total)
            outs.append(mixed[HEAD * h : HEAD * h + HEAD, :] / total)
        o_ref[rows, :] = jnp.concatenate(outs, 0).T.astype(bf16)


def kv_blocks(groups, first=0):
    half = groups // 2
    return [
        pl.BlockSpec((512, 128), lambda i, s: (0, i + first)),
        pl.BlockSpec((512, 128), lambda i, s: (0, i + first + groups)),
        pl.BlockSpec((512, 128), lambda i, s: (0, (i + first + half) % groups)),
        pl.BlockSpec((512, 128), lambda i, s: (0, (i + first + half) % groups + groups)),
    ]


def attend_forward(info, q, kv, kv_other, window):
    groups = q.shape[1] // 128
    block = pl.BlockSpec((512, 128), lambda i, s: (0, i))
    return pl.pallas_call(
        forward_kernel,
        grid_spec=pltpu.PrefetchScalarGridSpec(
            num_scalar_prefetch=1,
            grid=(groups,),
            in_specs=[
                block,
                *kv_blocks(groups),
                pl.BlockSpec((1, 2, 2, SPAN), lambda i, s: (i, 0, 0, 0)),
            ],
            out_specs=[block, pl.BlockSpec((1, 2, 512), lambda i, s: (i, 0, 0))],
            scratch_shapes=[pltpu.VMEM((2, 2, STRIP, 128), f32)],
        ),
        out_shape=[
            jax.ShapeDtypeStruct((512, 128 * groups), bf16),
            jax.ShapeDtypeStruct((groups, 2, 512), f32),
        ],
        compiler_params=pltpu.CompilerParams(vmem_limit_bytes=40 * MIB),
        cost_estimate=cost(17),
        name="attend_forward",
    )(info, q, kv, kv, kv_other, kv_other, window)


def backward_kernel(with_table, *refs):
    info_ref, q_ref, k_ref, v_ref, ko_ref, vo_ref, do_ref, lse_ref, win_ref = refs[:9]
    dq_ref, dk_ref, dv_ref, dko_ref, dvo_ref, *rest = refs[9:]
    qlen, core = info_ref[0], info_ref[1]
    strip_ref = rest[-1]
    for h in range(2):
        for kind in range(2):
            make_strip(win_ref, h, kind, strip_ref)
    if with_table:
        held_ref, strip_grad_ref = rest[:2]
        strip_grad_ref[...] = jnp.zeros_like(strip_grad_ref)
    keys = whole(core, k_ref[...], ko_ref[...])
    values = whole(core, v_ref[...], vo_ref[...])
    keys_turned = keys.T
    key_grads = [jnp.zeros((256, 128), f32) for _ in range(4)]
    value_grads = [jnp.zeros((256, 128), f32) for _ in range(4)]
    for ib in range(2):
        rows = slice(256 * ib, 256 * ib + 256)
        query = q_ref[rows, :] * jnp.asarray(0.125, bf16)
        grad = do_ref[rows, :]
        query_grads = []
        for h in range(2):
            mask = lane_mask(256, h)
            one = jnp.where(mask, query, jnp.zeros_like(query))
            grad_one = jnp.where(mask, grad, jnp.zeros_like(grad))
            log_total = lse_ref[0, h : h + 1, rows]
            probs, terms = [], []
            row_term = 0.0
            for kb in range(4):
                kr = slice(256 * kb, 256 * kb + 256)
                scores = score_block(info_ref, keys[kr], one, strip_ref, h, ib, kb)
                part = jnp.exp(scores - log_total)
                term = part * dotf(values[kr], grad_one, NT)
                row_term = row_term + jnp.sum(term, 0, keepdims=True)
                value_grads[kb] = value_grads[kb] + dotf(part.astype(bf16), grad_one)
                probs.append(part)
                terms.append(term)
            flat = None
            for kb in range(4):
                kr = slice(256 * kb, 256 * kb + 256)
                grad_scores = (terms[kb] - probs[kb] * row_term).astype(bf16)
                key_grads[kb] = key_grads[kb] + dotf(grad_scores, one)
                part = dotf(keys_turned[:, kr], grad_scores)
                flat = part if flat is None else flat + part
                if with_table:
                    for u in (0, 1):
                        tile = 2 * ib + u
                        where = strip_rows(tile, kb)
                        part = grad_scores[:, 128 * u : 128 * u + 128].astype(f32)
                        strip_grad_ref[h, 0, where, :] += part
                        cross = cross_mask(qlen, core, tile, kb)
                        if cross is not None:
                            strip_grad_ref[h, 1, where, :] += jnp.where(cross, part, 0.0)
            query_grads.append(flat[HEAD * h : HEAD * h + HEAD, :])
        dq_ref[rows, :] = (jnp.concatenate(query_grads, 0).T * 0.125).astype(bf16)
    for grads, own_ref, other_ref in (
        (key_grads, dk_ref, dko_ref),
        (value_grads, dv_ref, dvo_ref),
    ):
        first = jnp.concatenate(grads[:2], 0)
        second = jnp.concatenate(grads[2:], 0)
        own_ref[...] = jnp.where(core == 0, first, second)
        other_ref[...] = jnp.where(core == 0, second, first).astype(bf16)
    if with_table:
        for h in range(2):
            for kind in range(2):
                sum_strip(strip_grad_ref, h, kind, held_ref)


def attend_backward(info, q, kv, kv_other, grad, lse, window, with_table, first, count):
    groups = q.shape[1] // 128
    block = pl.BlockSpec((512, 128), lambda i, s: (0, i + first))
    rows = lambda kind: jax.ShapeDtypeStruct((512, 128 * count), kind)
    out_specs = [pl.BlockSpec((512, 128), lambda i, s: (0, i))] * 5
    out_shape = [rows(bf16), rows(f32), rows(f32), rows(bf16), rows(bf16)]
    scratch = [pltpu.VMEM((2, 2, STRIP, 128), f32)]
    if with_table:
        out_specs.append(pl.BlockSpec((1, 2, 2, 8, SPAN), lambda i, s: (i, 0, 0, 0, 0)))
        out_shape.append(jax.ShapeDtypeStruct((count, 2, 2, 8, SPAN), f32))
        scratch = scratch * 2
    return pl.pallas_call(
        functools.partial(backward_kernel, with_table),
        grid_spec=pltpu.PrefetchScalarGridSpec(
            num_scalar_prefetch=1,
            grid=(count,),
            in_specs=[
                block,
                *kv_blocks(groups, first),
                block,
                pl.BlockSpec((1, 2, 512), lambda i, s: (i + first, 0, 0)),
                pl.BlockSpec((1, 2, 2, SPAN), lambda i, s: (i + first, 0, 0, 0)),
            ],
            out_specs=out_specs,
            scratch_shapes=scratch,
        ),
        out_shape=out_shape,
        compiler_params=pltpu.CompilerParams(vmem_limit_bytes=48 * MIB),
        cost_estimate=cost(30),
        name="attend_backward",
    )(info, q, kv, kv, kv_other, kv_other, grad, lse, window)


def norm_parts(values):
    centre = jnp.mean(values, -1, keepdims=True)
    centred = values - centre
    scale = lax.rsqrt(jnp.mean(centred * centred, -1, keepdims=True) + EPS)
    return centred * scale, scale


def norm_back(grad, gain, normal, scale):
    scaled = grad * gain
    return scale * (
        scaled
        - jnp.mean(scaled, -1, keepdims=True)
        - normal * jnp.mean(scaled * normal, -1, keepdims=True)
    )


def normal_cdf(units):
    size = jnp.abs(units)
    t = 1.0 / (1.0 + (0.3275911 * 0.5**0.5) * size)
    bell = jnp.exp(-0.5 * units * units)
    poly = 0.5 * 1.061405429
    for coef in (-1.453152027, 1.421413741, -0.284496736, 0.254829592):
        poly = poly * t + 0.5 * coef
    tail = poly * t * bell
    return jnp.where(units >= 0, 1.0 - tail, tail), bell


def ffn_forward_kernel(
    keep,
    att_ref,
    x_ref,
    out_ref,
    up_ref,
    up_far_ref,
    down_ref,
    down_far_ref,
    bias_ref,
    gain_ref,
    shift_ref,
    result_ref,
    *rest,
):
    if keep:
        (
            low_ref,
            active_ref,
            slope_ref,
            n_one_ref,
            s_one_ref,
            n_two_ref,
            s_two_ref,
            normed_low,
            total,
        ) = rest
    else:
        normed_low, total = rest
    i = pl.program_id(0)

    @pl.when(i == 0)
    def _():
        before = x_ref[...].astype(f32) + (dotf(att_ref[...], out_ref[...]) + shift_ref[0:1, :])
        normal, scale = norm_parts(before)
        normed = normal * gain_ref[0:1, :] + shift_ref[1:2, :]
        normed_low[...] = normed.astype(bf16)
        total[...] = normed + shift_ref[2:3, :]
        if keep:
            n_one_ref[...] = normal
            s_one_ref[...] = scale
            low_ref[...] = normed_low[...]

    near = i < 2
    width = up_ref.shape[2]
    step = 256
    add = None
    for first in range(0, width, step):
        cols = slice(first, first + step)
        up = jnp.where(near, up_ref[0, :, cols], up_far_ref[0, :, cols])
        down = jnp.where(near, down_ref[0, cols, :], down_far_ref[0, cols, :])
        units = dotf(normed_low[...], up) + bias_ref[0, :, cols]
        side, bell = normal_cdf(units)
        active = (units * side).astype(bf16)
        if keep:
            active_ref[:, cols] = active
            slope_ref[:, cols] = (side + units * bell * 0.3989422804014327).astype(bf16)
        part = dotf(active, down)
        add = part if add is None else add + part
    total[...] += add

    @pl.when(i == pl.num_programs(0) - 1)
    def _():
        normal, scale = norm_parts(total[...])
        result = normal * gain_ref[1:2, :] + shift_ref[3:4, :]
        result_ref[...] = result.astype(result_ref.dtype)
        if keep:
            n_two_ref[...] = normal
            s_two_ref[...] = scale


def near_far(rows, cols):
    return [
        pl.BlockSpec((1, rows, cols), lambda i: (jnp.minimum(i, 1), 0, 0)),
        pl.BlockSpec((1, rows, cols), lambda i: (jnp.maximum(i - 2, 0), 0, 0)),
    ]


def ffn_forward(w, attended, inputs, keep, part=0, parts=1):
    rows, model = inputs.shape
    rows //= parts
    width = w["up"][0].shape[2]
    all_of = lambda *shape: pl.BlockSpec(shape, lambda i: (0,) * len(shape))
    by_step = pl.BlockSpec((rows, width), lambda i: (0, i))
    shape = lambda cols, kind: jax.ShapeDtypeStruct((rows, cols), kind)
    out_specs = [all_of(rows, model)]
    out_shape = [shape(model, f32 if keep else bf16)]
    if keep:
        out_specs += [all_of(rows, model), by_step, by_step]
        out_specs += [all_of(rows, model), all_of(rows, 1)] * 2
        out_shape += [shape(model, bf16), shape(4 * width, bf16), shape(4 * width, bf16)]
        out_shape += [shape(model, f32), shape(1, f32)] * 2
    flops = 2 * rows * model * (model + 8 * width)
    return pl.pallas_call(
        functools.partial(ffn_forward_kernel, keep),
        grid=(4,),
        in_specs=[
            pl.BlockSpec((rows, model), lambda i: (part, 0)),
            pl.BlockSpec((rows, model), lambda i: (part, 0)),
            all_of(model, model),
            *near_far(model, width),
            *near_far(width, model),
            pl.BlockSpec((1, 1, width), lambda i: (i, 0, 0)),
            all_of(2, model),
            all_of(4, model),
        ],
        out_specs=out_specs,
        out_shape=out_shape,
        scratch_shapes=[pltpu.VMEM((rows, model), bf16), pltpu.VMEM((rows, model), f32)],
        compiler_params=pltpu.CompilerParams(vmem_limit_bytes=48 * MIB),
        cost_estimate=cost(15),
        name="ffn_forward",
    )(
        attended,
        inputs,
        w["out"],
        *w["up"],
        *w["down"],
        w["up_bias"],
        w["gains"],
        w["shifts"],
    )


def top_back_kernel(gy_ref, n_two_ref, s_two_ref, gain_ref, after_ref, second_ref, sums_ref):
    gy = gy_ref[...].astype(f32)
    after = norm_back(gy, gain_ref[1:2, :], n_two_ref[...], s_two_ref[...])
    low = after.astype(bf16)
    after_ref[...] = after
    second_ref[...] = low
    sums_ref[0:1, :] = jnp.sum(gy * n_two_ref[...], 0, keepdims=True)
    sums_ref[1:2, :] = jnp.sum(low.astype(f32), 0, keepdims=True)
    sums_ref[2:3, :] = jnp.sum(gy, 0, keepdims=True)
    sums_ref[3:8, :] = jnp.zeros((5, sums_ref.shape[1]), f32)


def top_back(w, saved, grad_y):
    rows, model = grad_y.shape
    return pl.pallas_call(
        top_back_kernel,
        out_shape=[
            jax.ShapeDtypeStruct((rows, model), f32),
            jax.ShapeDtypeStruct((rows, model), bf16),
            jax.ShapeDtypeStruct((8, model), f32),
        ],
        compiler_params=pltpu.CompilerParams(vmem_limit_bytes=20 * MIB),
        cost_estimate=cost(2),
        name="top_back",
    )(grad_y, saved["n_two"], saved["s_two"], w["gains"])


def ffn_backward_kernel(deps, *refs):
    (
        after_ref,
        second_ref,
        slope_ref,
        n_one_ref,
        s_one_ref,
        out_ref,
        up_ref,
        up_far_ref,
        down_ref,
        down_far_ref,
        gain_ref,
    ) = refs[:11]
    hidden_ref, before_ref, branch_ref, att_ref, sums_ref, hidden_sums_ref, total = refs[11 + deps :]
    i = pl.program_id(0)

    def add_up(value):
        return jnp.sum(value, 0, keepdims=True)

    @pl.when(i == 0)
    def _():
        total[...] = after_ref[...]

    near = i < 2
    width = up_ref.shape[2]
    step = 256
    add = None
    for first in range(0, width, step):
        cols = slice(first, first + step)
        up = jnp.where(near, up_ref[0, :, cols], up_far_ref[0, :, cols])
        down = jnp.where(near, down_ref[0, cols, :], down_far_ref[0, cols, :])
        active = dotf(second_ref[...], down, NT)
        hidden = (active * slope_ref[:, cols].astype(f32)).astype(bf16)
        hidden_ref[:, cols] = hidden
        hidden_sums_ref[0, :, cols] = add_up(hidden.astype(f32))
        part = dotf(hidden, up, NT)
        add = part if add is None else add + part
    total[...] += add

    @pl.when(i == pl.num_programs(0) - 1)
    def _():
        normed = total[...]
        before = norm_back(normed, gain_ref[0:1, :], n_one_ref[...], s_one_ref[...])
        low = before.astype(bf16)
        before_ref[...] = before
        branch_ref[...] = low
        att_ref[...] = dotf(low, out_ref[...], NT).astype(bf16)
        sums_ref[0:1, :] = add_up(normed * n_one_ref[...])
        sums_ref[1:2, :] = add_up(low.astype(f32))
        sums_ref[2:3, :] = add_up(normed)
        sums_ref[3:8, :] = jnp.zeros((5, sums_ref.shape[1]), f32)


def ffn_backward(w, saved, after, second, deps=()):
    rows, model = after.shape
    width = w["up"][0].shape[2]
    all_of = lambda *shape: pl.BlockSpec(shape, lambda i: (0,) * len(shape))
    by_step = pl.BlockSpec((rows, width), lambda i: (0, i))
    by_block = pl.BlockSpec((1, 1, width), lambda i: (i, 0, 0))
    shape = lambda cols, kind: jax.ShapeDtypeStruct((rows, cols), kind)
    whole_rows = all_of(rows, model)
    return pl.pallas_call(
        functools.partial(ffn_backward_kernel, len(deps)),
        grid=(4,),
        in_specs=[
            whole_rows,
            whole_rows,
            by_step,
            whole_rows,
            all_of(rows, 1),
            all_of(model, model),
            *near_far(model, width),
            *near_far(width, model),
            all_of(2, model),
            *[pl.BlockSpec(memory_space=pl.ANY)] * len(deps),
        ],
        out_specs=[by_step, whole_rows, whole_rows, whole_rows, all_of(8, model), by_block],
        out_shape=[
            shape(4 * width, bf16),
            shape(model, f32),
            shape(model, bf16),
            shape(model, bf16),
            jax.ShapeDtypeStruct((8, model), f32),
            jax.ShapeDtypeStruct((4, 1, width), f32),
        ],
        scratch_shapes=[pltpu.VMEM((rows, model), f32)],
        compiler_params=pltpu.CompilerParams(vmem_limit_bytes=48 * MIB),
        cost_estimate=cost(15),
        name="ffn_backward",
    )(
        after,
        second,
        saved["slope"],
        saved["n_one"],
        saved["s_one"],
        w["out"],
        *w["up"],
        *w["down"],
        w["gains"],
        *deps,
    )


def weight_grad_kernel(l_ref, lo_ref, r_ref, ro_ref, o_ref):
    total = dotf(l_ref[...], r_ref[...], TN) + dotf(lo_ref[...], ro_ref[...], TN)
    o_ref[...] = total.astype(o_ref.dtype)


def weight_grad(left, left_far, right, right_far, kind, left_cols, right_cols):
    rows = left.shape[0]
    lf, ln, lw = left_cols
    rf, rn, rw = right_cols
    return pl.pallas_call(
        weight_grad_kernel,
        grid=(rn, ln),
        in_specs=[
            pl.BlockSpec((rows, lw), lambda j, i: (0, lf + i)),
            pl.BlockSpec((rows, lw), lambda j, i: (0, lf + i)),
            pl.BlockSpec((rows, rw), lambda j, i: (0, rf + j)),
            pl.BlockSpec((rows, rw), lambda j, i: (0, rf + j)),
        ],
        out_specs=pl.BlockSpec((lw, rw), lambda j, i: (i, j)),
        out_shape=jax.ShapeDtypeStruct((ln * lw, rn * rw), kind),
        compiler_params=pltpu.CompilerParams(vmem_limit_bytes=40 * MIB),
        cost_estimate=cost(4),
        name="weight_grad",
    )(left, left_far, right, right_far)


def split_grad_kernel(l_ref, lo_ref, r_ref, ro_ref, kept_ref, sent_ref):
    total = dotf(l_ref[...], r_ref[...], TN) + dotf(lo_ref[...], ro_ref[...], TN)
    half = total.shape[0] // 2
    kept_ref[...] = total[:half]
    sent_ref[...] = total[half:].astype(bf16)


def split_grad(left, left_far, right, right_far, width):
    rows, model = right.shape
    count = left_far.shape[1] // width
    left_block = pl.BlockSpec((rows, width), lambda i: (0, i))
    right_block = pl.BlockSpec((rows, model), lambda i: (0, 0))
    made = pl.BlockSpec((width // 2, model), lambda i: (i, 0))
    shape = (count * width // 2, model)
    return pl.pallas_call(
        split_grad_kernel,
        grid=(count,),
        in_specs=[left_block, left_block, right_block, right_block],
        out_specs=[made, made],
        out_shape=[jax.ShapeDtypeStruct(shape, f32), jax.ShapeDtypeStruct(shape, bf16)],
        compiler_params=pltpu.CompilerParams(vmem_limit_bytes=40 * MIB),
        cost_estimate=cost(4),
        name="split_grad",
    )(left, left_far, right, right_far)


def input_back_kernel(
    q_ref,
    k_ref,
    k_came_ref,
    v_ref,
    v_came_ref,
    before_ref,
    w_ref,
    near_ref,
    far_ref,
    grad_ref,
    low_ref,
    sums_ref,
    mixed,
    total,
):
    i = pl.program_id(0)
    which = i // 2

    @pl.when(i == 0)
    def _():
        total[...] = before_ref[...]

    @pl.when(which == 0)
    def _():
        mixed[...] = q_ref[...]

    @pl.when(which == 1)
    def _():
        mixed[...] = (k_ref[...] + k_came_ref[...].astype(f32)).astype(bf16)

    @pl.when(which == 2)
    def _():
        mixed[...] = (v_ref[...] + v_came_ref[...].astype(f32)).astype(bf16)

    @pl.when(i % 2 == 0)
    def _():
        near_ref[...] = mixed[...]

    @pl.when(i % 2 == 1)
    def _():
        far_ref[...] = mixed[...]

    sums_ref[0] = jnp.sum(mixed[...].astype(f32), 0, keepdims=True)
    total[...] += dotf(mixed[...], w_ref[...])

    @pl.when(i == 5)
    def _():
        grad_ref[...] = total[...]
        low_ref[...] = total[...].astype(bf16)


def input_back(grads, came, before, qkv, part=0, parts=1):
    q, k, v = grads
    k_came, v_came = came
    rows, model = q.shape
    rows //= parts
    half = model // 2

    def at(first, turn=False):
        def index(i):
            step = jnp.clip(i - first, 0, 1)
            return part, (1 - step if turn else step)

        return pl.BlockSpec((rows, half), index)

    split = pl.BlockSpec((rows, half), lambda i: (0, i // 2))
    full = pl.BlockSpec((rows, model), lambda i: (0, 0))
    return pl.pallas_call(
        input_back_kernel,
        grid=(6,),
        in_specs=[
            at(0),
            at(2),
            at(2, True),
            at(4),
            at(4, True),
            pl.BlockSpec((rows, model), lambda i: (part, 0)),
            pl.BlockSpec((half, model), lambda i: (i, 0)),
        ],
        out_specs=[split, split, full, full, pl.BlockSpec((1, 1, half), lambda i: (i, 0, 0))],
        out_shape=[
            jax.ShapeDtypeStruct((rows, 3 * half), bf16),
            jax.ShapeDtypeStruct((rows, 3 * half), bf16),
            jax.ShapeDtypeStruct((rows, model), f32),
            jax.ShapeDtypeStruct((rows, model), bf16),
            jax.ShapeDtypeStruct((6, 1, half), f32),
        ],
        scratch_shapes=[pltpu.VMEM((rows, half), bf16), pltpu.VMEM((rows, model), f32)],
        compiler_params=pltpu.CompilerParams(vmem_limit_bytes=40 * MIB),
        cost_estimate=cost(6),
        name="input_back",
    )(q, k, k_came, v, v_came, before, qkv)


def body(
    hidden,
    cotangent,
    pair_lengths,
    query_lengths,
    buckets,
    qkv_weight,
    qv_bias,
    out_weight,
    up_weight,
    ffn_bias,
    down_weight,
    norm_gains,
    vectors,
    bias_table,
):
    leading = lax.axis_index("section") == 0
    place = lax.axis_index("tensor")
    y, core = place // 2, place % 2
    plane = lax.axis_index("dp")
    planes = lax.axis_size("dp")
    odd = plane % 2
    local, model = hidden.shape[1], hidden.shape[2]
    total = 4 * local
    cols = qkv_weight.shape[3]
    width = up_weight.shape[2]
    heads = bias_table.shape[1]
    kinds = bias_table.shape[2] // 2
    near, far = slice(0, 2 * cols), slice(2 * cols, 4 * cols)

    def swap_z(value):
        return lax.ppermute(value, "dp", [(i, i ^ 1) for i in range(planes)])

    def mine(array):
        return lax.dynamic_index_in_dim(array, y, 0, keepdims=False)

    def theirs(array):
        return lax.dynamic_index_in_dim(array, 1 - y, 0, keepdims=False)

    def in_order(first, own, came, axis=0):
        return jnp.concatenate(
            [jnp.where(first, own, came), jnp.where(first, came, own)], axis
        )

    def own_half(block, axis=0):
        half = block.shape[axis] // 2
        return lax.dynamic_slice_in_dim(block, half * odd, half, axis)

    def edge_blocks(value):
        return value.reshape(2, local, model)

    def stage(work):
        shapes = jax.eval_shape(work)
        return lax.cond(
            pair_lengths[0] > 0,
            work,
            lambda: jax.tree.map(lambda leaf: jnp.zeros(leaf.shape, leaf.dtype), shapes),
        )

    qkv_own = qkv_weight[0].transpose(1, 2, 0)
    out_own, up_own, down_own = out_weight[0], up_weight[0], down_weight[0]
    x_sent, qkv_sent = theirs(hidden), own_half(qkv_own, 1)
    small = jnp.concatenate([qv_bias[0].reshape(-1), ffn_bias[0], bias_table[0].reshape(-1)])

    def first_stage():
        return (
            swap_y(x_sent),
            swap_y(small),
            swap_y(qkv_sent),
            own_half(out_own),
            own_half(up_own),
            own_half(down_own),
        )

    x_came, small_y, qkv_y, out_sent, up_sent, down_sent = stage(first_stage)
    onehot = (buckets[:, None] == jnp.arange(kinds, dtype=jnp.int32)[None, :]).astype(f32)
    onehot = jnp.pad(onehot, ((1, 0), (0, 0)))
    onehot = lax.dynamic_slice_in_dim(onehot, 256 * core, SPAN, 0)

    def second_stage():
        two = jnp.stack([small, small_y])
        four = jnp.concatenate([two, swap_c(two)])
        table = four[:, 2 * cols + width :].reshape(8 * heads, kinds)
        window = lax.dot_general(table, onehot, NT, precision=lax.Precision.HIGHEST)
        window = window.reshape(2 * heads, 2, 2, SPAN)
        return swap_y(out_sent), swap_y(up_sent), swap_z(qkv_y), four, window

    out_y, up_y, qkv_z, small, window = stage(second_stage)
    qv_all = small[:, : 2 * cols].reshape(4, 2, cols)
    q_bias = qv_all[:, 0].reshape(-1)
    kv_bias = jnp.concatenate([jnp.zeros((model,), f32), qv_all[:, 1].reshape(-1)])
    info = jnp.stack([mine(query_lengths), core, mine(pair_lengths)]).astype(jnp.int32)
    w = dict(
        up_bias=small[:, 2 * cols : 2 * cols + width].reshape(4, 1, width),
        gains=norm_gains[0],
        shifts=vectors[0],
    )

    def project(inputs, qkv):
        mixed = dotf(inputs, qkv, NT)
        kv = (mixed[:, model:] + kv_bias).astype(bf16)
        return (mixed[:, :model] + q_bias).astype(bf16), kv

    def third_stage():
        x0 = in_order(y == 0, mine(hidden), x_came)
        qkv = jnp.concatenate([qkv_own, in_order(odd == 0, qkv_y, qkv_z, 1)], 1)
        qkv = jnp.concatenate([qkv, swap_c(qkv)], 1).reshape(3 * model, model)
        q, kv = project(x0, qkv)
        kv_other = swap_c(kv)
        attended, _ = attend_forward(info, q, kv, kv_other, window)
        return x0, qkv, attended, swap_z(out_y), swap_z(up_y), swap_y(down_sent)

    x0, qkv, attended, out_z, up_z, down_y = stage(third_stage)

    def fourth_stage():
        out = jnp.concatenate([out_own, in_order(odd == 0, out_y, out_z)], 0)
        up = jnp.stack([up_own, in_order(odd == 0, up_y, up_z)])
        return jnp.concatenate([out, swap_c(out)], 0), up, swap_c(up), swap_z(down_y)

    w["out"], up, up_far, down_z = stage(fourth_stage)
    w["up"] = up, up_far

    def fifth_stage():
        down = jnp.stack([down_own, in_order(odd == 0, down_y, down_z)])
        return down, swap_c(down)

    w["down"] = stage(fifth_stage)

    def to_next(value):
        return lax.ppermute(value, "section", [(0, 1)])

    def to_last(value):
        return lax.ppermute(value, "section", [(1, 0)])

    middle = ffn_forward(w, attended, x0, False, 0, 2)[0]
    came_a, middle = stage(
        lambda: (to_next(middle), ffn_forward(w, attended, x0, False, 1, 2)[0])
    )
    x_a = jnp.where(leading, x0[:local], came_a)
    came_b, (q_a, kv_a) = stage(lambda: (to_next(middle), project(x_a, qkv)))

    def seventh_stage():
        x_b = jnp.where(leading, x0[local:], came_b)
        q_b, kv_b = project(x_b, qkv)
        kv = jnp.concatenate([kv_a, kv_b], 0)
        kv_other = swap_c(kv)
        x1, q = jnp.concatenate([x_a, x_b], 0), jnp.concatenate([q_a, q_b], 0)
        return x1, q, kv, kv_other

    x1, q, kv, kv_other = stage(seventh_stage)
    top_sent = theirs(cotangent)

    def eighth_stage():
        attended, lse = attend_forward(info, q, kv, kv_other, window)
        return swap_y(top_sent), swap_c(x1), attended, lse

    top_came, inputs_far, attended, lse = stage(eighth_stage)
    grad_top = in_order(y == 0, mine(cotangent), top_came)
    result, normed_low, active, slope, n_one, s_one, n_two, s_two = ffn_forward(
        w, attended, x1, True
    )
    saved = dict(slope=slope, n_one=n_one, s_one=s_one, n_two=n_two, s_two=s_two)

    def dense_back(after, second):
        names = ("hidden", "before", "branch", "attended", "low_sums", "hidden_sums")
        return dict(zip(names, ffn_backward(w, saved, after, second)))

    def attention_back(grads, table, first, count):
        return attend_backward(
            info, q, kv, kv_other, grads["attended"], lse, window, table, first, count
        )

    after, second, top_sums = top_back(w, saved, grad_top)

    def ninth_stage():
        return (
            swap_c(normed_low),
            swap_c(active[:, 2 * width :]),
            swap_c(attended[:, far]),
            dense_back(after, second),
        )

    normed_far, active_far, attended_far, grads = stage(ninth_stage)
    *qkv_grads, k_far, v_far = attention_back(grads, False, 0, 6)
    came = stage(lambda: (swap_c(k_far), swap_c(v_far)))

    def back(part, parts):
        return input_back(qkv_grads, came, grads["before"], qkv, part, parts)

    grad_a = back(0, 2)[3]
    came_a, grad_b = stage(lambda: (to_last(grad_a), back(1, 2)[3]))
    came_b = stage(lambda: to_last(grad_b))
    grad_y = jnp.where(leading, jnp.concatenate([came_a, came_b], 0), grad_top)

    thirds = width // 3

    def down_grad(kind, first):
        return weight_grad(
            active, active_far, second, second_far, kind, (first, 3, thirds), (0, 1, model)
        )

    def up_grad(kind, first):
        return weight_grad(
            normed_low, normed_far, hidden, hidden_far, kind, (0, 3, thirds), (first, 1, width)
        )

    def hops(value):
        if planes != 4:
            return lax.psum(value, "dp")
        value = value + lax.ppermute(value, "dp", [(0, 1), (3, 2)])
        value = value + lax.ppermute(value, "dp", [(1, 2), (2, 1)])
        back = lax.ppermute(value, "dp", [(1, 0), (2, 3)])
        return jnp.where((plane == 1) | (plane == 2), value, back)

    after, second, top_sums = top_back(w, saved, grad_y)
    second_far, grads = stage(lambda: (swap_c(second), dense_back(after, second)))
    hidden, branch = grads["hidden"], grads["branch"]

    def stage_2():
        return swap_c(hidden[:, 2 * width :]), swap_c(branch), down_grad(bf16, 3)

    hidden_far, branch_far, down_sent = stage(stage_2)
    up_sent = up_grad(bf16, 1)
    out_kept, out_sent = split_grad(attended, attended_far, branch, branch_far, 2 * cols)

    def stage_3():
        return (
            swap_y(down_sent),
            swap_y(up_sent),
            swap_y(out_sent),
            attention_back(grads, True, 0, 6),
            down_grad(f32, 0),
            up_grad(f32, 0),
        )

    *came, found, down_kept, up_kept = stage(stage_3)
    *qkv_grads, k_far, v_far, held = found
    kept = (down_kept, up_kept, out_kept)
    later = [(own + other.astype(f32)).astype(bf16) for own, other in zip(kept, came)]

    def stage_4():
        summed = lax.psum(later, "dp")
        near, far, grad_input, grad_low, qv_sums = input_back(
            qkv_grads, (swap_c(k_far), swap_c(v_far)), grads["before"], qkv
        )
        rest_kept, rest_sent = split_grad(near, swap_c(far), x1, inputs_far, 2 * cols)
        edge_low = edge_blocks(jnp.where(leading, grad_low, result.astype(bf16)))
        edge_came = swap_y(theirs(edge_low))
        parts = []
        for which in range(3):
            rows = slice(which * cols, which * cols + cols)
            rest = rest_kept[rows] + swap_y(rest_sent[rows]).astype(f32)
            parts.append(hops(rest.astype(bf16)))
        sums = token_sums(qv_sums)
        sums = sums[:2] + swap_c(sums[2:])
        sums = sums[0] + swap_y(sums[1])
        if planes == 4:
            sums = sums + swap_z(sums)
            sums = sums + lax.ppermute(sums, "dp", [(0, 2), (2, 0), (1, 3), (3, 1)])
        else:
            sums = lax.psum(sums, "dp")
        return summed, parts, sums, grad_input, edge_came

    share = model // 4

    def token_sums(qv_sums):
        wide = jnp.pad(held.reshape(4 * heads, 2, 8, SPAN), ((0, 0), (0, 0), (0, 0), (0, 8)))
        sums = sum(wide[:, :, s, s : s + SPAN] for s in range(8))
        sums = jnp.stack([sums[:, 0] - sums[:, 1], sums[:, 1]], 1).reshape(8 * heads, SPAN)
        grad_table = jnp.dot(sums, onehot, precision=lax.Precision.HIGHEST)
        grad_table = grad_table.reshape(4, heads * 2 * kinds)
        q_sums, _, v_sums = qv_sums.reshape(3, 4, cols)
        grad_ffn = grads["hidden_sums"].reshape(4, width)
        low_sums = grads["low_sums"]
        rows = [low_sums[0], top_sums[0], low_sums[1], low_sums[2], top_sums[1], top_sums[2]]
        by_share = jnp.stack(rows).reshape(6, 4, share)
        by_share = by_share.transpose(1, 0, 2).reshape(4, 6 * share)
        by_share = jnp.stack(
            [lax.dynamic_index_in_dim(by_share, place ^ flip, 0, False) for flip in (0, 2, 1, 3)]
        )
        return jnp.concatenate([grad_table, q_sums, v_sums, grad_ffn, by_share], 1)

    summed, parts, sums, grad_input, edge_came = stage(stage_4)
    grad_down, grad_up, grad_out = [value.astype(f32) for value in summed]
    grad_qkv = jnp.stack(parts).astype(f32)
    edge_own = mine(edge_blocks(jnp.where(leading, grad_input, result)))
    edge_came = edge_came.astype(f32)
    edges = jnp.stack([jnp.where(y == 0, edge_own, edge_came), jnp.where(y == 0, edge_came, edge_own)])
    grad_qkv = grad_qkv.reshape(1, 3, cols, model).transpose(0, 3, 1, 2)
    at = heads * 2 * kinds
    table_out = sums[:at].reshape(heads, 2 * kinds)
    qv_out = sums[at : at + 2 * cols].reshape(2, cols)
    ffn_out = sums[at + 2 * cols : at + 2 * cols + width]
    vec_out = sums[at + 2 * cols + width :].reshape(6, share)
    return (
        edges[None],
        grad_qkv,
        qv_out[None],
        grad_out[None],
        grad_up[None],
        ffn_out[None],
        grad_down[None],
        vec_out[:2][None],
        vec_out[2:][None],
        table_out[None],
    )


def solution(mesh):
    return jax.shard_map(
        body,
        mesh=mesh,
        in_specs=(
            P("dp", "tensor", None),
            P("dp", "tensor", None),
            P("dp"),
            P("dp"),
            P(),
            P("section", None, None, "tensor"),
            P("section", None, "tensor"),
            P("section", "tensor", None),
            P("section", None, "tensor"),
            P("section", "tensor"),
            P("section", "tensor", None),
            P("section", None, None),
            P("section", None, None),
            P("section", "tensor", None),
        ),
        out_specs=(
            P("section", "dp", "tensor", None),
            P("section", None, None, "tensor"),
            P("section", None, "tensor"),
            P("section", "tensor", None),
            P("section", None, "tensor"),
            P("section", "tensor"),
            P("section", "tensor", None),
            P("section", None, "tensor"),
            P("section", None, "tensor"),
            P("section", "tensor", None),
        ),
        check_vma=False,
    )
```

profile of v0, /device:TPU:0, one launch (start us, length us, event | category | flops | bytes accessed | tf_op | source)
XLA Modules:
  0.0 555.0 jit_solution(3020158744858703188)
XLA Ops:
  17.0 21.9 %conditional.17 = (bf16[256,768]{1,0:T(8,128)(2,1)}, f32[1344]{0:T(1024)}, bf16[3,96,768]{2,1,0:T(8,128)(2,1)}, bf16[96,768]{1,0:T(8,128)(2,1)S(1)}, bf16[384,76...) conditional(s32[]{:T(128)} %bitcast.21, () %tuple.174, (bf16[2,256,768]{2,1,0:T(8,128)(2,1)}, s32[]{:T(128)}, ...), branch_computations={%region_0.1_spmd, %region_1.2_spmd} | conditional | flops 8 | bytes 7984428 | solution.py:788
  25.4 13.6 %collective-permute-done.15 = f32[1344]{0:T(1024)} collective-permute-done((f32[1344]{0:T(1024)S(1)}, f32[1344]{0:T(1024)}, u32[]{:S(2)}, u32[]{:S(2)}) %collective-permute-start.15) | collective-permute-done | bytes 5408 | tf_op jit(solution)/shard_map/cond/branch_1_fun/ppermute | solution.py:37
  38.9 19.9 %conditional.18 = (bf16[96,768]{1,0:T(8,128)(2,1)}, bf16[384,768]{1,0:T(8,128)(2,1)}, bf16[3,96,768]{2,1,0:T(8,128)(2,1)}, f32[4,1344]{1,0:T(4,128)}, f32[6,2,2,...) conditional(s32[]{:T(128)} %bitcast.21, () %tuple.176, ...), branch_computations={%region_2.3_spmd, %region_3.4_spmd} | conditional | flops 16528512 | bytes 5393676 | solution.py:788
  59.5 41.1 %conditional.19 = (bf16[512,768]{1,0:T(8,128)(2,1)}, bf16[2304,768]{1,0:T(8,128)(2,1)}, bf16[512,768]{1,0:T(8,128)(2,1)}, bf16[96,768]{1,0:T(8,128)(2,1)}, bf16[...) conditional(s32[]{:T(128)} %bitcast.21, () %tuple.173, (s32[]{:T(128)}, bf16[2,256,768]{2,1,0:T(8,128)(2,1)}, ...), branch_computations={%region_4.5_spmd, %region_5.6_spmd} | conditional | flops 1836171264 | bytes 127384312 | solution.py:788
  82.1 18.4 %attend_forward.2 = (bf16[512,768]{1,0:T(8,128)(2,1)}, f32[6,2,512]{2,1,0:T(2,128)}) custom-call(s32[3]{0:T(128)S(1)} %copy-done.64, bf16[512,768]{1,0:T(8,128)(2,1)S(1)} %fusion.4.q_ref, bf16[512,1536]{1,0:T(8,128)(2,1)S(1)} %fusion.3.k_ref.v_ref, bf16[512,1536]{1,0:T(8,128)(2,1)S(1)} %fusion.3.k_ref.v_ref, ...), custom_call_target="tpu_custom_call" | custom-call | bytes 57800000 | tf_op jit(solution)/shard_map/cond/branch_1_fun/attend_forward/pallas_call | solution.py:181
  100.6 21.5 %conditional.20 = (bf16[768,768]{1,0:T(8,128)(2,1)S(1)}, bf16[2,768,768]{2,1,0:T(8,128)(2,1)}, bf16[2,768,768]{2,1,0:T(8,128)(2,1)}, bf16[384,768]{1,0:T(8,128)(2,1)}) conditional(s32[]{:T(128)} %bitcast.21, () %tuple.181, (s32[]{:T(128)}, bf16[96,768]{1,0:T(8,128)(2,1)}, bf16[96,768]{1,0:T(8,128)(2,1)}, bf16[192,768]{1,0:T(8,128)(2,1)}, ...), branch_computations={%region_6.7_spmd, %region_7.8_spmd} | conditional | flops 10764289 | bytes 33620188 | solution.py:788
  110.3 11.8 %collective-permute-done.19 = bf16[384,768]{1,0:T(8,128)(2,1)} collective-permute-done((bf16[384,768]{1,0:T(8,128)(2,1)}, bf16[384,768]{1,0:T(8,128)(2,1)}, u32[]{:S(2)}, u32[]{:S(2)}) %collective-permute-start.19) | collective-permute-done | bytes 589856 | tf_op jit(solution)/shard_map/cond/branch_1_fun/ppermute | solution.py:766
  122.1 9.3 %conditional.21 = (bf16[2,768,768]{2,1,0:T(8,128)(2,1)}, bf16[2,768,768]{2,1,0:T(8,128)(2,1)}) conditional(s32[]{:T(128)} %bitcast.21, () %tuple.183, (s32[]{:T(128)}, bf16[384,768]{1,0:T(8,128)(2,1)}, bf16[384,768]{1,0:T(8,128)(2,1)}, bf16[1,768,768]{2,1,0:T(8,128)(2,1)}) %tuple.184), branch_computations={%region_8.9_spmd, %region_9.10_spmd} | conditional | flops 4128769 | bytes 23593054 | solution.py:788
  131.4 9.6 %ffn_forward.4 = bf16[256,768]{1,0:T(8,128)(2,1)S(1)} custom-call(bf16[512,768]{1,0:T(8,128)(2,1)} %get-tuple-element.652.att_ref, bf16[512,768]{1,0:T(8,128)(2,1)} %get-tuple-element.651.x_ref, bf16[768,768]{1,0:T(8,128)(2,1)S(1)} %get-tuple-element.656.out_ref, bf16[2,768,768]{2,1,0:T(8,128)(2,1)} %get-tuple-element.657.up_ref, ...), custom_call_target="tpu_custom_call" | custom-call | bytes 51000000 | tf_op jit(solution)/shard_map/ffn_forward/pallas_call | solution.py:426
  141.1 15.2 %conditional.22 = (bf16[256,768]{1,0:T(8,128)(2,1)}, bf16[256,768]{1,0:T(8,128)(2,1)}) conditional(s32[]{:T(128)} %bitcast.21, () %tuple.180, (bf16[256,768]{1,0:T(8,128)(2,1)S(1)}, bf16[512,768]{1,0:T(8,128)(2,1)}, bf16[512,768]{1,0:T(8,128)(2,1)}, bf16[768,768]{1,0:T(8,128)(2,1)S(1)}, bf16[2,768,768]{2,1,0:T(8,128)(2,1)}, ...), branch_computations={%region_10.11_spmd, %region_11.12_spmd} | conditional | bytes 52597496 | solution.py:788
  146.0 10.3 %ffn_forward.3 = bf16[256,768]{1,0:T(8,128)(2,1)} custom-call(bf16[512,768]{1,0:T(8,128)(2,1)} %get-tuple-element.390.att_ref, bf16[512,768]{1,0:T(8,128)(2,1)} %get-tuple-element.391.x_ref, bf16[768,768]{1,0:T(8,128)(2,1)S(1)} %get-tuple-element.392.out_ref, bf16[2,768,768]{2,1,0:T(8,128)(2,1)} %get-tuple-element.393.up_ref, ...), custom_call_target="tpu_custom_call" | custom-call | bytes 51000000 | tf_op jit(solution)/shard_map/cond/branch_1_fun/ffn_forward/pallas_call | solution.py:426
  157.4 10.3 %conditional.23 = (bf16[256,768]{1,0:T(8,128)(2,1)}, bf16[256,768]{1,0:T(8,128)(2,1)S(1)}, bf16[256,1536]{1,0:T(8,128)(2,1)S(1)}) conditional(s32[]{:T(128)} %bitcast.21, () %tuple.179, (bf16[256,768]{1,0:T(8,128)(2,1)}, bf16[256,768]{1,0:T(8,128)(2,1)S(1)}, bf16[2304,768]{1,0:T(8,128)(2,1)}, f32[4,1,192]{2,1,0:T(1,128)S(1)}, ...), branch_computations={%region_12.13_spmd, %region_13.14_spmd} | conditional | flops 907149312 | bytes 11424836 | solution.py:788
  167.7 10.6 %conditional.24 = (bf16[512,768]{1,0:T(8,128)(2,1)}, bf16[512,768]{1,0:T(8,128)(2,1)}, bf16[512,1536]{1,0:T(8,128)(2,1)}, bf16[512,1536]{1,0:T(8,128)(2,1)}) conditional(s32[]{:T(128)} %bitcast.21, () %tuple.172, (pred[]{:T(512)}, bf16[512,768]{1,0:T(8,128)(2,1)}, bf16[256,768]{1,0:T(8,128)(2,1)}, bf16[256,768]{1,0:T(8,128)(2,1)S(1)}, ...), branch_computations={%region_14.15_spmd, %region_15.16_spmd} | conditional | flops 913637376 | bytes 34624644 | solution.py:788
  178.3 21.3 %conditional.25 = (bf16[256,768]{1,0:T(8,128)(2,1)}, bf16[512,768]{1,0:T(8,128)(2,1)}, bf16[512,768]{1,0:T(8,128)(2,1)}, f32[6,2,512]{2,1,0:T(2,128)S(1)}) conditional(s32[]{:T(128)} %bitcast.21, () %tuple.191, (bf16[2,256,768]{2,1,0:T(8,128)(2,1)}, s32[]{:T(128)}, bf16[512,768]{1,0:T(8,128)(2,1)}, s32[3]{0:T(128)S(1)}, ...), branch_computations={%region_16.17_spmd, %region_17.18_spmd} | conditional | bytes 63649204 | solution.py:788
  180.3 18.9 %attend_forward.3 = (bf16[512,768]{1,0:T(8,128)(2,1)}, f32[6,2,512]{2,1,0:T(2,128)S(1)}) custom-call(s32[3]{0:T(128)S(1)} %get-tuple-element.417.info_ref, bf16[512,768]{1,0:T(8,128)(2,1)} %get-tuple-element.418.q_ref, bf16[512,1536]{1,0:T(8,128)(2,1)} %get-tuple-element.419.k_ref.v_ref, bf16[512,1536]{1,0:T(8,128)(2,1)} %get-tuple-element.419.k_ref.v_ref, ...), custom_call_target="tpu_custom_call" | custom-call | bytes 57800000 | tf_op jit(solution)/shard_map/cond/branch_1_fun/attend_forward/pallas_call | solution.py:181
  201.0 17.6 %ffn_forward.5 = (f32[512,768]{1,0:T(8,128)}, bf16[512,768]{1,0:T(8,128)(2,1)}, bf16[512,3072]{1,0:T(8,128)(2,1)}, bf16[512,3072]{1,0:T(8,128)(2,1)S(1)}, f32[51...) custom-call(bf16[512,768]{1,0:T(8,128)(2,1)S(1)} %copy-done.7, ...), custom_call_target="tpu_custom_call" | custom-call | bytes 51000000 | tf_op jit(solution)/shard_map/ffn_forward/pallas_call | solution.py:426
  220.4 15.6 %conditional.26 = (bf16[512,768]{1,0:T(8,128)(2,1)}, bf16[512,1536]{1,0:T(8,128)(2,1)}, bf16[512,384]{1,0:T(8,128)(2,1)}, bf16[512,768]{1,0:T(8,128)(2,1)S(1)}, f32[512,768]{1,0:T(8,128)}) conditional(s32[]{:T(128)} %bitcast.21, () %tuple.190, (bf16[512,768]{1,0:T(8,128)(2,1)}, bf16[512,3072]{1,0:T(8,128)(2,1)}, bf16[512,768]{1,0:T(8,128)(2,1)S(1)}, ...), branch_computations={%region_18.19_spmd, %region_19.20_spmd} | conditional | bytes 65942368 | solution.py:788
  222.7 13.1 %ffn_backward.2 = (bf16[512,3072]{1,0:T(8,128)(2,1)}, f32[512,768]{1,0:T(8,128)}, bf16[512,768]{1,0:T(8,128)(2,1)}, bf16[512,768]{1,0:T(8,128)(2,1)S(1)}, f32[8,768]{1,0:T(8,128)}, /*index=5*/f32[4,1,768]{2,1,0:T(1,128)}) custom-call(f32[512,768]{1,0:T(8,128)S(1)} %get-tuple-element.427.refs_0_, bf16[512,768]{1,0:T(8,128)(2,1)S(1)} %get-tuple-element.428.refs_1_, ...), custom_call_target="tpu_custom_call" | custom-call | bytes 51000000 | tf_op jit(solution)/shard_map/cond/branch_1_fun/ffn_backward/pallas_call | solution.py:546
  236.0 28.4 %attend_backward.3 = (bf16[512,768]{1,0:T(8,128)(2,1)}, f32[512,768]{1,0:T(8,128)}, f32[512,768]{1,0:T(8,128)}, bf16[512,768]{1,0:T(8,128)(2,1)S(1)}, bf16[512,768]{1,0:T(8,128)(2,1)S(1)}) custom-call(s32[3]{0:T(128)S(1)} %copy-done.62, bf16[512,768]{1,0:T(8,128)(2,1)} %get-tuple-element.669.refs_1_, bf16[512,1536]{1,0:T(8,128)(2,1)} %get-tuple-element.670.refs_2_.refs_3_, ...), custom_call_target="tpu_custom_call" | custom-call | bytes 102000000 | tf_op jit(solution)/shard_map/attend_backward/pallas_call | solution.py:284
  275.9 13.6 %conditional.28 = (bf16[256,768]{1,0:T(8,128)(2,1)}, bf16[256,768]{1,0:T(8,128)(2,1)S(1)}) conditional(s32[]{:T(128)} %bitcast.21, () %tuple.189, (bf16[256,768]{1,0:T(8,128)(2,1)S(1)}, bf16[512,768]{1,0:T(8,128)(2,1)S(1)}, f32[512,768]{1,0:T(8,128)S(1)}, bf16[512,768]{1,0:T(8,128)(2,1)}, f32[512,768]{1,0:T(8,128)S(1)}, ...), branch_computations={%region_22.23_spmd, %region_23.24_spmd} | conditional | bytes 21972920 | solution.py:788
  289.6 12.8 %conditional.29 = (bf16[256,768]{1,0:T(8,128)(2,1)}) conditional(s32[]{:T(128)} %bitcast.21, () %tuple.197, bf16[256,768]{1,0:T(8,128)(2,1)S(1)} %get-tuple-element.696), branch_computations={%region_24.25_spmd, %region_25.26_spmd} | conditional | bytes 1572912 | solution.py:788
  290.9 11.5 %collective-permute-done.7 = bf16[256,768]{1,0:T(8,128)(2,1)} collective-permute-done((bf16[256,768]{1,0:T(8,128)(2,1)S(1)}, bf16[256,768]{1,0:T(8,128)(2,1)}, u32[]{:S(2)}, u32[]{:S(2)}) %collective-permute-start.7) | collective-permute-done | bytes 393248 | tf_op jit(solution)/shard_map/cond/branch_1_fun/ppermute | solution.py:867
  306.6 13.1 %conditional.30 = (bf16[512,768]{1,0:T(8,128)(2,1)}, bf16[512,768]{1,0:T(8,128)(2,1)}, f32[512,768]{1,0:T(8,128)}, bf16[512,768]{1,0:T(8,128)(2,1)S(1)}, bf16[51...) conditional(s32[]{:T(128)} %bitcast.21, () %tuple.188, ...), branch_computations={%region_26.27_spmd, %region_27.28_spmd} | conditional | bytes 54145824 | solution.py:788
  306.6 13.1 %ffn_backward.3 = (bf16[512,3072]{1,0:T(8,128)(2,1)}, f32[512,768]{1,0:T(8,128)}, bf16[512,768]{1,0:T(8,128)(2,1)S(1)}, bf16[512,768]{1,0:T(8,128)(2,1)}, f32[8,...) custom-call(f32[512,768]{1,0:T(8,128)S(1)} %get-tuple-element.452.refs_0_, bf16[512,768]{1,0:T(8,128)(2,1)S(1)} %get-tuple-element.451.refs_1_, ...), custom_call_target="tpu_custom_call" | custom-call | bytes 51000000 | tf_op jit(solution)/shard_map/cond/branch_1_fun/ffn_backward/pallas_call | solution.py:546
  333.8 60.4 %conditional.32 = (bf16[512,768]{1,0:T(8,128)(2,1)}, f32[512,768]{1,0:T(8,128)}, f32[512,768]{1,0:T(8,128)}, bf16[512,768]{1,0:T(8,128)(2,1)}, bf16[512,768]{1,0...) conditional(s32[]{:T(128)} %bitcast.21, () %tuple.171, ...), branch_computations={%region_30.31_spmd, %region_31.32_spmd} | conditional | flops 1327104 | bytes 148123712 | solution.py:788
  345.0 31.8 %attend_backward.2 = (bf16[512,768]{1,0:T(8,128)(2,1)}, f32[512,768]{1,0:T(8,128)}, f32[512,768]{1,0:T(8,128)}, bf16[512,768]{1,0:T(8,128)(2,1)}, bf16[512,768]{...) custom-call(s32[3]{0:T(128)S(1)} %get-tuple-element.474.refs_0_, bf16[512,768]{1,0:T(8,128)(2,1)} %get-tuple-element.475.refs_1_, ...), custom_call_target="tpu_custom_call" | custom-call | bytes 102000000 | tf_op jit(solution)/shard_map/cond/branch_1_fun/attend_backward/pallas_call | solution.py:284
  376.8 17.0 %collective-permute-done.13 = bf16[192,768]{1,0:T(8,128)(2,1)S(1)} collective-permute-done((bf16[192,768]{1,0:T(8,128)(2,1)S(1)}, bf16[192,768]{1,0:T(8,128)(2,1)S(1)}, u32[]{:S(2)}, u32[]{:S(2)}) %collective-permute-start.13) | collective-permute-done | bytes 294944 | tf_op jit(solution)/shard_map/cond/branch_1_fun/ppermute | solution.py:37
  396.3 145.9 %conditional.33 = (f32[2496]{0:T(1024)}, f32[512,768]{1,0:T(8,128)}, f32[1,768,768]{2,1,0:T(8,128)}, f32[1,768,768]{2,1,0:T(8,128)}, f32[1,192,768]{2,1,0:T(8,12...) conditional(s32[]{:T(128)} %bitcast.21, () %tuple.170, ...), branch_computations={%region_32.33_spmd, %region_33.37_spmd} | conditional | flops 23212224 | bytes 139145408 | solution.py:788
  398.7 9.4 %fusion.15 = f32[12,2,1,1792]{3,2,1,0:T(1,128)S(1)} fusion(f32[12,2,8,1792]{3,2,1,0:T(8,128)} %bitcast.10), kind=kLoop, calls=%fused_computation.66 | loop fusion | flops 301056 | bytes 1720320 | tf_op jit(solution)/shard_map/cond/branch_1_fun/add | solution.py:1002
  483.1 9.8 %collective-permute-done.35 = f32[2496]{0:T(1024)S(1)} collective-permute-done((f32[2496]{0:T(1024)S(1)}, f32[2496]{0:T(1024)S(1)}, u32[]{:S(2)}, u32[]{:S(2)}) %collective-permute-start.35) | collective-permute-done | bytes 10016 | tf_op jit(solution)/shard_map/cond/branch_1_fun/ppermute | solution.py:993
  500.7 24.1 %all-reduce.7.cloned.1.call-done = (bf16[1,768,768]{2,1,0:T(8,128)(2,1)}, bf16[1,768,768]{2,1,0:T(8,128)(2,1)}, bf16[1,192,768]{2,1,0:T(8,128)(2,1)}) async-done(((bf16[1,768,768]{2,1,0:T(8,128)(2,1)}, bf16[1,768,768]{2,1,0:T(8,128)(2,1)}, bf16[1,192,768]{2,1,0:T(8,128)(2,1)}), (bf16[1,768,768]{2,1,0:T(8,128)(2,1)}, bf16[1,768,768]{2,1,0:T(8,128)(2,1)}, ...) | async-done | bytes 2654224 | tf_op jit(solution)/shard_map/cond/branch_1_fun/psum | solution.py:976
  532.8 9.5 %collective-permute-done.40 = bf16[192,768]{1,0:T(8,128)(2,1)S(1)} collective-permute-done((bf16[192,768]{1,0:T(8,128)(2,1)S(1)}, bf16[192,768]{1,0:T(8,128)(2,1)S(1)}, u32[]{:S(2)}, u32[]{:S(2)}) %collective-permute-start.40) | collective-permute-done | bytes 294944 | tf_op jit(solution)/shard_map/cond/branch_1_fun/ppermute | solution.py:946
  (388 shorter events, 279.9 us)
Async XLA Ops:
  17.0 21.9 %collective-permute-start.16 = (bf16[3,96,768]{2,1,0:T(8,128)(2,1)S(1)}, bf16[3,96,768]{2,1,0:T(8,128)(2,1)}, u32[]{:S(2)}, u32[]{:S(2)}) collective-permute-start(bf16[3,96,768]{2,1,0:T(8,128)(2,1)S(1)} %get-tuple-element.351), channel_id=1, source_target_pairs={{0,2},{2,0},{1,3},{3,1},{4,6},{6,4},{5,7},{7,5},{8,10},{10,8},{9,1... | collective-permute-start | bytes 1327112 | tf_op jit(solution)/shard_map/cond/branch_1_fun/ppermute | solution.py:37
  21.1 17.8 %collective-permute-start.14 = (bf16[256,768]{1,0:T(8,128)(2,1)S(1)}, bf16[256,768]{1,0:T(8,128)(2,1)}, u32[]{:S(2)}, u32[]{:S(2)}) collective-permute-start(bf16[256,768]{1,0:T(8,128)(2,1)S(1)} %dynamic-slice_bitcast_fusion.2), channel_id=1, source_target_pairs={{0,2},{2,0},{1,3},{3,1},{4,6},{6,4},{5,7},{7,5},{8,10},{10,8},{9,1... | collective-permute-start | bytes 1179656 | tf_op jit(solution)/shard_map/cond/branch_1_fun/ppermute | solution.py:37
  21.4 17.5 %collective-permute-start.15 = (f32[1344]{0:T(1024)S(1)}, f32[1344]{0:T(1024)}, u32[]{:S(2)}, u32[]{:S(2)}) collective-permute-start(f32[1344]{0:T(1024)S(1)} %get-tuple-element.350), channel_id=1, source_target_pairs={{0,2},{2,0},{1,3},{3,1},{4,6},{6,4},{5,7},{7,5},{8,10},{10,8},{9,1... | collective-permute-start | bytes 16136 | tf_op jit(solution)/shard_map/cond/branch_1_fun/ppermute | solution.py:37
  43.2 15.6 %collective-permute-start.51 = (bf16[384,768]{1,0:T(8,128)(2,1)S(1)}, bf16[384,768]{1,0:T(8,128)(2,1)}, u32[]{:S(2)}, u32[]{:S(2)}) collective-permute-start(bf16[384,768]{1,0:T(8,128)(2,1)S(1)} %get-tuple-element.357), channel_id=1, source_target_pairs={{0,2},{2,0},{1,3},{3,1},{4,6},{6,4},{5,7},{7,5},{8,10},{10,8},{9,1... | collective-permute-start | bytes 1769480 | tf_op jit(solution)/shard_map/cond/branch_1_fun/ppermute | solution.py:37
  75.9 24.7 %collective-permute-start.27 = (bf16[384,768]{1,0:T(8,128)(2,1)}, bf16[384,768]{1,0:T(8,128)(2,1)}, u32[]{:S(2)}, u32[]{:S(2)}) collective-permute-start(bf16[384,768]{1,0:T(8,128)(2,1)} %get-tuple-element.376), channel_id=1, source_target_pairs={{0,2},{2,0},{1,3},{3,1},{4,6},{6,4},{5,7},{7,5},{8,10},{10,8},{9,1... | collective-permute-start | bytes 1769480 | tf_op jit(solution)/shard_map/cond/branch_1_fun/ppermute | solution.py:37
  77.6 22.9 %collective-permute-start.26 = (bf16[384,768]{1,0:T(8,128)(2,1)}, bf16[384,768]{1,0:T(8,128)(2,1)}, u32[]{:S(2)}, u32[]{:S(2)}) collective-permute-start(bf16[384,768]{1,0:T(8,128)(2,1)} %get-tuple-element.375), channel_id=1, source_target_pairs={{0,4},{4,0},{8,12},{12,8},{1,5},{5,1},{9,13},{13,9},{2,6},{6,2},{1... | collective-permute-start | bytes 1769480 | tf_op jit(solution)/shard_map/cond/branch_1_fun/ppermute | solution.py:766
  79.2 21.3 %collective-permute-start.25 = (bf16[96,768]{1,0:T(8,128)(2,1)}, bf16[96,768]{1,0:T(8,128)(2,1)}, u32[]{:S(2)}, u32[]{:S(2)}) collective-permute-start(bf16[96,768]{1,0:T(8,128)(2,1)} %get-tuple-element.374), channel_id=1, source_target_pairs={{0,4},{4,0},{8,12},{12,8},{1,5},{5,1},{9,13},{13,9},{2,6},{6,2},{1... | collective-permute-start | bytes 442376 | tf_op jit(solution)/shard_map/cond/branch_1_fun/ppermute | solution.py:766
  104.8 17.3 %collective-permute-start.18 = (bf16[2,768,768]{2,1,0:T(8,128)(2,1)}, bf16[2,768,768]{2,1,0:T(8,128)(2,1)}, u32[]{:S(2)}, u32[]{:S(2)}) collective-permute-start(bf16[2,768,768]{2,1,0:T(8,128)(2,1)} %pad_maximum_fusion), channel_id=1, source_target_pairs={{0,1},{1,0},{2,3},{3,2},{4,5},{5,4},{6,7},{7,6},{8,9},{9,8},{10,11... | collective-permute-start | bytes 7077896 | tf_op jit(solution)/shard_map/cond/branch_1_fun/ppermute | solution.py:41
  106.4 15.6 %collective-permute-start.19 = (bf16[384,768]{1,0:T(8,128)(2,1)}, bf16[384,768]{1,0:T(8,128)(2,1)}, u32[]{:S(2)}, u32[]{:S(2)}) collective-permute-start(bf16[384,768]{1,0:T(8,128)(2,1)} %get-tuple-element.384), channel_id=1, source_target_pairs={{0,4},{4,0},{8,12},{12,8},{1,5},{5,1},{9,13},{13,9},{2,6},{6,2},{1... | collective-permute-start | bytes 1769480 | tf_op jit(solution)/shard_map/cond/branch_1_fun/ppermute | solution.py:766
  141.1 15.2 %collective-permute-start = (bf16[256,768]{1,0:T(8,128)(2,1)S(1)}, bf16[256,768]{1,0:T(8,128)(2,1)}, u32[]{:S(2)}, u32[]{:S(2)}) collective-permute-start(bf16[256,768]{1,0:T(8,128)(2,1)S(1)} %get-tuple-element.389), channel_id=1, source_target_pairs={{0,16},{1,17},{2,18},{3,19},{4,20},{5,21},{6,22},{7,23},{8,24},{9,... | collective-permute-start | bytes 1179656 | tf_op jit(solution)/shard_map/cond/branch_1_fun/ppermute | solution.py:864
  178.3 20.9 %collective-permute-start.22 = (bf16[512,768]{1,0:T(8,128)(2,1)}, bf16[512,768]{1,0:T(8,128)(2,1)}, u32[]{:S(2)}, u32[]{:S(2)}) collective-permute-start(bf16[512,768]{1,0:T(8,128)(2,1)} %get-tuple-element.416), channel_id=1, source_target_pairs={{0,1},{1,0},{2,3},{3,2},{4,5},{5,4},{6,7},{7,6},{8,9},{9,8},{10,11... | collective-permute-start | bytes 2359304 | tf_op jit(solution)/shard_map/cond/branch_1_fun/ppermute | solution.py:41
  179.6 19.5 %collective-permute-start.21 = (bf16[256,768]{1,0:T(8,128)(2,1)S(1)}, bf16[256,768]{1,0:T(8,128)(2,1)}, u32[]{:S(2)}, u32[]{:S(2)}) collective-permute-start(bf16[256,768]{1,0:T(8,128)(2,1)S(1)} %dynamic-slice_bitcast_fusion.3), channel_id=1, source_target_pairs={{0,2},{2,0},{1,3},{3,1},{4,6},{6,4},{5,7},{7,5},{8,10},{10,8},{9,1... | collective-permute-start | bytes 1179656 | tf_op jit(solution)/shard_map/cond/branch_1_fun/ppermute | solution.py:37
  221.9 13.9 %collective-permute-start.2 = (bf16[512,1536]{1,0:T(8,128)(2,1)S(1)}, bf16[512,1536]{1,0:T(8,128)(2,1)}, u32[]{:S(2)}, u32[]{:S(2)}) collective-permute-start(bf16[512,1536]{1,0:T(8,128)(2,1)S(1)} %slice.172), channel_id=1, source_target_pairs={{0,1},{1,0},{2,3},{3,2},{4,5},{5,4},{6,7},{7,6},{8,9},{9,8},{10,11... | collective-permute-start | bytes 4718600 | tf_op jit(solution)/shard_map/cond/branch_1_fun/ppermute | solution.py:41
  222.0 13.8 %collective-permute-start.1 = (bf16[512,768]{1,0:T(8,128)(2,1)}, bf16[512,768]{1,0:T(8,128)(2,1)}, u32[]{:S(2)}, u32[]{:S(2)}) collective-permute-start(bf16[512,768]{1,0:T(8,128)(2,1)} %get-tuple-element.424), channel_id=1, source_target_pairs={{0,1},{1,0},{2,3},{3,2},{4,5},{5,4},{6,7},{7,6},{8,9},{9,8},{10,11... | collective-permute-start | bytes 2359304 | tf_op jit(solution)/shard_map/cond/branch_1_fun/ppermute | solution.py:41
  275.9 13.6 %collective-permute-start.6 = (bf16[256,768]{1,0:T(8,128)(2,1)S(1)}, bf16[256,768]{1,0:T(8,128)(2,1)}, u32[]{:S(2)}, u32[]{:S(2)}) collective-permute-start(bf16[256,768]{1,0:T(8,128)(2,1)S(1)} %get-tuple-element.442), channel_id=1, source_target_pairs={{16,0},{17,1},{18,2},{19,3},{20,4},{21,5},{22,6},{23,7},{24,8},{25... | collective-permute-start | bytes 1179656 | tf_op jit(solution)/shard_map/cond/branch_1_fun/ppermute | solution.py:867
  333.8 60.0 %collective-permute-start.12 = (bf16[768,768]{1,0:T(8,128)(2,1)S(1)}, bf16[768,768]{1,0:T(8,128)(2,1)S(1)}, u32[]{:S(2)}, u32[]{:S(2)}) collective-permute-start(bf16[768,768]{1,0:T(8,128)(2,1)S(1)} %get-tuple-element.496), channel_id=1, source_target_pairs={{0,2},{2,0},{1,3},{3,1},{4,6},{6,4},{5,7},{7,5},{8,10},{10,8},{9,1... | collective-permute-start | bytes 3538952 | tf_op jit(solution)/shard_map/cond/branch_1_fun/ppermute | solution.py:37
  335.4 58.6 %collective-permute-start.11 = (bf16[768,768]{1,0:T(8,128)(2,1)}, bf16[768,768]{1,0:T(8,128)(2,1)S(1)}, u32[]{:S(2)}, u32[]{:S(2)}) collective-permute-start(bf16[768,768]{1,0:T(8,128)(2,1)} %get-tuple-element.495), channel_id=1, source_target_pairs={{0,2},{2,0},{1,3},{3,1},{4,6},{6,4},{5,7},{7,5},{8,10},{10,8},{9,1... | collective-permute-start | bytes 3538952 | tf_op jit(solution)/shard_map/cond/branch_1_fun/ppermute | solution.py:37
  335.9 57.9 %collective-permute-start.13 = (bf16[192,768]{1,0:T(8,128)(2,1)S(1)}, bf16[192,768]{1,0:T(8,128)(2,1)S(1)}, u32[]{:S(2)}, u32[]{:S(2)}) collective-permute-start(bf16[192,768]{1,0:T(8,128)(2,1)S(1)} %get-tuple-element.497), channel_id=1, source_target_pairs={{0,2},{2,0},{1,3},{3,1},{4,6},{6,4},{5,7},{7,5},{8,10},{10,8},{9,1... | collective-permute-start | bytes 884744 | tf_op jit(solution)/shard_map/cond/branch_1_fun/ppermute | solution.py:37
  396.3 128.6 %all-reduce.7.cloned.1.call-start = ((), (), s32[]{:S(2)}) async-start(), calls=%async_computation | async-start | bytes 5308416 | tf_op jit(solution)/shard_map/cond/branch_1_fun/psum | solution.py:976
  430.0 14.6 %collective-permute-start.41 = (bf16[192,768]{1,0:T(8,128)(2,1)S(1)}, bf16[192,768]{1,0:T(8,128)(2,1)S(1)}, u32[]{:S(2)}, u32[]{:S(2)}) collective-permute-start(bf16[192,768]{1,0:T(8,128)(2,1)S(1)} %get-tuple-element.926), channel_id=1, source_target_pairs={{0,2},{2,0},{1,3},{3,1},{4,6},{6,4},{5,7},{7,5},{8,10},{10,8},{9,1... | collective-permute-start | bytes 884744 | tf_op jit(solution)/shard_map/cond/branch_1_fun/ppermute | solution.py:37
  430.5 20.0 %collective-permute-start.37 = (bf16[192,768]{1,0:T(8,128)(2,1)S(1)}, bf16[192,768]{1,0:T(8,128)(2,1)S(1)}, u32[]{:S(2)}, u32[]{:S(2)}) collective-permute-start(bf16[192,768]{1,0:T(8,128)(2,1)S(1)} %get-tuple-element.927), channel_id=1, source_target_pairs={{0,2},{2,0},{1,3},{3,1},{4,6},{6,4},{5,7},{7,5},{8,10},{10,8},{9,1... | collective-permute-start | bytes 884744 | tf_op jit(solution)/shard_map/cond/branch_1_fun/ppermute | solution.py:37
  437.1 19.1 %collective-permute-start.32 = (f32[2,2496]{1,0:T(2,128)S(1)}, f32[2,2496]{1,0:T(2,128)S(1)}, u32[]{:S(2)}, u32[]{:S(2)}) collective-permute-start(f32[2,2496]{1,0:T(2,128)S(1)} %slice.229), channel_id=1, source_target_pairs={{0,1},{1,0},{2,3},{3,2},{4,5},{5,4},{6,7},{7,6},{8,9},{9,8},{10,11... | collective-permute-start | bytes 59912 | tf_op jit(solution)/shard_map/cond/branch_1_fun/ppermute | solution.py:41
  452.7 15.1 %collective-permute-start.46 = (bf16[192,768]{1,0:T(8,128)(2,1)S(1)}, bf16[192,768]{1,0:T(8,128)(2,1)S(1)}, u32[]{:S(2)}, u32[]{:S(2)}) collective-permute-start(bf16[192,768]{1,0:T(8,128)(2,1)S(1)} %get-tuple-element.922), channel_id=1, source_target_pairs={{0,4},{12,8},{1,5},{13,9},{2,6},{14,10},{3,7},{15,11},{16,20},{28,... | collective-permute-start | bytes 884744 | tf_op jit(solution)/shard_map/cond/branch_1_fun/ppermute | solution.py:944
  460.1 20.8 %collective-permute-start.42 = (bf16[192,768]{1,0:T(8,128)(2,1)S(1)}, bf16[192,768]{1,0:T(8,128)(2,1)S(1)}, u32[]{:S(2)}, u32[]{:S(2)}) collective-permute-start(bf16[192,768]{1,0:T(8,128)(2,1)S(1)} %get-tuple-element.923), channel_id=1, source_target_pairs={{0,4},{12,8},{1,5},{13,9},{2,6},{14,10},{3,7},{15,11},{16,20},{28,... | collective-permute-start | bytes 884744 | tf_op jit(solution)/shard_map/cond/branch_1_fun/ppermute | solution.py:944
  464.0 28.9 %collective-permute-start.38 = (bf16[192,768]{1,0:T(8,128)(2,1)S(1)}, bf16[192,768]{1,0:T(8,128)(2,1)S(1)}, u32[]{:S(2)}, u32[]{:S(2)}) collective-permute-start(bf16[192,768]{1,0:T(8,128)(2,1)S(1)} %get-tuple-element.924), channel_id=1, source_target_pairs={{0,4},{12,8},{1,5},{13,9},{2,6},{14,10},{3,7},{15,11},{16,20},{28,... | collective-permute-start | bytes 884744 | tf_op jit(solution)/shard_map/cond/branch_1_fun/ppermute | solution.py:944
  467.8 25.8 %collective-permute-start.47 = (bf16[192,768]{1,0:T(8,128)(2,1)S(1)}, bf16[192,768]{1,0:T(8,128)(2,1)S(1)}, u32[]{:S(2)}, u32[]{:S(2)}) collective-permute-start(bf16[192,768]{1,0:T(8,128)(2,1)S(1)} %add.184), channel_id=1, source_target_pairs={{4,8},{8,4},{5,9},{9,5},{6,10},{10,6},{7,11},{11,7},{20,24},{24,20... | collective-permute-start | bytes 884744 | tf_op jit(solution)/shard_map/cond/branch_1_fun/ppermute | solution.py:945
  470.0 22.8 %collective-permute-start.35 = (f32[2496]{0:T(1024)S(1)}, f32[2496]{0:T(1024)S(1)}, u32[]{:S(2)}, u32[]{:S(2)}) collective-permute-start(f32[2496]{0:T(1024)S(1)} %add.175), channel_id=1, source_target_pairs={{0,8},{8,0},{4,12},{12,4},{1,9},{9,1},{5,13},{13,5},{2,10},{10,2},... | collective-permute-start | bytes 29960 | tf_op jit(solution)/shard_map/cond/branch_1_fun/ppermute | solution.py:993
  481.0 14.1 %collective-permute-start.43 = (bf16[192,768]{1,0:T(8,128)(2,1)S(1)}, bf16[192,768]{1,0:T(8,128)(2,1)S(1)}, u32[]{:S(2)}, u32[]{:S(2)}) collective-permute-start(bf16[192,768]{1,0:T(8,128)(2,1)S(1)} %add.181), channel_id=1, source_target_pairs={{4,8},{8,4},{5,9},{9,5},{6,10},{10,6},{7,11},{11,7},{20,24},{24,20... | collective-permute-start | bytes 884744 | tf_op jit(solution)/shard_map/cond/branch_1_fun/ppermute | solution.py:945
  481.7 18.1 %collective-permute-start.49 = (bf16[256,768]{1,0:T(8,128)(2,1)S(1)}, bf16[256,768]{1,0:T(8,128)(2,1)S(1)}, u32[]{:S(2)}, u32[]{:S(2)}) collective-permute-start(bf16[256,768]{1,0:T(8,128)(2,1)S(1)} %dynamic-slice_bitcast_fusion.4), channel_id=1, source_target_pairs={{0,2},{2,0},{1,3},{3,1},{4,6},{6,4},{5,7},{7,5},{8,10},{10,8},{9,1... | collective-permute-start | bytes 1179656 | tf_op jit(solution)/shard_map/cond/branch_1_fun/ppermute | solution.py:37
  492.9 38.3 %collective-permute-start.39 = (bf16[192,768]{1,0:T(8,128)(2,1)S(1)}, bf16[192,768]{1,0:T(8,128)(2,1)S(1)}, u32[]{:S(2)}, u32[]{:S(2)}) collective-permute-start(bf16[192,768]{1,0:T(8,128)(2,1)S(1)} %add.178), channel_id=1, source_target_pairs={{4,8},{8,4},{5,9},{9,5},{6,10},{10,6},{7,11},{11,7},{20,24},{24,20... | collective-permute-start | bytes 884744 | tf_op jit(solution)/shard_map/cond/branch_1_fun/ppermute | solution.py:945
  493.7 38.9 %collective-permute-start.48 = (bf16[192,768]{1,0:T(8,128)(2,1)S(1)}, bf16[192,768]{1,0:T(8,128)(2,1)S(1)}, u32[]{:S(2)}, u32[]{:S(2)}) collective-permute-start(bf16[192,768]{1,0:T(8,128)(2,1)S(1)} %add.185), channel_id=1, source_target_pairs={{4,0},{8,12},{5,1},{9,13},{6,2},{10,14},{7,3},{11,15},{20,16},{24,... | collective-permute-start | bytes 884744 | tf_op jit(solution)/shard_map/cond/branch_1_fun/ppermute | solution.py:946
  495.2 37.5 %collective-permute-start.44 = (bf16[192,768]{1,0:T(8,128)(2,1)S(1)}, bf16[192,768]{1,0:T(8,128)(2,1)S(1)}, u32[]{:S(2)}, u32[]{:S(2)}) collective-permute-start(bf16[192,768]{1,0:T(8,128)(2,1)S(1)} %add.182), channel_id=1, source_target_pairs={{4,0},{8,12},{5,1},{9,13},{6,2},{10,14},{7,3},{11,15},{20,16},{24,... | collective-permute-start | bytes 884744 | tf_op jit(solution)/shard_map/cond/branch_1_fun/ppermute | solution.py:946
  (91 other events, 712.2 us)
Sparse Core Ops, SparseCore 0:
  400.3 124.5 all-reduce.6
where the time goes:
time: 566 us; the launch traced here: 555 us
  Pallas kernels  211 us (37%)
  waiting for transfers between devices  150 us (27%)
  other arithmetic  60.9 us (11%)
  starting transfers between devices  57.6 us (10%)
  local copies, waits for them, and re-layouts  45.3 us (8%)
  between operations  15.6 us (3%)
  matrix products  13.1 us (2%)
    pallas_call x2, Pallas kernels, attend_backward(): pl.pallas_call(functools.partial(backward_kernel, with_table), grid_spec=...  60.2 us
    ppermute x15, waiting for transfers between devices, swap_y(): return lax.ppermute(value, 'tensor', SWAP_Y)  50.8 us
    pallas_call x3, Pallas kernels, ffn_forward(): pl.pallas_call(functools.partial(ffn_forward_kernel, keep), grid=(4,), in...  37.5 us
    pallas_call x2, Pallas kernels, attend_forward(): pl.pallas_call(forward_kernel, grid_spec=pltpu.PrefetchScalarGridSpec(num...  37.3 us
    pallas_call x2, Pallas kernels, ffn_backward(): pl.pallas_call(functools.partial(ffn_backward_kernel, len(deps)), grid=(4...  26.2 us
    psum x1, waiting for transfers between devices, stage_4(): summed = lax.psum(later, 'dp')  24.1 us
    pallas_call x3, Pallas kernels, input_back(): pl.pallas_call(input_back_kernel, grid=(6,), in_specs=[at(0), at(2), at(2...  24 us
    ppermute x15, starting transfers between devices, swap_y(): return lax.ppermute(value, 'tensor', SWAP_Y)  20 us
  transfers between devices with their start and end apart: 55, of which 23 were waited for; matrix products, arithmetic and copies ran while one was open for 11% of the time, Pallas kernels for 25%

commit v1 on v0

--- a/solution.py
+++ b/solution.py
@@ -195,7 +195,7 @@
             jax.ShapeDtypeStruct((512, 128 * groups), bf16),
             jax.ShapeDtypeStruct((groups, 2, 512), f32),
         ],
-        compiler_params=pltpu.CompilerParams(vmem_limit_bytes=40 * MIB),
+        compiler_params=pltpu.CompilerParams(vmem_limit_bytes=24 * MIB),
         cost_estimate=cost(17),
         name="attend_forward",
     )(info, q, kv, kv, kv_other, kv_other, window)
@@ -297,7 +297,7 @@
             scratch_shapes=scratch,
         ),
         out_shape=out_shape,
-        compiler_params=pltpu.CompilerParams(vmem_limit_bytes=48 * MIB),
+        compiler_params=pltpu.CompilerParams(vmem_limit_bytes=36 * MIB),
         cost_estimate=cost(30),
         name="attend_backward",
     )(info, q, kv, kv, kv_other, kv_other, grad, lse, window)
@@ -439,7 +439,7 @@
         out_specs=out_specs,
         out_shape=out_shape,
         scratch_shapes=[pltpu.VMEM((rows, model), bf16), pltpu.VMEM((rows, model), f32)],
-        compiler_params=pltpu.CompilerParams(vmem_limit_bytes=48 * MIB),
+        compiler_params=pltpu.CompilerParams(vmem_limit_bytes=32 * MIB),
         cost_estimate=cost(15),
         name="ffn_forward",
     )(
@@ -475,7 +475,7 @@
             jax.ShapeDtypeStruct((rows, model), bf16),
             jax.ShapeDtypeStruct((8, model), f32),
         ],
-        compiler_params=pltpu.CompilerParams(vmem_limit_bytes=20 * MIB),
+        compiler_params=pltpu.CompilerParams(vmem_limit_bytes=16 * MIB),
         cost_estimate=cost(2),
         name="top_back",
     )(grad_y, saved["n_two"], saved["s_two"], w["gains"])
@@ -568,7 +568,7 @@
             jax.ShapeDtypeStruct((4, 1, width), f32),
         ],
         scratch_shapes=[pltpu.VMEM((rows, model), f32)],
-        compiler_params=pltpu.CompilerParams(vmem_limit_bytes=48 * MIB),
+        compiler_params=pltpu.CompilerParams(vmem_limit_bytes=32 * MIB),
         cost_estimate=cost(15),
         name="ffn_backward",
     )(
@@ -605,7 +605,7 @@
         ],
         out_specs=pl.BlockSpec((lw, rw), lambda j, i: (i, j)),
         out_shape=jax.ShapeDtypeStruct((ln * lw, rn * rw), kind),
-        compiler_params=pltpu.CompilerParams(vmem_limit_bytes=40 * MIB),
+        compiler_params=pltpu.CompilerParams(vmem_limit_bytes=20 * MIB),
         cost_estimate=cost(4),
         name="weight_grad",
     )(left, left_far, right, right_far)
@@ -631,93 +631,70 @@
         in_specs=[left_block, left_block, right_block, right_block],
         out_specs=[made, made],
         out_shape=[jax.ShapeDtypeStruct(shape, f32), jax.ShapeDtypeStruct(shape, bf16)],
-        compiler_params=pltpu.CompilerParams(vmem_limit_bytes=40 * MIB),
+        compiler_params=pltpu.CompilerParams(vmem_limit_bytes=20 * MIB),
         cost_estimate=cost(4),
         name="split_grad",
     )(left, left_far, right, right_far)
 
 
-def input_back_kernel(
-    q_ref,
-    k_ref,
-    k_came_ref,
-    v_ref,
-    v_came_ref,
-    before_ref,
-    w_ref,
-    near_ref,
-    far_ref,
-    grad_ref,
-    low_ref,
-    sums_ref,
-    mixed,
-    total,
-):
-    i = pl.program_id(0)
-    which = i // 2
-
-    @pl.when(i == 0)
-    def _():
-        total[...] = before_ref[...]
-
-    @pl.when(which == 0)
-    def _():
-        mixed[...] = q_ref[...]
-
-    @pl.when(which == 1)
-    def _():
-        mixed[...] = (k_ref[...] + k_came_ref[...].astype(f32)).astype(bf16)
-
-    @pl.when(which == 2)
-    def _():
-        mixed[...] = (v_ref[...] + v_came_ref[...].astype(f32)).astype(bf16)
-
-    @pl.when(i % 2 == 0)
-    def _():
-        near_ref[...] = mixed[...]
-
-    @pl.when(i % 2 == 1)
-    def _():
-        far_ref[...] = mixed[...]
-
-    sums_ref[0] = jnp.sum(mixed[...].astype(f32), 0, keepdims=True)
-    total[...] += dotf(mixed[...], w_ref[...])
-
-    @pl.when(i == 5)
-    def _():
-        grad_ref[...] = total[...]
-        low_ref[...] = total[...].astype(bf16)
-
-
-def input_back(grads, came, before, qkv, part=0, parts=1):
-    q, k, v = grads
-    k_came, v_came = came
-    rows, model = q.shape
-    rows //= parts
+IN_VMEM = pl.BlockSpec(memory_space=pltpu.VMEM)
+
+
+def project_kernel(x_ref, near_ref, far_ref, bias_ref, q_ref, kv_ref):
+    inputs = x_ref[...]
+    half = near_ref.shape[1]
+    for which in range(3):
+        for side, ref in enumerate((near_ref, far_ref)):
+            made = dotf(inputs, ref[which], NT) + bias_ref[2 * which + side]
+            first = half * side + 2 * half * max(which - 1, 0)
+            out_ref = kv_ref if which else q_ref
+            out_ref[:, first : first + half] = made.astype(bf16)
+
+
+def project(inputs, near, far, bias):
+    rows, model = inputs.shape
+    return pl.pallas_call(
+        project_kernel,
+        in_specs=[IN_VMEM] * 4,
+        out_specs=[IN_VMEM] * 2,
+        out_shape=[
+            jax.ShapeDtypeStruct((rows, model), bf16),
+            jax.ShapeDtypeStruct((rows, 2 * model), bf16),
+        ],
+        compiler_params=pltpu.CompilerParams(vmem_limit_bytes=16 * MIB),
+        cost_estimate=cost(4),
+        name="project",
+    )(inputs, near, far, bias)
+
+
+def input_back_kernel(*refs):
+    q_ref, k_ref, k_came_ref, v_ref, v_came_ref, before_ref, *weights = refs[:8]
+    near_ref, far_ref, grad_ref, low_ref, sums_ref = refs[8:]
+    half = near_ref.shape[1] // 3
+    total = before_ref[...]
+    for which in range(3):
+        for side in range(2):
+            cols = slice(half * side, half * side + half)
+            other = slice(half * (1 - side), half * (1 - side) + half)
+            if which == 0:
+                mixed = q_ref[:, cols]
+            else:
+                own, came = (k_ref, k_came_ref) if which == 1 else (v_ref, v_came_ref)
+                mixed = (own[:, cols] + came[:, other].astype(f32)).astype(bf16)
+            (far_ref if side else near_ref)[:, half * which : half * which + half] = mixed
+            sums_ref[2 * which + side] = jnp.sum(mixed.astype(f32), 0, keepdims=True)
+            total = total + dotf(mixed, weights[side][which])
+    grad_ref[...] = total
+    low_ref[...] = total.astype(bf16)
+
+
+def input_back(q, k, k_came, v, v_came, before, near, far):
+    rows, model = before.shape
     half = model // 2
-
-    def at(first, turn=False):
-        def index(i):
-            step = jnp.clip(i - first, 0, 1)
-            return part, (1 - step if turn else step)
-
-        return pl.BlockSpec((rows, half), index)
-
-    split = pl.BlockSpec((rows, half), lambda i: (0, i // 2))
-    full = pl.BlockSpec((rows, model), lambda i: (0, 0))
     return pl.pallas_call(
         input_back_kernel,
-        grid=(6,),
-        in_specs=[
-            at(0),
-            at(2),
-            at(2, True),
-            at(4),
-            at(4, True),
-            pl.BlockSpec((rows, model), lambda i: (part, 0)),
-            pl.BlockSpec((half, model), lambda i: (i, 0)),
-        ],
-        out_specs=[split, split, full, full, pl.BlockSpec((1, 1, half), lambda i: (i, 0, 0))],
+        in_specs=[IN_VMEM] * 8,
+        out_specs=[IN_VMEM] * 5,
         out_shape=[
             jax.ShapeDtypeStruct((rows, 3 * half), bf16),
             jax.ShapeDtypeStruct((rows, 3 * half), bf16),
@@ -725,11 +702,10 @@
             jax.ShapeDtypeStruct((rows, model), bf16),
             jax.ShapeDtypeStruct((6, 1, half), f32),
         ],
-        scratch_shapes=[pltpu.VMEM((rows, half), bf16), pltpu.VMEM((rows, model), f32)],
-        compiler_params=pltpu.CompilerParams(vmem_limit_bytes=40 * MIB),
+        compiler_params=pltpu.CompilerParams(vmem_limit_bytes=24 * MIB),
         cost_estimate=cost(6),
         name="input_back",
-    )(q, k, k_came, v, v_came, before, qkv)
+    )(q, k, k_came, v, v_came, before, near, far)
 
 
 def body(
@@ -793,72 +769,67 @@
 
     qkv_own = qkv_weight[0].transpose(1, 2, 0)
     out_own, up_own, down_own = out_weight[0], up_weight[0], down_weight[0]
-    x_sent, qkv_sent = theirs(hidden), own_half(qkv_own, 1)
     small = jnp.concatenate([qv_bias[0].reshape(-1), ffn_bias[0], bias_table[0].reshape(-1)])
 
-    def first_stage():
+    def send_small():
+        return swap_y(small), theirs(hidden), own_half(qkv_own, 1)
+
+    small_y, x_sent, qkv_sent = stage(send_small)
+
+    def gather_small():
+        two = jnp.stack([small, small_y])
+        four = jnp.concatenate([two, swap_c(two)])
+        table = four[:, 2 * cols + width :].reshape(8 * heads, kinds)
+        turned = lax.dynamic_slice_in_dim(jnp.pad(buckets, (1, 0)), 256 * core, SPAN, 0)
+        onehot = (turned[:, None] == jnp.arange(kinds, dtype=jnp.int32)[None, :]).astype(f32)
+        window = lax.dot_general(table, onehot, NT, precision=lax.Precision.HIGHEST)
+        qv_all = four[:, : 2 * cols].reshape(4, 2, cols)
+        q_bias, v_bias = qv_all[:, 0].reshape(-1), qv_all[:, 1].reshape(-1)
+        bias = jnp.concatenate([q_bias, jnp.zeros((model,), f32), v_bias])
+        info = jnp.stack([mine(query_lengths), core, mine(pair_lengths)]).astype(jnp.int32)
         return (
-            swap_y(x_sent),
-            swap_y(small),
-            swap_y(qkv_sent),
+            window.reshape(2 * heads, 2, 2, SPAN),
+            onehot,
+            bias.reshape(6, 1, 2 * cols),
+            four[:, 2 * cols : 2 * cols + width].reshape(4, 1, width),
+            info,
             own_half(out_own),
             own_half(up_own),
             own_half(down_own),
         )
 
-    x_came, small_y, qkv_y, out_sent, up_sent, down_sent = stage(first_stage)
-    onehot = (buckets[:, None] == jnp.arange(kinds, dtype=jnp.int32)[None, :]).astype(f32)
-    onehot = jnp.pad(onehot, ((1, 0), (0, 0)))
-    onehot = lax.dynamic_slice_in_dim(onehot, 256 * core, SPAN, 0)
+    x_came, qkv_y, found = stage(lambda: (swap_y(x_sent), swap_y(qkv_sent), stage(gather_small)))
+    window, onehot, bias, up_bias, info, out_sent, up_sent, down_sent = found
+    w = dict(up_bias=up_bias, gains=norm_gains[0], shifts=vectors[0])
 
     def second_stage():
-        two = jnp.stack([small, small_y])
-        four = jnp.concatenate([two, swap_c(two)])
-        table = four[:, 2 * cols + width :].reshape(8 * heads, kinds)
-        window = lax.dot_general(table, onehot, NT, precision=lax.Precision.HIGHEST)
-        window = window.reshape(2 * heads, 2, 2, SPAN)
-        return swap_y(out_sent), swap_y(up_sent), swap_z(qkv_y), four, window
-
-    out_y, up_y, qkv_z, small, window = stage(second_stage)
-    qv_all = small[:, : 2 * cols].reshape(4, 2, cols)
-    q_bias = qv_all[:, 0].reshape(-1)
-    kv_bias = jnp.concatenate([jnp.zeros((model,), f32), qv_all[:, 1].reshape(-1)])
-    info = jnp.stack([mine(query_lengths), core, mine(pair_lengths)]).astype(jnp.int32)
-    w = dict(
-        up_bias=small[:, 2 * cols : 2 * cols + width].reshape(4, 1, width),
-        gains=norm_gains[0],
-        shifts=vectors[0],
-    )
-
-    def project(inputs, qkv):
-        mixed = dotf(inputs, qkv, NT)
-        kv = (mixed[:, model:] + kv_bias).astype(bf16)
-        return (mixed[:, :model] + q_bias).astype(bf16), kv
+        x0 = in_order(y == 0, mine(hidden), x_came)
+        return swap_z(qkv_y), swap_y(out_sent), swap_y(up_sent), x0
+
+    qkv_z, out_y, up_y, x0 = stage(second_stage)
+
+    def gather_qkv():
+        near = jnp.concatenate([qkv_own, in_order(odd == 0, qkv_y, qkv_z, 1)], 1)
+        far = swap_c(near)
+        q, kv = project(x0, near, far, bias)
+        return (near, far), q, kv, swap_c(kv)
 
     def third_stage():
-        x0 = in_order(y == 0, mine(hidden), x_came)
-        qkv = jnp.concatenate([qkv_own, in_order(odd == 0, qkv_y, qkv_z, 1)], 1)
-        qkv = jnp.concatenate([qkv, swap_c(qkv)], 1).reshape(3 * model, model)
-        q, kv = project(x0, qkv)
-        kv_other = swap_c(kv)
-        attended, _ = attend_forward(info, q, kv, kv_other, window)
-        return x0, qkv, attended, swap_z(out_y), swap_z(up_y), swap_y(down_sent)
-
-    x0, qkv, attended, out_z, up_z, down_y = stage(third_stage)
+        return stage(gather_qkv), swap_y(down_sent), swap_z(out_y), swap_z(up_y)
+
+    (qkv, q, kv, kv_other), down_y, out_z, up_z = stage(third_stage)
+    out = jnp.concatenate([out_own, in_order(odd == 0, out_y, out_z)], 0)
+    up = jnp.stack([up_own, in_order(odd == 0, up_y, up_z)])
 
     def fourth_stage():
-        out = jnp.concatenate([out_own, in_order(odd == 0, out_y, out_z)], 0)
-        up = jnp.stack([up_own, in_order(odd == 0, up_y, up_z)])
-        return jnp.concatenate([out, swap_c(out)], 0), up, swap_c(up), swap_z(down_y)
-
-    w["out"], up, up_far, down_z = stage(fourth_stage)
+        found = stage(lambda: attend_forward(info, q, kv, kv_other, window)[0])
+        return swap_z(down_y), swap_c(out), swap_c(up), found
+
+    down_z, out_far, up_far, attended = stage(fourth_stage)
+    down = jnp.stack([down_own, in_order(odd == 0, down_y, down_z)])
+    w["down"] = down, stage(lambda: swap_c(down))
+    w["out"] = jnp.concatenate([out, out_far], 0)
     w["up"] = up, up_far
-
-    def fifth_stage():
-        down = jnp.stack([down_own, in_order(odd == 0, down_y, down_z)])
-        return down, swap_c(down)
-
-    w["down"] = stage(fifth_stage)
 
     def to_next(value):
         return lax.ppermute(value, "section", [(0, 1)])
@@ -870,18 +841,14 @@
     came_a, middle = stage(
         lambda: (to_next(middle), ffn_forward(w, attended, x0, False, 1, 2)[0])
     )
-    x_a = jnp.where(leading, x0[:local], came_a)
-    came_b, (q_a, kv_a) = stage(lambda: (to_next(middle), project(x_a, qkv)))
-
-    def seventh_stage():
-        x_b = jnp.where(leading, x0[local:], came_b)
-        q_b, kv_b = project(x_b, qkv)
-        kv = jnp.concatenate([kv_a, kv_b], 0)
-        kv_other = swap_c(kv)
-        x1, q = jnp.concatenate([x_a, x_b], 0), jnp.concatenate([q_a, q_b], 0)
-        return x1, q, kv, kv_other
-
-    x1, q, kv, kv_other = stage(seventh_stage)
+    came_b = stage(lambda: to_next(middle))
+
+    def project_again():
+        x1 = jnp.where(leading, x0, jnp.concatenate([came_a, came_b], 0))
+        q, kv = project(x1, *qkv, bias)
+        return x1, q, kv, swap_c(kv)
+
+    x1, q, kv, kv_other = stage(project_again)
     top_sent = theirs(cotangent)
 
     def eighth_stage():
@@ -915,16 +882,14 @@
         )
 
     normed_far, active_far, attended_far, grads = stage(ninth_stage)
-    *qkv_grads, k_far, v_far = attention_back(grads, False, 0, 6)
-    came = stage(lambda: (swap_c(k_far), swap_c(v_far)))
-
-    def back(part, parts):
-        return input_back(qkv_grads, came, grads["before"], qkv, part, parts)
-
-    grad_a = back(0, 2)[3]
-    came_a, grad_b = stage(lambda: (to_last(grad_a), back(1, 2)[3]))
-    came_b = stage(lambda: to_last(grad_b))
-    grad_y = jnp.where(leading, jnp.concatenate([came_a, came_b], 0), grad_top)
+    grad_q, grad_k, grad_v, k_far, v_far = attention_back(grads, False, 0, 6)
+
+    def to_middle():
+        k_came, v_came = swap_c(k_far), swap_c(v_far)
+        found = input_back(grad_q, grad_k, k_came, grad_v, v_came, grads["before"], *qkv)
+        return to_last(found[3])
+
+    grad_y = jnp.where(leading, stage(to_middle), grad_top)
 
     thirds = width // 3
 
@@ -933,59 +898,59 @@
             active, active_far, second, second_far, kind, (first, 3, thirds), (0, 1, model)
         )
 
-    def up_grad(kind, first):
-        return weight_grad(
-            normed_low, normed_far, hidden, hidden_far, kind, (0, 3, thirds), (first, 1, width)
-        )
-
-    def hops(value):
-        if planes != 4:
-            return lax.psum(value, "dp")
-        value = value + lax.ppermute(value, "dp", [(0, 1), (3, 2)])
-        value = value + lax.ppermute(value, "dp", [(1, 2), (2, 1)])
-        back = lax.ppermute(value, "dp", [(1, 0), (2, 3)])
-        return jnp.where((plane == 1) | (plane == 2), value, back)
-
     after, second, top_sums = top_back(w, saved, grad_y)
-    second_far, grads = stage(lambda: (swap_c(second), dense_back(after, second)))
+    second_far = stage(lambda: swap_c(second))
+    down_sent = down_grad(bf16, 3)
+
+    def through_dense():
+        return dense_back(after, second), down_grad(f32, 0)
+
+    down_came, (grads, down_kept) = stage(lambda: (swap_y(down_sent), stage(through_dense)))
     hidden, branch = grads["hidden"], grads["branch"]
-
-    def stage_2():
-        return swap_c(hidden[:, 2 * width :]), swap_c(branch), down_grad(bf16, 3)
-
-    hidden_far, branch_far, down_sent = stage(stage_2)
-    up_sent = up_grad(bf16, 1)
-    out_kept, out_sent = split_grad(attended, attended_far, branch, branch_far, 2 * cols)
-
-    def stage_3():
-        return (
-            swap_y(down_sent),
-            swap_y(up_sent),
-            swap_y(out_sent),
-            attention_back(grads, True, 0, 6),
-            down_grad(f32, 0),
-            up_grad(f32, 0),
-        )
-
-    *came, found, down_kept, up_kept = stage(stage_3)
-    *qkv_grads, k_far, v_far, held = found
-    kept = (down_kept, up_kept, out_kept)
-    later = [(own + other.astype(f32)).astype(bf16) for own, other in zip(kept, came)]
-
-    def stage_4():
-        summed = lax.psum(later, "dp")
+    low_sum = lambda own, came: (own + came.astype(f32)).astype(bf16)
+    down = low_sum(down_kept, down_came)
+
+    def exchange_dense():
+        return swap_c(hidden[:, 2 * width :]), swap_c(branch)
+
+    def send_dense(hidden_far, branch_far):
+        args = normed_low, normed_far, hidden, hidden_far
+        sent = weight_grad(*args, bf16, (0, 3, thirds), (1, 1, width))
+        return sent, split_grad(attended, attended_far, branch, branch_far, 2 * cols)
+
+    def through_attention(hidden_far):
+        args = normed_low, normed_far, hidden, hidden_far
+        kept = weight_grad(*args, f32, (0, 3, thirds), (0, 1, width))
+        return attention_back(grads, True, 0, 6), kept
+
+    def through_input(q_grad, k_grad, v_grad, k_far, v_far):
+        came = swap_c(k_far), swap_c(v_far)
         near, far, grad_input, grad_low, qv_sums = input_back(
-            qkv_grads, (swap_c(k_far), swap_c(v_far)), grads["before"], qkv
+            q_grad, k_grad, came[0], v_grad, came[1], grads["before"], *qkv
         )
         rest_kept, rest_sent = split_grad(near, swap_c(far), x1, inputs_far, 2 * cols)
+        return rest_kept, rest_sent, grad_input, grad_low, qv_sums
+
+    def after_down():
+        hidden_far, branch_far = stage(exchange_dense)
+        up_sent, (out_kept, out_sent) = stage(lambda: send_dense(hidden_far, branch_far))
+        up_came, out_came, (found, up_kept) = stage(
+            lambda: (
+                swap_y(up_sent),
+                swap_y(out_sent),
+                stage(lambda: through_attention(hidden_far)),
+            )
+        )
+        return found, low_sum(up_kept, up_came), low_sum(out_kept, out_came)
+
+    def after_up():
+        rest_kept, rest_sent, *found = stage(lambda: through_input(*attention_found))
+        return low_sum(rest_kept, stage(lambda: swap_y(rest_sent))), found
+
+    def through_sums(held, qv_sums, grad_low):
         edge_low = edge_blocks(jnp.where(leading, grad_low, result.astype(bf16)))
         edge_came = swap_y(theirs(edge_low))
-        parts = []
-        for which in range(3):
-            rows = slice(which * cols, which * cols + cols)
-            rest = rest_kept[rows] + swap_y(rest_sent[rows]).astype(f32)
-            parts.append(hops(rest.astype(bf16)))
-        sums = token_sums(qv_sums)
+        sums = token_sums(held, qv_sums)
         sums = sums[:2] + swap_c(sums[2:])
         sums = sums[0] + swap_y(sums[1])
         if planes == 4:
@@ -993,11 +958,11 @@
             sums = sums + lax.ppermute(sums, "dp", [(0, 2), (2, 0), (1, 3), (3, 1)])
         else:
             sums = lax.psum(sums, "dp")
-        return summed, parts, sums, grad_input, edge_came
+        return sums, edge_came
 
     share = model // 4
 
-    def token_sums(qv_sums):
+    def token_sums(held, qv_sums):
         wide = jnp.pad(held.reshape(4 * heads, 2, 8, SPAN), ((0, 0), (0, 0), (0, 0), (0, 8)))
         sums = sum(wide[:, :, s, s : s + SPAN] for s in range(8))
         sums = jnp.stack([sums[:, 0] - sums[:, 1], sums[:, 1]], 1).reshape(8 * heads, SPAN)
@@ -1014,9 +979,15 @@
         )
         return jnp.concatenate([grad_table, q_sums, v_sums, grad_ffn, by_share], 1)
 
-    summed, parts, sums, grad_input, edge_came = stage(stage_4)
-    grad_down, grad_up, grad_out = [value.astype(f32) for value in summed]
-    grad_qkv = jnp.stack(parts).astype(f32)
+    grad_down, (found, *later) = stage(lambda: (lax.psum(down, "dp"), stage(after_down)))
+    *attention_found, held = found
+    summed, (rest, found) = stage(lambda: (lax.psum(later, "dp"), stage(after_up)))
+    grad_input, grad_low, qv_sums = found
+    grad_qkv, (sums, edge_came) = stage(
+        lambda: (lax.psum(rest, "dp"), stage(lambda: through_sums(held, qv_sums, grad_low)))
+    )
+    grad_down, grad_qkv = grad_down.astype(f32), grad_qkv.astype(f32)
+    grad_up, grad_out = [value.astype(f32) for value in summed]
     edge_own = mine(edge_blocks(jnp.where(leading, grad_input, result)))
     edge_came = edge_came.astype(f32)
     edges = jnp.stack([jnp.where(y == 0, edge_own, edge_came), jnp.where(y == 0, edge_came, edge_own)])

time: 566 us -> 532 us (0.940)
  starting transfers between devices: 57.6 us -> 34.9 us
  matrix products: 13.1 us -> 2.09 us
  local copies, waits for them, and re-layouts: 45.3 us -> 36.1 us
  Pallas kernels: 211 us -> 220 us
    ppermute x10 -> x1, waiting for transfers between devices: 27.3 us -> 0.41 us  [through_sums(): sums = sums + lax.ppermute(sums, 'dp', [(0, 2), (2, 0), (1, 3), (3, 1)])]
    ppermute x20, waiting for transfers between devices: 12.3 us -> 32.3 us  [swap_c(): return lax.ppermute(value, 'tensor', SWAP_C)]
    ppermute x10 -> x1, starting transfers between devices: 19.9 us -> 1.62 us  [through_sums(): sums = sums + lax.ppermute(sums, 'dp', [(0, 2), (2, 0), (1, 3), (3, 1)])]
    ppermute x5, waiting for transfers between devices: 13.7 us -> 0.75 us  [swap_z(): return lax.ppermute(value, 'dp', [(i, i ^ 1) for i in range(planes)])]
    dot_general x4 -> x1, matrix products: 11.4 us -> 0.9 us  [gather_small(): window = lax.dot_general(table, onehot, NT, precision=lax.Precision.HIGHEST)]
    cond x63 -> x4, local copies, waits for them, and re-layouts: 9.72 us -> 1.05 us
    convert_element_type x12 -> x9, other arithmetic: 7.05 us -> 15.3 us  [the longest x8 14.6 us: body(): low_sum = lambda own, came: (own + came.astype(f32)).astype(bf16)]
    psum x1 -> x3, waiting for transfers between devices: 24.1 us -> 30.5 us  [the longest x1 22.4 us: body(): lax.psum(later, 'dp')]
  transfers between devices with their start and end apart: 55 -> 45, of which waited for: 23 -> 24; matrix products, arithmetic and copies ran while one was open for 11% -> 12% of each run, Pallas kernels for 25% -> 27%
where the time goes in v1:
time: 532 us; the launch traced here: 521 us
  Pallas kernels  220 us (41%)
  waiting for transfers between devices  146 us (27%)
  other arithmetic  64.3 us (12%)
  local copies, waits for them, and re-layouts  36.1 us (7%)
  starting transfers between devices  34.9 us (7%)
  between operations  15.2 us (3%)
    pallas_call x2, Pallas kernels, attend_backward(): pl.pallas_call(functools.partial(backward_kernel, with_table), grid_spec=...  60.4 us
    ppermute x13, waiting for transfers between devices, swap_y(): return lax.ppermute(value, 'tensor', SWAP_Y)  53.2 us
    pallas_call x2, Pallas kernels, attend_forward(): pl.pallas_call(forward_kernel, grid_spec=pltpu.PrefetchScalarGridSpec(num...  38 us
    pallas_call x3, Pallas kernels, ffn_forward(): pl.pallas_call(functools.partial(ffn_forward_kernel, keep), grid=(4,), in...  36.3 us
    ppermute x20, waiting for transfers between devices, swap_c(): return lax.ppermute(value, 'tensor', SWAP_C)  32.3 us
    pallas_call x2, Pallas kernels, ffn_backward(): pl.pallas_call(functools.partial(ffn_backward_kernel, len(deps)), grid=(4...  27.7 us
    psum x1, waiting for transfers between devices, body(): lax.psum(later, 'dp')  22.4 us
    ppermute x1, waiting for transfers between devices, to_last(): return lax.ppermute(value, 'section', [(1, 0)])  20.8 us
  transfers between devices with their start and end apart: 45, of which 24 were waited for; matrix products, arithmetic and copies ran while one was open for 12% of the time, Pallas kernels for 27%

profile of v1, /device:TPU:0, one launch (start us, length us, event | category | flops | bytes accessed | tf_op | source)
XLA Modules:
  0.0 521.4 jit_solution(17666783563554725449)
XLA Ops:
  16.3 20.2 %conditional.31 = (bf16[256,768]{1,0:T(8,128)(2,1)}, bf16[3,96,768]{2,1,0:T(8,128)(2,1)}, f32[6,2,2,1792]{3,0,2,1:T(8,128)}, f32[1792,32]{0,1:T(8,128)}, f32[6,1...) conditional(s32[]{:T(128)} %bitcast.27, () %tuple.269, ...), branch_computations={%region_2.3_spmd, %region_3.6_spmd} | conditional | flops 16705180 | bytes 6686416 | solution.py:764
  37.6 17.4 %conditional.32 = (bf16[3,96,768]{2,1,0:T(8,128)(2,1)}, bf16[96,768]{1,0:T(8,128)(2,1)}, bf16[384,768]{1,0:T(8,128)(2,1)}, bf16[512,768]{1,0:T(8,128)(2,1)S(1)}) conditional(s32[]{:T(128)} %bitcast.27, () %tuple.277, (bf16[3,96,768]{2,1,0:T(8,128)(2,1)}, bf16[96,768]{1,0:T(8,128)(2,1)}, bf16[384,768]{1,0:T(8,128)(2,1)}, s32[]{:T(128)}, ...), branch_computations={%region_6.7_spmd, %region_7.8_spmd} | conditional | flops 1966084 | bytes 7864520 | solution.py:764
  55.0 18.7 %conditional.33 = (bf16[3,384,768]{2,1,0:T(8,128)(2,1)}, bf16[3,384,768]{2,1,0:T(8,128)(2,1)}, bf16[512,768]{1,0:T(8,128)(2,1)}, bf16[512,1536]{1,0:T(8,128)(2,1...) conditional(s32[]{:T(128)} %bitcast.27, () %tuple.276, ...), branch_computations={%region_8.9_spmd, %region_9.12_spmd} | conditional | flops 5750787 | bytes 37604984 | solution.py:764
  57.5 16.2 %conditional.1 = (bf16[3,384,768]{2,1,0:T(8,128)(2,1)}, bf16[3,384,768]{2,1,0:T(8,128)(2,1)}, bf16[512,768]{1,0:T(8,128)(2,1)}, bf16[512,1536]{1,0:T(8,128)(2,1)}, bf16[512,1536]{1,0:T(8,128)(2,1)}) conditional(s32[]{:T(128)} %bitcast.9, () %tuple.172, (s32[]{:T(128)}, bf16[3,96,768]{2,1,0:T(8,128)(2,1)}, bf16[3,96,768]{2,1,0:T(8,128)(2,1)}, ...), branch_computations={%region_10.10_spmd, %region_11.11_spmd} | conditional | flops 5750785 | bytes 32296322 | solution.py:764
  77.8 22.1 %conditional.34 = (bf16[384,768]{1,0:T(8,128)(2,1)}, bf16[384,768]{1,0:T(8,128)(2,1)}, bf16[2,768,768]{2,1,0:T(8,128)(2,1)}, bf16[512,768]{1,0:T(8,128)(2,1)}) conditional(s32[]{:T(128)} %bitcast.27, () %tuple.275, (bf16[384,768]{1,0:T(8,128)(2,1)}, bf16[384,768]{1,0:T(8,128)(2,1)S(1)}, bf16[2,768,768]{2,1,0:T(8,128)(2,1)}, s32[2]{0:T(128)S(1)}, ...), branch_computations={%region_12.13_spmd, %region_13.16_spmd} | conditional | flops 2 | bytes 72300056 | solution.py:764
  80.0 20.0 %conditional.2 = (bf16[512,768]{1,0:T(8,128)(2,1)}) conditional(s32[]{:T(128)} %bitcast.10, () %tuple.176, (s32[3]{0:T(128)}, bf16[512,768]{1,0:T(8,128)(2,1)}, bf16[512,1536]{1,0:T(8,128)(2,1)}, bf16[512,1536]{1,0:T(8,128)(2,1)}, f32[6,2,2,1792]{3,0,2,1:T(8,128)}) %tuple.177), branch_computations={%region_14.14_spmd, %region_15.15_spmd} | conditional | bytes 58144072 | solution.py:764
  81.0 18.9 %attend_forward.2 = (bf16[512,768]{1,0:T(8,128)(2,1)}, f32[6,2,512]{2,1,0:T(2,128)}) custom-call(s32[3]{0:T(128)} %get-tuple-element.677.info_ref, bf16[512,768]{1,0:T(8,128)(2,1)} %get-tuple-element.678.q_ref, bf16[512,1536]{1,0:T(8,128)(2,1)} %get-tuple-element.679.k_ref.v_ref, bf16[512,1536]{1,0:T(8,128)(2,1)} %get-tuple-element.679.k_ref.v_ref, ...), custom_call_target="tpu_custom_call" | custom-call | bytes 57800000 | tf_op jit(solution)/shard_map/cond/branch_1_fun/cond/branch_1_fun/attend_forward/pallas_call | solution.py:181
  120.0 14.1 %conditional.36 = (bf16[256,768]{1,0:T(8,128)(2,1)}, bf16[256,768]{1,0:T(8,128)(2,1)S(1)}) conditional(s32[]{:T(128)} %bitcast.27, () %tuple.274, (bf16[256,768]{1,0:T(8,128)(2,1)S(1)}, bf16[512,768]{1,0:T(8,128)(2,1)}, bf16[512,768]{1,0:T(8,128)(2,1)S(1)}, bf16[768,768]{1,0:T(8,128)(2,1)S(1)}, bf16[2,768,768]{2,1,0:T(8,128)(2,1)}, ...), branch_computations={%region_18.19_spmd, %region_19.20_spmd} | conditional | bytes 52597496 | solution.py:764
  157.2 22.2 %conditional.39 = (bf16[256,768]{1,0:T(8,128)(2,1)}, bf16[512,768]{1,0:T(8,128)(2,1)}, bf16[512,768]{1,0:T(8,128)(2,1)}, f32[6,2,512]{2,1,0:T(2,128)S(1)}) conditional(s32[]{:T(128)} %bitcast.27, () %tuple.286, (s32[]{:T(128)}, bf16[2,256,768]{2,1,0:T(8,128)(2,1)S(1)}, bf16[512,768]{1,0:T(8,128)(2,1)}, s32[3]{0:T(128)}, ...), branch_computations={%region_24.25_spmd, %region_25.26_spmd} | conditional | flops 4 | bytes 63649248 | solution.py:764
  160.2 19.0 %attend_forward.3 = (bf16[512,768]{1,0:T(8,128)(2,1)}, f32[6,2,512]{2,1,0:T(2,128)S(1)}) custom-call(s32[3]{0:T(128)} %get-tuple-element.715.info_ref, bf16[512,768]{1,0:T(8,128)(2,1)} %get-tuple-element.716.q_ref, bf16[512,1536]{1,0:T(8,128)(2,1)} %get-tuple-element.717.k_ref.v_ref, bf16[512,1536]{1,0:T(8,128)(2,1)} %get-tuple-element.717.k_ref.v_ref, ...), custom_call_target="tpu_custom_call" | custom-call | bytes 57800000 | tf_op jit(solution)/shard_map/cond/branch_1_fun/attend_forward/pallas_call | solution.py:181
  181.7 17.3 %ffn_forward.5 = (f32[512,768]{1,0:T(8,128)}, bf16[512,768]{1,0:T(8,128)(2,1)}, bf16[512,3072]{1,0:T(8,128)(2,1)S(1)}, bf16[512,3072]{1,0:T(8,128)(2,1)}, f32[51...) custom-call(bf16[512,768]{1,0:T(8,128)(2,1)S(1)} %copy-done.7, ...), custom_call_target="tpu_custom_call" | custom-call | bytes 51000000 | tf_op jit(solution)/shard_map/ffn_forward/pallas_call | solution.py:426
  200.7 14.4 %conditional.40 = (bf16[512,768]{1,0:T(8,128)(2,1)}, bf16[512,1536]{1,0:T(8,128)(2,1)}, bf16[512,384]{1,0:T(8,128)(2,1)}, bf16[512,768]{1,0:T(8,128)(2,1)S(1)}, f32[512,768]{1,0:T(8,128)S(1)}) conditional(s32[]{:T(128)} %bitcast.27, () %tuple.285, (bf16[512,768]{1,0:T(8,128)(2,1)}, bf16[512,3072]{1,0:T(8,128)(2,1)S(1)}, ...), branch_computations={%region_26.27_spmd, %region_27.28_spmd} | conditional | bytes 65942368 | solution.py:764
  201.6 13.3 %ffn_backward.2 = (bf16[512,3072]{1,0:T(8,128)(2,1)}, f32[512,768]{1,0:T(8,128)S(1)}, bf16[512,768]{1,0:T(8,128)(2,1)}, bf16[512,768]{1,0:T(8,128)(2,1)S(1)}, f32[8,768]{1,0:T(8,128)}, /*index=5*/f32[4,1,768]{2,1,0:T(1,128)}) custom-call(f32[512,768]{1,0:T(8,128)S(1)} %get-tuple-element.725.refs_0_, bf16[512,768]{1,0:T(8,128)(2,1)S(1)} %get-tuple-element.726.refs_1_, ...), custom_call_target="tpu_custom_call" | custom-call | bytes 51000000 | tf_op jit(solution)/shard_map/cond/branch_1_fun/ffn_backward/pallas_call | solution.py:546
  215.1 28.5 %attend_backward.3 = (bf16[512,768]{1,0:T(8,128)(2,1)}, f32[512,768]{1,0:T(8,128)}, f32[512,768]{1,0:T(8,128)}, bf16[512,768]{1,0:T(8,128)(2,1)}, bf16[512,768]{1,0:T(8,128)(2,1)}) custom-call(s32[3]{0:T(128)} %get-tuple-element.1072.refs_0_, bf16[512,768]{1,0:T(8,128)(2,1)} %get-tuple-element.1099.refs_1_, ...), custom_call_target="tpu_custom_call" | custom-call | bytes 102000000 | tf_op jit(solution)/shard_map/attend_backward/pallas_call | solution.py:284
  243.7 33.0 %conditional.41 = (bf16[512,768]{1,0:T(8,128)(2,1)}) conditional(s32[]{:T(128)} %bitcast.27, () %tuple.268, (bf16[512,768]{1,0:T(8,128)(2,1)}, bf16[512,768]{1,0:T(8,128)(2,1)}, bf16[512,768]{1,0:T(8,128)(2,1)}, f32[512,768]{1,0:T(8,128)}, f32[512,768]{1,0:T(8,128)}, /*index=5*/f32[512,768]{1,0:T(8,128)S(1)}, bf16[3,384,768]{2,1,0:T(8,128)(2,1)}, ...), branch_computations={%region_28.29_spmd, %region_29.30_spmd} | conditional | bytes 29837312 | solution.py:764
  255.9 20.8 %collective-permute-done.11 = bf16[512,768]{1,0:T(8,128)(2,1)} collective-permute-done((bf16[512,768]{1,0:T(8,128)(2,1)S(1)}, bf16[512,768]{1,0:T(8,128)(2,1)}, u32[]{:S(2)}, u32[]{:S(2)}) %collective-permute-start.11) | collective-permute-done | bytes 786464 | tf_op jit(solution)/shard_map/cond/branch_1_fun/ppermute | solution.py:838
  287.9 30.0 %conditional.43 = (bf16[512,768]{1,0:T(8,128)(2,1)}, f32[512,768]{1,0:T(8,128)}, bf16[512,768]{1,0:T(8,128)(2,1)}, bf16[512,3072]{1,0:T(8,128)(2,1)}, f32[4,1,76...) conditional(s32[]{:T(128)} %bitcast.27, () %tuple.267, ...), branch_computations={%region_32.33_spmd, %region_33.36_spmd} | conditional | flops 589826 | bytes 72857824 | solution.py:764
  288.3 19.0 %conditional.3 = (bf16[512,768]{1,0:T(8,128)(2,1)}, f32[512,768]{1,0:T(8,128)}, bf16[512,768]{1,0:T(8,128)(2,1)}, bf16[512,3072]{1,0:T(8,128)(2,1)}, f32[4,1,768...) conditional(s32[]{:T(128)} %bitcast.12, () %tuple.190, (f32[512,768]{1,0:T(8,128)}, ...), branch_computations={%region_34.34_spmd, %region_35.35_spmd} | conditional | bytes 64600056 | solution.py:764
  288.3 14.4 %ffn_backward.3 = (bf16[512,3072]{1,0:T(8,128)(2,1)}, f32[512,768]{1,0:T(8,128)}, bf16[512,768]{1,0:T(8,128)(2,1)}, bf16[512,768]{1,0:T(8,128)(2,1)}, f32[8,768]{1,0:T(8,128)}, /*index=5*/f32[4,1,768]{2,1,0:T(1,128)}) custom-call(f32[512,768]{1,0:T(8,128)} %get-tuple-element.747.refs_0_, bf16[512,768]{1,0:T(8,128)(2,1)S(1)} %get-tuple-element.748.refs_1_.r_ref, ...), custom_call_target="tpu_custom_call" | custom-call | bytes 51000000 | tf_op jit(solution)/shard_map/cond/branch_1_fun/cond/branch_1_fun/ffn_backward/pallas_call | solution.py:546
  322.0 64.5 %conditional.44 = (bf16[512,768]{1,0:T(8,128)(2,1)}, f32[512,768]{1,0:T(8,128)}, f32[512,768]{1,0:T(8,128)}, bf16[512,768]{1,0:T(8,128)(2,1)}, bf16[512,768]{1,0...) conditional(s32[]{:T(128)} %bitcast.27, () %tuple.266, ...), branch_computations={%region_36.37_spmd, %region_37.49_spmd} | conditional | flops 3391494 | bytes 188758112 | solution.py:764
  323.1 60.6 %conditional.8 = (bf16[512,768]{1,0:T(8,128)(2,1)}, f32[512,768]{1,0:T(8,128)}, f32[512,768]{1,0:T(8,128)}, bf16[512,768]{1,0:T(8,128)(2,1)}, bf16[512,768]{1,0:...) conditional(s32[]{:T(128)} %bitcast.15, () %tuple.212, ...), branch_computations={%region_38.38_spmd, %region_39.47_spmd} | conditional | flops 2211844 | bytes 173422400 | solution.py:764
  338.2 40.5 %conditional.7 = (bf16[512,768]{1,0:T(8,128)(2,1)}, f32[512,768]{1,0:T(8,128)}, f32[512,768]{1,0:T(8,128)}, bf16[512,768]{1,0:T(8,128)(2,1)}, bf16[512,768]{1,0:...) conditional(s32[]{:T(128)} %bitcast.14, () %tuple.205, ...), branch_computations={%region_44.43_spmd, %region_45.46_spmd} | conditional | flops 737282 | bytes 125922232 | solution.py:764
  340.3 36.9 %conditional.4 = (bf16[512,768]{1,0:T(8,128)(2,1)}, f32[512,768]{1,0:T(8,128)}, f32[512,768]{1,0:T(8,128)}, bf16[512,768]{1,0:T(8,128)(2,1)}, bf16[512,768]{1,0:...) conditional(s32[]{:T(128)} %bitcast.13, () %tuple.202, (s32[3]{0:T(128)}, ...), branch_computations={%region_46.44_spmd, %region_47.45_spmd} | conditional | bytes 115600056 | solution.py:764
  340.3 31.9 %attend_backward.2 = (bf16[512,768]{1,0:T(8,128)(2,1)}, f32[512,768]{1,0:T(8,128)}, f32[512,768]{1,0:T(8,128)}, bf16[512,768]{1,0:T(8,128)(2,1)}, bf16[512,768]{...) custom-call(s32[3]{0:T(128)} %get-tuple-element.802.refs_0_, bf16[512,768]{1,0:T(8,128)(2,1)} %get-tuple-element.803.refs_1_, ...), custom_call_target="tpu_custom_call" | custom-call | bytes 102000000 | tf_op jit(solution)/shard_map/cond/branch_1_fun/cond/branch_1_fun/cond/branch_1_fun/cond/branch_1_fun/attend_backward/pallas_call | solution.py:284
  386.6 72.7 %conditional.45 = (bf16[576,768]{1,0:T(8,128)(2,1)}, f32[512,768]{1,0:T(8,128)}, bf16[512,768]{1,0:T(8,128)(2,1)}, f32[6,1,384]{2,1,0:T(1,128)}, f32[1,768,768]{2,1,0:T(8,128)}, /*index=5*/f32[1,192,768]{2,1,0:T(8,128)}) conditional(s32[]{:T(128)} %bitcast.27, () %tuple.265, (s32[2]{0:T(128)S(1)}, bf16[512,768]{1,0:T(8,128)(2,1)}, ...), branch_computations={%region_49.50_spmd, %region_50.59_spmd} | conditional | flops 2801668 | bytes 68898448 | solution.py:764
  387.3 44.6 %conditional.11 = (bf16[576,768]{1,0:T(8,128)(2,1)}, f32[512,768]{1,0:T(8,128)}, bf16[512,768]{1,0:T(8,128)(2,1)}, f32[6,1,384]{2,1,0:T(1,128)}) conditional(s32[]{:T(128)} %bitcast.18, () %tuple.223, (s32[2]{0:T(128)S(1)}, bf16[512,768]{1,0:T(8,128)(2,1)}, bf16[512,768]{1,0:T(8,128)(2,1)}, bf16[512,768]{1,0:T(8,128)(2,1)}, f32[512,768]{1,0:T(8,128)}, ...), branch_computations={%region_51.51_spmd, %region_52.56_spmd} | conditional | flops 1327106 | bytes 55627216 | solution.py:764
  387.6 18.6 %conditional.9 = (f32[576,768]{1,0:T(8,128)S(1)}, f32[512,768]{1,0:T(8,128)}, bf16[512,768]{1,0:T(8,128)(2,1)}, f32[6,1,384]{2,1,0:T(1,128)}, bf16[576,768]{1,0:T(8,128)(2,1)S(1)}) conditional(s32[]{:T(128)} %bitcast.17, () %tuple.219, (bf16[512,768]{1,0:T(8,128)(2,1)}, bf16[512,768]{1,0:T(8,128)(2,1)}, bf16[512,768]{1,0:T(8,128)(2,1)}, ...), branch_computations={%region_53.52_spmd, %region_54.53_spmd} | conditional | bytes 45010208 | solution.py:764
  406.2 23.1 %conditional.10 = (f32[576,768]{1,0:T(8,128)}) conditional(s32[]{:T(128)} %bitcast.17, () %tuple.221, bf16[576,768]{1,0:T(8,128)(2,1)S(1)} %get-tuple-element.920), branch_computations={%region_55.54_spmd, %region_56.55_spmd} | conditional | flops 442368 | bytes 6193200 | solution.py:764
  406.4 21.6 %collective-permute-done.21 = bf16[576,768]{1,0:T(8,128)(2,1)S(1)} collective-permute-done((bf16[576,768]{1,0:T(8,128)(2,1)S(1)}, bf16[576,768]{1,0:T(8,128)(2,1)S(1)}, u32[]{:S(2)}, u32[]{:S(2)}) %collective-permute-start.21) | collective-permute-done | bytes 884768 | tf_op jit(solution)/shard_map/cond/branch_1_fun/cond/branch_1_fun/cond/branch_1_fun/ppermute | solution.py:37
  432.0 22.4 %all-reduce.9.cloned.1.call-done = (bf16[1,768,768]{2,1,0:T(8,128)(2,1)}, bf16[1,192,768]{2,1,0:T(8,128)(2,1)}) async-done(((bf16[1,768,768]{2,1,0:T(8,128)(2,1)}, bf16[1,192,768]{2,1,0:T(8,128)(2,1)}), (bf16[1,768,768]{2,1,0:T(8,128)(2,1)}, bf16[1,192,768]{2,1,0:T(8,128)(2,1)})) %all-reduce.9.cloned.1.call-update) | async-done | bytes 1474576 | tf_op jit(solution)/shard_map/cond/branch_1_fun/psum | solution.py:984
  461.0 48.6 %conditional.46 = (bf16[576,768]{1,0:T(8,128)(2,1)}, f32[2496]{0:T(1024)}, f32[384]{0:T(512)}, f32[768]{0:T(1024)}, f32[384]{0:T(512)}, /*index=5*/f32[192]{0:T(...) conditional(s32[]{:T(128)} %bitcast.27, () %tuple.294, ...), branch_computations={%region_59.60_spmd, %region_60.64_spmd} | conditional | flops 18346178 | bytes 16377357 | solution.py:764
  461.8 39.7 %conditional.12 = (f32[2496]{0:T(1024)}, f32[256,768]{1,0:T(8,128)}, f32[384]{0:T(512)}, f32[768]{0:T(1024)}, f32[384]{0:T(512)}, /*index=5*/f32[192]{0:T(256)},...) conditional(s32[]{:T(128)} %bitcast.26, () %tuple.229, ...), branch_computations={%region_62.62_spmd, %region_63.63_spmd} | conditional | flops 17903808 | bytes 11067159 | solution.py:764
  (286 shorter events, 355.1 us)
Async XLA Ops:
  10.4 5.9 %collective-permute-start.22 = (f32[1344]{0:T(1024)S(1)}, f32[1344]{0:T(1024)}, u32[]{:S(2)}, u32[]{:S(2)}) collective-permute-start(f32[1344]{0:T(1024)S(1)} %get-tuple-element.611), channel_id=1, source_target_pairs={{0,2},{2,0},{1,3},{3,1},{4,6},{6,4},{5,7},{7,5},{8,10},{10,8},{9,1... | collective-permute-start | bytes 16136 | tf_op jit(solution)/shard_map/cond/branch_1_fun/ppermute | solution.py:37
  16.3 20.2 %collective-permute-start.36 = (bf16[3,96,768]{2,1,0:T(8,128)(2,1)S(1)}, bf16[3,96,768]{2,1,0:T(8,128)(2,1)}, u32[]{:S(2)}, u32[]{:S(2)}) collective-permute-start(bf16[3,96,768]{2,1,0:T(8,128)(2,1)S(1)} %get-tuple-element.628), channel_id=1, source_target_pairs={{0,2},{2,0},{1,3},{3,1},{4,6},{6,4},{5,7},{7,5},{8,10},{10,8},{9,1... | collective-permute-start | bytes 1327112 | tf_op jit(solution)/shard_map/cond/branch_1_fun/ppermute | solution.py:37
  17.3 19.2 %collective-permute-start.35 = (bf16[256,768]{1,0:T(8,128)(2,1)}, bf16[256,768]{1,0:T(8,128)(2,1)}, u32[]{:S(2)}, u32[]{:S(2)}) collective-permute-start(bf16[256,768]{1,0:T(8,128)(2,1)} %get-tuple-element.627), channel_id=1, source_target_pairs={{0,2},{2,0},{1,3},{3,1},{4,6},{6,4},{5,7},{7,5},{8,10},{10,8},{9,1... | collective-permute-start | bytes 1179656 | tf_op jit(solution)/shard_map/cond/branch_1_fun/ppermute | solution.py:37
  19.2 5.9 %collective-permute-start.34 = (f32[2,1344]{1,0:T(2,128)S(1)}, f32[2,1344]{1,0:T(2,128)S(1)}, u32[]{:S(2)}, u32[]{:S(2)}) collective-permute-start(f32[2,1344]{1,0:T(2,128)S(1)} %pad_maximum_fusion.5), channel_id=1, source_target_pairs={{0,1},{1,0},{2,3},{3,2},{4,5},{5,4},{6,7},{7,6},{8,9},{9,8},{10,11... | collective-permute-start | bytes 32264 | tf_op jit(solution)/shard_map/cond/branch_1_fun/cond/branch_1_fun/ppermute | solution.py:41
  37.6 17.4 %collective-permute-start.25 = (bf16[384,768]{1,0:T(8,128)(2,1)}, bf16[384,768]{1,0:T(8,128)(2,1)}, u32[]{:S(2)}, u32[]{:S(2)}) collective-permute-start(bf16[384,768]{1,0:T(8,128)(2,1)} %get-tuple-element.650), channel_id=1, source_target_pairs={{0,2},{2,0},{1,3},{3,1},{4,6},{6,4},{5,7},{7,5},{8,10},{10,8},{9,1... | collective-permute-start | bytes 1769480 | tf_op jit(solution)/shard_map/cond/branch_1_fun/ppermute | solution.py:37
  38.0 17.0 %collective-permute-start.23 = (bf16[3,96,768]{2,1,0:T(8,128)(2,1)}, bf16[3,96,768]{2,1,0:T(8,128)(2,1)}, u32[]{:S(2)}, u32[]{:S(2)}) collective-permute-start(bf16[3,96,768]{2,1,0:T(8,128)(2,1)} %get-tuple-element.648), channel_id=1, source_target_pairs={{0,4},{4,0},{8,12},{12,8},{1,5},{5,1},{9,13},{13,9},{2,6},{6,2},{1... | collective-permute-start | bytes 1327112 | tf_op jit(solution)/shard_map/cond/branch_1_fun/ppermute | solution.py:742
  39.7 15.3 %collective-permute-start.24 = (bf16[96,768]{1,0:T(8,128)(2,1)}, bf16[96,768]{1,0:T(8,128)(2,1)}, u32[]{:S(2)}, u32[]{:S(2)}) collective-permute-start(bf16[96,768]{1,0:T(8,128)(2,1)} %get-tuple-element.649), channel_id=1, source_target_pairs={{0,2},{2,0},{1,3},{3,1},{4,6},{6,4},{5,7},{7,5},{8,10},{10,8},{9,1... | collective-permute-start | bytes 442376 | tf_op jit(solution)/shard_map/cond/branch_1_fun/ppermute | solution.py:37
  55.0 18.7 %collective-permute-start.30 = (bf16[384,768]{1,0:T(8,128)(2,1)}, bf16[384,768]{1,0:T(8,128)(2,1)}, u32[]{:S(2)}, u32[]{:S(2)}) collective-permute-start(bf16[384,768]{1,0:T(8,128)(2,1)} %get-tuple-element.676), channel_id=1, source_target_pairs={{0,4},{4,0},{8,12},{12,8},{1,5},{5,1},{9,13},{13,9},{2,6},{6,2},{1... | collective-permute-start | bytes 1769480 | tf_op jit(solution)/shard_map/cond/branch_1_fun/ppermute | solution.py:742
  56.7 17.0 %collective-permute-start.28 = (bf16[384,768]{1,0:T(8,128)(2,1)}, bf16[384,768]{1,0:T(8,128)(2,1)}, u32[]{:S(2)}, u32[]{:S(2)}) collective-permute-start(bf16[384,768]{1,0:T(8,128)(2,1)} %get-tuple-element.674), channel_id=1, source_target_pairs={{0,2},{2,0},{1,3},{3,1},{4,6},{6,4},{5,7},{7,5},{8,10},{10,8},{9,1... | collective-permute-start | bytes 1769480 | tf_op jit(solution)/shard_map/cond/branch_1_fun/ppermute | solution.py:37
  57.0 16.7 %collective-permute-start.29 = (bf16[96,768]{1,0:T(8,128)(2,1)}, bf16[96,768]{1,0:T(8,128)(2,1)}, u32[]{:S(2)}, u32[]{:S(2)}) collective-permute-start(bf16[96,768]{1,0:T(8,128)(2,1)} %get-tuple-element.675), channel_id=1, source_target_pairs={{0,4},{4,0},{8,12},{12,8},{1,5},{5,1},{9,13},{13,9},{2,6},{6,2},{1... | collective-permute-start | bytes 442376 | tf_op jit(solution)/shard_map/cond/branch_1_fun/ppermute | solution.py:742
  77.8 22.1 %collective-permute-start.2 = (bf16[2,768,768]{2,1,0:T(8,128)(2,1)}, bf16[2,768,768]{2,1,0:T(8,128)(2,1)}, u32[]{:S(2)}, u32[]{:S(2)}) collective-permute-start(bf16[2,768,768]{2,1,0:T(8,128)(2,1)} %get-tuple-element.685), channel_id=1, source_target_pairs={{0,1},{1,0},{2,3},{3,2},{4,5},{5,4},{6,7},{7,6},{8,9},{9,8},{10,11... | collective-permute-start | bytes 7077896 | tf_op jit(solution)/shard_map/cond/branch_1_fun/ppermute | solution.py:41
  78.0 22.0 %collective-permute-start.1 = (bf16[384,768]{1,0:T(8,128)(2,1)S(1)}, bf16[384,768]{1,0:T(8,128)(2,1)}, u32[]{:S(2)}, u32[]{:S(2)}) collective-permute-start(bf16[384,768]{1,0:T(8,128)(2,1)S(1)} %get-tuple-element.684), channel_id=1, source_target_pairs={{0,1},{1,0},{2,3},{3,2},{4,5},{5,4},{6,7},{7,6},{8,9},{9,8},{10,11... | collective-permute-start | bytes 1769480 | tf_op jit(solution)/shard_map/cond/branch_1_fun/ppermute | solution.py:41
  78.3 21.6 %collective-permute-start = (bf16[384,768]{1,0:T(8,128)(2,1)}, bf16[384,768]{1,0:T(8,128)(2,1)}, u32[]{:S(2)}, u32[]{:S(2)}) collective-permute-start(bf16[384,768]{1,0:T(8,128)(2,1)} %get-tuple-element.683), channel_id=1, source_target_pairs={{0,4},{4,0},{8,12},{12,8},{1,5},{5,1},{9,13},{13,9},{2,6},{6,2},{1... | collective-permute-start | bytes 1769480 | tf_op jit(solution)/shard_map/cond/branch_1_fun/ppermute | solution.py:742
  105.0 4.7 collective-permute-start.3
  120.1 14.1 %collective-permute-start.4 = (bf16[256,768]{1,0:T(8,128)(2,1)S(1)}, bf16[256,768]{1,0:T(8,128)(2,1)}, u32[]{:S(2)}, u32[]{:S(2)}) collective-permute-start(bf16[256,768]{1,0:T(8,128)(2,1)S(1)} %get-tuple-element.692), channel_id=1, source_target_pairs={{0,16},{1,17},{2,18},{3,19},{4,20},{5,21},{6,22},{7,23},{8,24},{9,... | collective-permute-start | bytes 1179656 | tf_op jit(solution)/shard_map/cond/branch_1_fun/ppermute | solution.py:835
  134.2 10.2 %collective-permute-start.5 = (bf16[256,768]{1,0:T(8,128)(2,1)S(1)}, bf16[256,768]{1,0:T(8,128)(2,1)}, u32[]{:S(2)}, u32[]{:S(2)}) collective-permute-start(bf16[256,768]{1,0:T(8,128)(2,1)S(1)} %param.21), channel_id=1, source_target_pairs={{0,16},{1,17},{2,18},{3,19},{4,20},{5,21},{6,22},{7,23},{8,24},{9,... | collective-permute-start | bytes 1179656 | tf_op jit(solution)/shard_map/cond/branch_1_fun/ppermute | solution.py:835
  157.2 22.0 %collective-permute-start.33 = (bf16[512,768]{1,0:T(8,128)(2,1)}, bf16[512,768]{1,0:T(8,128)(2,1)}, u32[]{:S(2)}, u32[]{:S(2)}) collective-permute-start(bf16[512,768]{1,0:T(8,128)(2,1)} %get-tuple-element.714), channel_id=1, source_target_pairs={{0,1},{1,0},{2,3},{3,2},{4,5},{5,4},{6,7},{7,6},{8,9},{9,8},{10,11... | collective-permute-start | bytes 2359304 | tf_op jit(solution)/shard_map/cond/branch_1_fun/ppermute | solution.py:41
  157.4 21.9 %collective-permute-start.32 = (bf16[256,768]{1,0:T(8,128)(2,1)S(1)}, bf16[256,768]{1,0:T(8,128)(2,1)}, u32[]{:S(2)}, u32[]{:S(2)}) collective-permute-start(bf16[256,768]{1,0:T(8,128)(2,1)S(1)} %dynamic-slice_bitcast_fusion.1), channel_id=1, source_target_pairs={{0,2},{2,0},{1,3},{3,1},{4,6},{6,4},{5,7},{7,5},{8,10},{10,8},{9,1... | collective-permute-start | bytes 1179656 | tf_op jit(solution)/shard_map/cond/branch_1_fun/ppermute | solution.py:37
  200.8 14.1 %collective-permute-start.7 = (bf16[512,1536]{1,0:T(8,128)(2,1)S(1)}, bf16[512,1536]{1,0:T(8,128)(2,1)}, u32[]{:S(2)}, u32[]{:S(2)}) collective-permute-start(bf16[512,1536]{1,0:T(8,128)(2,1)S(1)} %slice.148), channel_id=1, source_target_pairs={{0,1},{1,0},{2,3},{3,2},{4,5},{5,4},{6,7},{7,6},{8,9},{9,8},{10,11... | collective-permute-start | bytes 4718600 | tf_op jit(solution)/shard_map/cond/branch_1_fun/ppermute | solution.py:41
  201.0 13.9 %collective-permute-start.6 = (bf16[512,768]{1,0:T(8,128)(2,1)}, bf16[512,768]{1,0:T(8,128)(2,1)}, u32[]{:S(2)}, u32[]{:S(2)}) collective-permute-start(bf16[512,768]{1,0:T(8,128)(2,1)} %get-tuple-element.722), channel_id=1, source_target_pairs={{0,1},{1,0},{2,3},{3,2},{4,5},{5,4},{6,7},{7,6},{8,9},{9,8},{10,11... | collective-permute-start | bytes 2359304 | tf_op jit(solution)/shard_map/cond/branch_1_fun/ppermute | solution.py:41
  201.4 13.5 %collective-permute-start.8 = (bf16[512,384]{1,0:T(8,128)(2,1)S(1)}, bf16[512,384]{1,0:T(8,128)(2,1)}, u32[]{:S(2)}, u32[]{:S(2)}) collective-permute-start(bf16[512,384]{1,0:T(8,128)(2,1)S(1)} %slice.149), channel_id=1, source_target_pairs={{0,1},{1,0},{2,3},{3,2},{4,5},{5,4},{6,7},{7,6},{8,9},{9,8},{10,11... | collective-permute-start | bytes 1179656 | tf_op jit(solution)/shard_map/cond/branch_1_fun/ppermute | solution.py:41
  254.6 22.1 %collective-permute-start.11 = (bf16[512,768]{1,0:T(8,128)(2,1)S(1)}, bf16[512,768]{1,0:T(8,128)(2,1)}, u32[]{:S(2)}, u32[]{:S(2)}) collective-permute-start(bf16[512,768]{1,0:T(8,128)(2,1)S(1)} %get-tuple-element.746), channel_id=1, source_target_pairs={{16,0},{17,1},{18,2},{19,3},{20,4},{21,5},{22,6},{23,7},{24,8},{25... | collective-permute-start | bytes 2359304 | tf_op jit(solution)/shard_map/cond/branch_1_fun/ppermute | solution.py:838
  287.9 28.2 %collective-permute-start.13 = (bf16[768,768]{1,0:T(8,128)(2,1)S(1)}, bf16[768,768]{1,0:T(8,128)(2,1)}, u32[]{:S(2)}, u32[]{:S(2)}) collective-permute-start(bf16[768,768]{1,0:T(8,128)(2,1)S(1)} %get-tuple-element.789), channel_id=1, source_target_pairs={{0,2},{2,0},{1,3},{3,1},{4,6},{6,4},{5,7},{7,5},{8,10},{10,8},{9,1... | collective-permute-start | bytes 3538952 | tf_op jit(solution)/shard_map/cond/branch_1_fun/ppermute | solution.py:37
  322.0 61.7 %all-reduce.7.cloned.1.call-start = ((), (), s32[]{:S(2)}) async-start(), calls=%async_computation | async-start | bytes 2359296 | tf_op jit(solution)/shard_map/cond/branch_1_fun/psum | solution.py:982
  325.7 4.7 collective-permute-start.14
  338.2 39.0 %collective-permute-start.16 = (bf16[768,768]{1,0:T(8,128)(2,1)}, bf16[768,768]{1,0:T(8,128)(2,1)}, u32[]{:S(2)}, u32[]{:S(2)}) collective-permute-start(bf16[768,768]{1,0:T(8,128)(2,1)} %get-tuple-element.838), channel_id=1, source_target_pairs={{0,2},{2,0},{1,3},{3,1},{4,6},{6,4},{5,7},{7,5},{8,10},{10,8},{9,1... | collective-permute-start | bytes 3538952 | tf_op jit(solution)/shard_map/cond/branch_1_fun/cond/branch_1_fun/cond/branch_1_fun/ppermute | solution.py:37
  338.6 38.6 %collective-permute-start.17 = (bf16[192,768]{1,0:T(8,128)(2,1)S(1)}, bf16[192,768]{1,0:T(8,128)(2,1)S(1)}, u32[]{:S(2)}, u32[]{:S(2)}) collective-permute-start(bf16[192,768]{1,0:T(8,128)(2,1)S(1)} %get-tuple-element.839), channel_id=1, source_target_pairs={{0,2},{2,0},{1,3},{3,1},{4,6},{6,4},{5,7},{7,5},{8,10},{10,8},{9,1... | collective-permute-start | bytes 884744 | tf_op jit(solution)/shard_map/cond/branch_1_fun/cond/branch_1_fun/cond/branch_1_fun/ppermute | solution.py:37
  386.6 67.9 %all-reduce.9.cloned.1.call-start = ((), (), s32[]{:S(2)}) async-start(), calls=%async_computation.1 | async-start | bytes 2949120 | tf_op jit(solution)/shard_map/cond/branch_1_fun/psum | solution.py:984
  406.2 21.8 %collective-permute-start.21 = (bf16[576,768]{1,0:T(8,128)(2,1)S(1)}, bf16[576,768]{1,0:T(8,128)(2,1)S(1)}, u32[]{:S(2)}, u32[]{:S(2)}) collective-permute-start(bf16[576,768]{1,0:T(8,128)(2,1)S(1)} %param.53), channel_id=1, source_target_pairs={{0,2},{2,0},{1,3},{3,1},{4,6},{6,4},{5,7},{7,5},{8,10},{10,8},{9,1... | collective-permute-start | bytes 2654216 | tf_op jit(solution)/shard_map/cond/branch_1_fun/cond/branch_1_fun/cond/branch_1_fun/ppermute | solution.py:37
  461.0 48.6 %all-reduce.11.cloned.1.call-start = ((), (), s32[]{:S(2)}) async-start(), calls=%async_computation.2 | async-start | bytes 1769472 | tf_op jit(solution)/shard_map/cond/branch_1_fun/psum | solution.py:987
  485.2 4.6 collective-permute-start.40
  487.9 12.6 %collective-permute-start.41 = (bf16[256,768]{1,0:T(8,128)(2,1)S(1)}, bf16[256,768]{1,0:T(8,128)(2,1)S(1)}, u32[]{:S(2)}, u32[]{:S(2)}) collective-permute-start(bf16[256,768]{1,0:T(8,128)(2,1)S(1)} %dynamic-slice_bitcast_fusion.4), channel_id=1, source_target_pairs={{0,2},{2,0},{1,3},{3,1},{4,6},{6,4},{5,7},{7,5},{8,10},{10,8},{9,1... | collective-permute-start | bytes 1179656 | tf_op jit(solution)/shard_map/cond/branch_1_fun/cond/branch_1_fun/ppermute | solution.py:37
  (43 other events, 313.9 us)
Sparse Core Ops, SparseCore 0:
  325.8 54.2 all-reduce.6
  389.8 64.5 all-reduce.8
  464.3 45.1 all-reduce.10

commit v2 on v1

--- a/solution.py
+++ b/solution.py
@@ -22,6 +22,7 @@
 TILE_BASE = (0, 128, 512, 640)
 STRIP = 1664
 SPAN = STRIP + 128
+PIECE = 32
 MIB = 2**20
 
 
@@ -84,52 +85,71 @@
     return (lane < HEAD) if which == 0 else (lane >= HEAD)
 
 
-def cross_mask(qlen, core, tile, kb):
-    key_low = KEY_BASE[kb] == 0
+def cross_mask(info_ref, tile, first):
+    key_low = first < 256
     row_low = tile < 2
     if not key_low and not row_low:
         return None
-    shape = (256, 128)
+    qlen, core = info_ref[0], info_ref[1]
+    shape = (PIECE, 128)
     if row_low:
-        first = 256 * core + 128 * tile
-        row_side = first + lax.broadcasted_iota(jnp.int32, shape, 1) < qlen
+        row = 256 * core + 128 * tile + lax.broadcasted_iota(jnp.int32, shape, 1)
+        row_side = row < qlen
     if key_low:
-        key_side = lax.broadcasted_iota(jnp.int32, shape, 0) < qlen
+        key_side = first + lax.broadcasted_iota(jnp.int32, shape, 0) < qlen
     if row_low and key_low:
         return row_side != key_side
     return row_side if row_low else key_side
 
 
-def strip_rows(tile, kb):
-    first = KEY_BASE[kb] - TILE_BASE[tile] + 640
-    return slice(first, first + 256)
-
-
-def score_block(info_ref, keys, query, strip_ref, h, ib, kb):
-    qlen, core, plen = info_ref[0], info_ref[1], info_ref[2]
-    raw = dotf(keys, query, NT)
+def pieces(kb):
+    for at in range(0, 256, PIECE):
+        yield KEY_BASE[kb] + at, slice(256 * kb + at, 256 * kb + at + PIECE), slice(at, at + PIECE)
+
+
+def strip_rows(tile, first):
+    start = first - TILE_BASE[tile] + 640
+    return slice(start, start + PIECE)
+
+
+def piece_scores(info_ref, raw, strip_ref, h, ib, first):
     parts = []
     for u in (0, 1):
         tile = 2 * ib + u
-        rows = strip_rows(tile, kb)
+        rows = strip_rows(tile, first)
         bias = strip_ref[h, 0, rows, :]
-        cross = cross_mask(qlen, core, tile, kb)
+        cross = cross_mask(info_ref, tile, first)
         if cross is not None:
             bias = jnp.where(cross, strip_ref[h, 1, rows, :], bias)
         parts.append(raw[:, 128 * u : 128 * u + 128] + bias)
     scores = jnp.concatenate(parts, 1)
-    if kb != 0:
-        live = KEY_BASE[kb] + lax.broadcasted_iota(jnp.int32, (256, 256), 0) < plen
+    if first >= 256:
+        live = first + lax.broadcasted_iota(jnp.int32, (PIECE, 256), 0) < info_ref[2]
         scores = jnp.where(live, scores, NEG)
     return scores
 
 
+def by_eight(value):
+    return value.reshape(PIECE // 8, 8, 256)
+
+
 def whole(core, own, other):
     return jnp.concatenate([jnp.where(core == 0, own, other), jnp.where(core == 0, other, own)], 0)
 
 
 def forward_kernel(
-    info_ref, q_ref, k_ref, v_ref, ko_ref, vo_ref, win_ref, o_ref, lse_ref, strip_ref
+    info_ref,
+    q_ref,
+    k_ref,
+    v_ref,
+    ko_ref,
+    vo_ref,
+    win_ref,
+    o_ref,
+    lse_ref,
+    strip_ref,
+    score_ref,
+    prob_ref,
 ):
     core = info_ref[1]
     for h in range(2):
@@ -145,20 +165,19 @@
         outs = []
         for h in range(2):
             one = jnp.where(lane_mask(256, h), query, jnp.zeros_like(query))
-            blocks = [
-                score_block(
-                    info_ref, keys[256 * kb : 256 * kb + 256], one, strip_ref, h, ib, kb
-                )
-                for kb in range(4)
-            ]
-            top = functools.reduce(
-                jnp.maximum, [jnp.max(s, 0, keepdims=True) for s in blocks]
-            )
-            mixed = None
+            top = None
             for kb in range(4):
-                probs = jnp.exp(blocks[kb] - top).astype(bf16)
-                part = dotf(turned[h][:, 256 * kb : 256 * kb + 256], probs)
-                mixed = part if mixed is None else mixed + part
+                raw = dotf(keys[256 * kb : 256 * kb + 256], one, NT)
+                for first, at, within in pieces(kb):
+                    scores = piece_scores(info_ref, raw[within], strip_ref, h, ib, first)
+                    score_ref[h, at, :] = scores
+                    most = jnp.max(by_eight(scores), 0)
+                    top = most if top is None else jnp.maximum(top, most)
+            top = jnp.max(top, 0, keepdims=True)
+            for kb in range(4):
+                for _, at, _ in pieces(kb):
+                    prob_ref[h, at, :] = jnp.exp(score_ref[h, at, :] - top).astype(bf16)
+            mixed = dotf(turned[h], prob_ref[h])
             total = mixed[HEAD * (1 - h) : HEAD * (1 - h) + 1, :]
             lse_ref[0, h : h + 1, rows] = top + jnp.log(total)
             outs.append(mixed[HEAD * h : HEAD * h + HEAD, :] / total)
@@ -189,7 +208,11 @@
                 pl.BlockSpec((1, 2, 2, SPAN), lambda i, s: (i, 0, 0, 0)),
             ],
             out_specs=[block, pl.BlockSpec((1, 2, 512), lambda i, s: (i, 0, 0))],
-            scratch_shapes=[pltpu.VMEM((2, 2, STRIP, 128), f32)],
+            scratch_shapes=[
+                pltpu.VMEM((2, 2, STRIP, 128), f32),
+                pltpu.VMEM((2, 1024, 256), f32),
+                pltpu.VMEM((2, 1024, 256), bf16),
+            ],
         ),
         out_shape=[
             jax.ShapeDtypeStruct((512, 128 * groups), bf16),
@@ -204,19 +227,18 @@
 def backward_kernel(with_table, *refs):
     info_ref, q_ref, k_ref, v_ref, ko_ref, vo_ref, do_ref, lse_ref, win_ref = refs[:9]
     dq_ref, dk_ref, dv_ref, dko_ref, dvo_ref, *rest = refs[9:]
-    qlen, core = info_ref[0], info_ref[1]
-    strip_ref = rest[-1]
+    core = info_ref[1]
+    *rest, strip_ref, wide_ref, term_ref, prob_ref, grad_ref = rest
     for h in range(2):
         for kind in range(2):
             make_strip(win_ref, h, kind, strip_ref)
     if with_table:
-        held_ref, strip_grad_ref = rest[:2]
+        held_ref, strip_grad_ref = rest
         strip_grad_ref[...] = jnp.zeros_like(strip_grad_ref)
     keys = whole(core, k_ref[...], ko_ref[...])
     values = whole(core, v_ref[...], vo_ref[...])
     keys_turned = keys.T
-    key_grads = [jnp.zeros((256, 128), f32) for _ in range(4)]
-    value_grads = [jnp.zeros((256, 128), f32) for _ in range(4)]
+    key_grad = value_grad = 0.0
     for ib in range(2):
         rows = slice(256 * ib, 256 * ib + 256)
         query = q_ref[rows, :] * jnp.asarray(0.125, bf16)
@@ -227,41 +249,43 @@
             one = jnp.where(mask, query, jnp.zeros_like(query))
             grad_one = jnp.where(mask, grad, jnp.zeros_like(grad))
             log_total = lse_ref[0, h : h + 1, rows]
-            probs, terms = [], []
             row_term = 0.0
             for kb in range(4):
                 kr = slice(256 * kb, 256 * kb + 256)
-                scores = score_block(info_ref, keys[kr], one, strip_ref, h, ib, kb)
-                part = jnp.exp(scores - log_total)
-                term = part * dotf(values[kr], grad_one, NT)
-                row_term = row_term + jnp.sum(term, 0, keepdims=True)
-                value_grads[kb] = value_grads[kb] + dotf(part.astype(bf16), grad_one)
-                probs.append(part)
-                terms.append(term)
-            flat = None
+                raw = dotf(keys[kr], one, NT)
+                grad_probs = dotf(values[kr], grad_one, NT)
+                for first, at, within in pieces(kb):
+                    scores = piece_scores(info_ref, raw[within], strip_ref, h, ib, first)
+                    probs = jnp.exp(scores - log_total)
+                    term = probs * grad_probs[within]
+                    wide_ref[h, at, :] = probs
+                    term_ref[h, at, :] = term
+                    prob_ref[h, at, :] = probs.astype(bf16)
+                    row_term = row_term + jnp.sum(by_eight(term), 0)
+            row_term = jnp.sum(row_term, 0, keepdims=True)
             for kb in range(4):
-                kr = slice(256 * kb, 256 * kb + 256)
-                grad_scores = (terms[kb] - probs[kb] * row_term).astype(bf16)
-                key_grads[kb] = key_grads[kb] + dotf(grad_scores, one)
-                part = dotf(keys_turned[:, kr], grad_scores)
-                flat = part if flat is None else flat + part
-                if with_table:
-                    for u in (0, 1):
-                        tile = 2 * ib + u
-                        where = strip_rows(tile, kb)
-                        part = grad_scores[:, 128 * u : 128 * u + 128].astype(f32)
-                        strip_grad_ref[h, 0, where, :] += part
-                        cross = cross_mask(qlen, core, tile, kb)
-                        if cross is not None:
-                            strip_grad_ref[h, 1, where, :] += jnp.where(cross, part, 0.0)
+                for first, at, _ in pieces(kb):
+                    low = (term_ref[h, at, :] - wide_ref[h, at, :] * row_term).astype(bf16)
+                    grad_ref[h, at, :] = low
+                    if with_table:
+                        for u in (0, 1):
+                            tile = 2 * ib + u
+                            where = strip_rows(tile, first)
+                            part = low[:, 128 * u : 128 * u + 128].astype(f32)
+                            strip_grad_ref[h, 0, where, :] += part
+                            cross = cross_mask(info_ref, tile, first)
+                            if cross is not None:
+                                strip_grad_ref[h, 1, where, :] += jnp.where(cross, part, 0.0)
+            value_grad = value_grad + dotf(prob_ref[h], grad_one)
+            key_grad = key_grad + dotf(grad_ref[h], one)
+            flat = dotf(keys_turned, grad_ref[h])
             query_grads.append(flat[HEAD * h : HEAD * h + HEAD, :])
         dq_ref[rows, :] = (jnp.concatenate(query_grads, 0).T * 0.125).astype(bf16)
     for grads, own_ref, other_ref in (
-        (key_grads, dk_ref, dko_ref),
-        (value_grads, dv_ref, dvo_ref),
+        (key_grad, dk_ref, dko_ref),
+        (value_grad, dv_ref, dvo_ref),
     ):
-        first = jnp.concatenate(grads[:2], 0)
-        second = jnp.concatenate(grads[2:], 0)
+        first, second = grads[:512], grads[512:]
         own_ref[...] = jnp.where(core == 0, first, second)
         other_ref[...] = jnp.where(core == 0, second, first).astype(bf16)
     if with_table:
@@ -281,6 +305,7 @@
         out_specs.append(pl.BlockSpec((1, 2, 2, 8, SPAN), lambda i, s: (i, 0, 0, 0, 0)))
         out_shape.append(jax.ShapeDtypeStruct((count, 2, 2, 8, SPAN), f32))
         scratch = scratch * 2
+    scratch += [pltpu.VMEM((2, 1024, 256), f32)] * 2 + [pltpu.VMEM((2, 1024, 256), bf16)] * 2
     return pl.pallas_call(
         functools.partial(backward_kernel, with_table),
         grid_spec=pltpu.PrefetchScalarGridSpec(
@@ -614,7 +639,7 @@
 def split_grad_kernel(l_ref, lo_ref, r_ref, ro_ref, kept_ref, sent_ref):
     total = dotf(l_ref[...], r_ref[...], TN) + dotf(lo_ref[...], ro_ref[...], TN)
     half = total.shape[0] // 2
-    kept_ref[...] = total[:half]
+    kept_ref[...] = total[:half].astype(bf16)
     sent_ref[...] = total[half:].astype(bf16)
 
 
@@ -630,7 +655,7 @@
         grid=(count,),
         in_specs=[left_block, left_block, right_block, right_block],
         out_specs=[made, made],
-        out_shape=[jax.ShapeDtypeStruct(shape, f32), jax.ShapeDtypeStruct(shape, bf16)],
+        out_shape=[jax.ShapeDtypeStruct(shape, bf16)] * 2,
         compiler_params=pltpu.CompilerParams(vmem_limit_bytes=20 * MIB),
         cost_estimate=cost(4),
         name="split_grad",
@@ -771,10 +796,13 @@
     out_own, up_own, down_own = out_weight[0], up_weight[0], down_weight[0]
     small = jnp.concatenate([qv_bias[0].reshape(-1), ffn_bias[0], bias_table[0].reshape(-1)])
 
-    def send_small():
-        return swap_y(small), theirs(hidden), own_half(qkv_own, 1)
-
-    small_y, x_sent, qkv_sent = stage(send_small)
+    x_sent, qkv_sent = theirs(hidden), own_half(qkv_own, 1)
+
+    def first_stage():
+        halves = own_half(out_own), own_half(up_own), own_half(down_own)
+        return swap_y(small), swap_y(x_sent), swap_y(qkv_sent), halves
+
+    small_y, x_came, qkv_y, (out_sent, up_sent, down_sent) = stage(first_stage)
 
     def gather_small():
         two = jnp.stack([small, small_y])
@@ -793,20 +821,15 @@
             bias.reshape(6, 1, 2 * cols),
             four[:, 2 * cols : 2 * cols + width].reshape(4, 1, width),
             info,
-            own_half(out_own),
-            own_half(up_own),
-            own_half(down_own),
-        )
-
-    x_came, qkv_y, found = stage(lambda: (swap_y(x_sent), swap_y(qkv_sent), stage(gather_small)))
-    window, onehot, bias, up_bias, info, out_sent, up_sent, down_sent = found
+            in_order(y == 0, mine(hidden), x_came),
+        )
+
+    def second_stage():
+        return swap_z(qkv_y), swap_y(out_sent), swap_y(up_sent), stage(gather_small)
+
+    qkv_z, out_y, up_y, found = stage(second_stage)
+    window, onehot, bias, up_bias, info, x0 = found
     w = dict(up_bias=up_bias, gains=norm_gains[0], shifts=vectors[0])
-
-    def second_stage():
-        x0 = in_order(y == 0, mine(hidden), x_came)
-        return swap_z(qkv_y), swap_y(out_sent), swap_y(up_sent), x0
-
-    qkv_z, out_y, up_y, x0 = stage(second_stage)
 
     def gather_qkv():
         near = jnp.concatenate([qkv_own, in_order(odd == 0, qkv_y, qkv_z, 1)], 1)
@@ -903,12 +926,11 @@
     down_sent = down_grad(bf16, 3)
 
     def through_dense():
-        return dense_back(after, second), down_grad(f32, 0)
+        return dense_back(after, second), down_grad(bf16, 0)
 
     down_came, (grads, down_kept) = stage(lambda: (swap_y(down_sent), stage(through_dense)))
     hidden, branch = grads["hidden"], grads["branch"]
-    low_sum = lambda own, came: (own + came.astype(f32)).astype(bf16)
-    down = low_sum(down_kept, down_came)
+    down = down_kept + down_came
 
     def exchange_dense():
         return swap_c(hidden[:, 2 * width :]), swap_c(branch)
@@ -920,7 +942,7 @@
 
     def through_attention(hidden_far):
         args = normed_low, normed_far, hidden, hidden_far
-        kept = weight_grad(*args, f32, (0, 3, thirds), (0, 1, width))
+        kept = weight_grad(*args, bf16, (0, 3, thirds), (0, 1, width))
         return attention_back(grads, True, 0, 6), kept
 
     def through_input(q_grad, k_grad, v_grad, k_far, v_far):
@@ -941,24 +963,59 @@
                 stage(lambda: through_attention(hidden_far)),
             )
         )
-        return found, low_sum(up_kept, up_came), low_sum(out_kept, out_came)
+        return found, up_kept + up_came, out_kept + out_came
+
+    def over_planes(value, beside):
+        if planes != 4:
+            return lax.psum(value, "dp").astype(f32), stage(beside)
+        rows = value.shape[0] // 2
+        first, second = value[:rows], value[rows:]
+        held, sent = jnp.where(odd == 0, first, second), jnp.where(odd == 0, second, first)
+        came, found = stage(lambda: (swap_z(sent), stage(beside)))
+        held = held + came
+        far_planes = [(0, 2), (2, 0), (1, 3), (3, 1)]
+        held = held + stage(lambda: lax.ppermute(held, "dp", far_planes))
+        return in_order(odd == 0, held, stage(lambda: swap_z(held))).astype(f32), found
 
     def after_up():
-        rest_kept, rest_sent, *found = stage(lambda: through_input(*attention_found))
-        return low_sum(rest_kept, stage(lambda: swap_y(rest_sent))), found
-
-    def through_sums(held, qv_sums, grad_low):
+        rest_kept, rest_sent, grad_input, grad_low, qv_sums = stage(
+            lambda: through_input(*attention_found)
+        )
+        def own_sums():
+            sums = token_sums(held, qv_sums)
+            sums = sums[:2] + swap_c(sums[2:])
+            if planes == 4:
+                sums = sums + swap_z(sums)
+                sums = sums + lax.ppermute(sums, "dp", [(0, 2), (2, 0), (1, 3), (3, 1)])
+            else:
+                sums = lax.psum(sums, "dp")
+            return sums, grad_down.astype(f32)[None]
+
+        rest_came, (sums, down_out) = stage(
+            lambda: (swap_y(rest_sent), stage(own_sums))
+        )
+        rest = rest_kept + rest_came
+        grad_qkv, found = over_planes(
+            rest, lambda: through_sums(sums, grad_input, grad_low)
+        )
+        return down_out, grad_qkv.reshape(1, 3, cols, model), found
+
+    def through_sums(sums, grad_input, grad_low):
         edge_low = edge_blocks(jnp.where(leading, grad_low, result.astype(bf16)))
-        edge_came = swap_y(theirs(edge_low))
-        sums = token_sums(held, qv_sums)
-        sums = sums[:2] + swap_c(sums[2:])
+        edge_own = mine(edge_blocks(jnp.where(leading, grad_input, result)))
+        edge_came = swap_y(theirs(edge_low)).astype(f32)
+        edges = [jnp.where(y == 0, edge_own, edge_came), jnp.where(y == 0, edge_came, edge_own)]
         sums = sums[0] + swap_y(sums[1])
-        if planes == 4:
-            sums = sums + swap_z(sums)
-            sums = sums + lax.ppermute(sums, "dp", [(0, 2), (2, 0), (1, 3), (3, 1)])
-        else:
-            sums = lax.psum(sums, "dp")
-        return sums, edge_came
+        at = heads * 2 * kinds
+        vec_out = sums[at + 2 * cols + width :].reshape(1, 6, share)
+        return (
+            jnp.stack(edges)[None],
+            sums[at : at + 2 * cols].reshape(1, 2, cols),
+            sums[at + 2 * cols : at + 2 * cols + width].reshape(1, width),
+            vec_out[:, :2],
+            vec_out[:, 2:],
+            sums[:at].reshape(1, heads, 2 * kinds),
+        )
 
     share = model // 4
 
@@ -981,33 +1038,21 @@
 
     grad_down, (found, *later) = stage(lambda: (lax.psum(down, "dp"), stage(after_down)))
     *attention_found, held = found
-    summed, (rest, found) = stage(lambda: (lax.psum(later, "dp"), stage(after_up)))
-    grad_input, grad_low, qv_sums = found
-    grad_qkv, (sums, edge_came) = stage(
-        lambda: (lax.psum(rest, "dp"), stage(lambda: through_sums(held, qv_sums, grad_low)))
+    (up_out, out_out), (down_out, qkv_out, found) = stage(
+        lambda: (lax.psum(later, "dp"), stage(after_up))
     )
-    grad_down, grad_qkv = grad_down.astype(f32), grad_qkv.astype(f32)
-    grad_up, grad_out = [value.astype(f32) for value in summed]
-    edge_own = mine(edge_blocks(jnp.where(leading, grad_input, result)))
-    edge_came = edge_came.astype(f32)
-    edges = jnp.stack([jnp.where(y == 0, edge_own, edge_came), jnp.where(y == 0, edge_came, edge_own)])
-    grad_qkv = grad_qkv.reshape(1, 3, cols, model).transpose(0, 3, 1, 2)
-    at = heads * 2 * kinds
-    table_out = sums[:at].reshape(heads, 2 * kinds)
-    qv_out = sums[at : at + 2 * cols].reshape(2, cols)
-    ffn_out = sums[at + 2 * cols : at + 2 * cols + width]
-    vec_out = sums[at + 2 * cols + width :].reshape(6, share)
+    edges, qv_out, ffn_out, gain_out, vec_out, table_out = found
     return (
-        edges[None],
-        grad_qkv,
-        qv_out[None],
-        grad_out[None],
-        grad_up[None],
-        ffn_out[None],
-        grad_down[None],
-        vec_out[:2][None],
-        vec_out[2:][None],
-        table_out[None],
+        edges,
+        qkv_out.transpose(0, 3, 1, 2),
+        qv_out,
+        out_out.astype(f32)[None],
+        up_out.astype(f32)[None],
+        ffn_out,
+        down_out,
+        gain_out,
+        vec_out,
+        table_out,
     )
 
 

time: 532 us -> 511 us (0.961)
  Pallas kernels: 220 us -> 212 us
  waiting for transfers between devices: 146 us -> 139 us
  local copies, waits for them, and re-layouts: 36.1 us -> 29.7 us
    ppermute x5 -> x7, waiting for transfers between devices: 0.75 us -> 25.7 us  [swap_z(): return lax.ppermute(value, 'dp', [(i, i ^ 1) for i in range(planes)])]
    ppermute x13, waiting for transfers between devices: 53.2 us -> 29.5 us  [swap_y(): return lax.ppermute(value, 'tensor', SWAP_Y)]
    psum x1, waiting for transfers between devices: 22.4 us -> 0.01 us  [body(): lax.psum(later, 'dp')]
    ppermute x1 -> x2, waiting for transfers between devices: 0.41 us -> 21.7 us  [the longest x1 21.6 us: over_planes(): held = held + stage(lambda: lax.ppermute(held, 'dp', far_planes))]
    convert_element_type x9 -> x1, other arithmetic: 15.5 us -> 1.35 us  [over_planes(): in_order(odd == 0, held, stage(lambda: swap_z(held))).astype(f32)]
    add x3 -> x9, other arithmetic: 0.62 us -> 12 us  [the longest x2 4.76 us: after_down(): return (found, up_kept + up_came, out_kept + out_came)]
    psum x1 -> x0, waiting for transfers between devices: 8.09 us -> none  [body(): lax.psum(rest, 'dp')]
  transfers between devices with their start and end apart: 45 -> 47, of which waited for: 24 -> 25; matrix products, arithmetic and copies ran while one was open for 12% -> 12% of each run, Pallas kernels for 27% -> 27%
where the time goes in v2:
time: 511 us; the launch traced here: 501 us
  Pallas kernels  212 us (41%)
  waiting for transfers between devices  139 us (27%)
  other arithmetic  60.9 us (12%)
  starting transfers between devices  39.8 us (8%)
  local copies, waits for them, and re-layouts  29.7 us (6%)
  between operations  15.4 us (3%)
    pallas_call x2, Pallas kernels, attend_backward(): pl.pallas_call(functools.partial(backward_kernel, with_table), grid_spec=...  56.2 us
    pallas_call x2, Pallas kernels, attend_forward(): pl.pallas_call(forward_kernel, grid_spec=pltpu.PrefetchScalarGridSpec(num...  36.2 us
    pallas_call x3, Pallas kernels, ffn_forward(): pl.pallas_call(functools.partial(ffn_forward_kernel, keep), grid=(4,), in...  36.2 us
    ppermute x20, waiting for transfers between devices, swap_c(): return lax.ppermute(value, 'tensor', SWAP_C)  32.3 us
    ppermute x13, waiting for transfers between devices, swap_y(): return lax.ppermute(value, 'tensor', SWAP_Y)  29.5 us
    pallas_call x2, Pallas kernels, ffn_backward(): pl.pallas_call(functools.partial(ffn_backward_kernel, len(deps)), grid=(4...  27.5 us
    ppermute x7, waiting for transfers between devices, swap_z(): return lax.ppermute(value, 'dp', [(i, i ^ 1) for i in range(planes)])  25.7 us
    ppermute x1, waiting for transfers between devices, over_planes(): held = held + stage(lambda: lax.ppermute(held, 'dp', far_planes))  21.6 us
  transfers between devices with their start and end apart: 47, of which 25 were waited for; matrix products, arithmetic and copies ran while one was open for 12% of the time, Pallas kernels for 27%

profile of v2, /device:TPU:0, one launch (start us, length us, event | category | flops | bytes accessed | tf_op | source)
XLA Modules:
  0.0 501.0 jit_solution(4449214783868762801)
XLA Ops:
  11.2 21.9 %conditional.32 = (f32[1344]{0:T(1024)}, bf16[256,768]{1,0:T(8,128)(2,1)}, bf16[3,96,768]{2,1,0:T(8,128)(2,1)}, bf16[96,768]{1,0:T(8,128)(2,1)S(1)}, bf16[384,76...) conditional(s32[]{:T(128)} %bitcast.34, () %tuple.266, (f32[1344]{0:T(1024)S(1)}, bf16[2,256,768]{2,1,0:T(8,128)(2,1)}, ...), branch_computations={%region_0.1_spmd, %region_1.2_spmd} | conditional | flops 8 | bytes 7984428 | solution.py:789
  18.8 14.4 %collective-permute-done.23 = f32[1344]{0:T(1024)} collective-permute-done((f32[1344]{0:T(1024)S(1)}, f32[1344]{0:T(1024)}, u32[]{:S(2)}, u32[]{:S(2)}) %collective-permute-start.23) | collective-permute-done | bytes 5408 | tf_op jit(solution)/shard_map/cond/branch_1_fun/ppermute | solution.py:38
  33.2 17.9 %conditional.33 = (bf16[3,96,768]{2,1,0:T(8,128)(2,1)}, bf16[96,768]{1,0:T(8,128)(2,1)}, bf16[384,768]{1,0:T(8,128)(2,1)}, f32[6,2,2,1792]{3,0,2,1:T(8,128)}, f3...) conditional(s32[]{:T(128)} %bitcast.34, () %tuple.268, ...), branch_computations={%region_2.3_spmd, %region_3.6_spmd} | conditional | flops 18671254 | bytes 8554106 | solution.py:789
  52.1 20.0 %conditional.34 = (bf16[3,384,768]{2,1,0:T(8,128)(2,1)}, bf16[3,384,768]{2,1,0:T(8,128)(2,1)}, bf16[512,768]{1,0:T(8,128)(2,1)}, bf16[512,1536]{1,0:T(8,128)(2,1...) conditional(s32[]{:T(128)} %bitcast.34, () %tuple.265, ...), branch_computations={%region_6.7_spmd, %region_7.10_spmd} | conditional | flops 5750787 | bytes 37604984 | solution.py:789
  55.7 16.4 %conditional.1 = (bf16[3,384,768]{2,1,0:T(8,128)(2,1)}, bf16[3,384,768]{2,1,0:T(8,128)(2,1)}, bf16[512,768]{1,0:T(8,128)(2,1)}, bf16[512,1536]{1,0:T(8,128)(2,1)}, bf16[512,1536]{1,0:T(8,128)(2,1)}) conditional(s32[]{:T(128)} %bitcast.9, () %tuple.158, (s32[]{:T(128)}, bf16[3,96,768]{2,1,0:T(8,128)(2,1)}, bf16[3,96,768]{2,1,0:T(8,128)(2,1)}, ...), branch_computations={%region_8.8_spmd, %region_9.9_spmd} | conditional | flops 5750785 | bytes 32296322 | solution.py:789
  77.4 21.3 %conditional.35 = (bf16[384,768]{1,0:T(8,128)(2,1)}, bf16[384,768]{1,0:T(8,128)(2,1)}, bf16[2,768,768]{2,1,0:T(8,128)(2,1)}, bf16[512,768]{1,0:T(8,128)(2,1)}) conditional(s32[]{:T(128)} %bitcast.34, () %tuple.264, (bf16[384,768]{1,0:T(8,128)(2,1)}, bf16[384,768]{1,0:T(8,128)(2,1)S(1)}, bf16[2,768,768]{2,1,0:T(8,128)(2,1)}, s32[2]{0:T(128)S(1)}, ...), branch_computations={%region_10.11_spmd, %region_11.14_spmd} | conditional | flops 2 | bytes 72300056 | solution.py:789
  79.5 19.2 %conditional.2 = (bf16[512,768]{1,0:T(8,128)(2,1)}) conditional(s32[]{:T(128)} %bitcast.10, () %tuple.162, (s32[3]{0:T(128)}, bf16[512,768]{1,0:T(8,128)(2,1)}, bf16[512,1536]{1,0:T(8,128)(2,1)}, bf16[512,1536]{1,0:T(8,128)(2,1)}, f32[6,2,2,1792]{3,0,2,1:T(8,128)}) %tuple.163), branch_computations={%region_12.12_spmd, %region_13.13_spmd} | conditional | bytes 58144072 | solution.py:789
  80.6 18.1 %attend_forward.2 = (bf16[512,768]{1,0:T(8,128)(2,1)}, f32[6,2,512]{2,1,0:T(2,128)}) custom-call(s32[3]{0:T(128)} %get-tuple-element.704.info_ref, bf16[512,768]{1,0:T(8,128)(2,1)} %get-tuple-element.705.q_ref, bf16[512,1536]{1,0:T(8,128)(2,1)} %get-tuple-element.706.k_ref.v_ref, bf16[512,1536]{1,0:T(8,128)(2,1)} %get-tuple-element.706.k_ref.v_ref, ...), custom_call_target="tpu_custom_call" | custom-call | bytes 57800000 | tf_op jit(solution)/shard_map/cond/branch_1_fun/cond/branch_1_fun/attend_forward/pallas_call | solution.py:200
  156.3 20.1 %conditional.40 = (bf16[256,768]{1,0:T(8,128)(2,1)}, bf16[512,768]{1,0:T(8,128)(2,1)}, bf16[512,768]{1,0:T(8,128)(2,1)}, f32[6,2,512]{2,1,0:T(2,128)S(1)}) conditional(s32[]{:T(128)} %bitcast.34, () %tuple.261, (bf16[2,256,768]{2,1,0:T(8,128)(2,1)S(1)}, s32[]{:T(128)}, bf16[512,768]{1,0:T(8,128)(2,1)}, s32[3]{0:T(128)}, ...), branch_computations={%region_22.23_spmd, %region_23.24_spmd} | conditional | bytes 63649204 | solution.py:789
  158.1 18.1 %attend_forward.3 = (bf16[512,768]{1,0:T(8,128)(2,1)}, f32[6,2,512]{2,1,0:T(2,128)S(1)}) custom-call(s32[3]{0:T(128)} %get-tuple-element.742.info_ref, bf16[512,768]{1,0:T(8,128)(2,1)} %get-tuple-element.743.q_ref, bf16[512,1536]{1,0:T(8,128)(2,1)} %get-tuple-element.744.k_ref.v_ref, bf16[512,1536]{1,0:T(8,128)(2,1)} %get-tuple-element.744.k_ref.v_ref, ...), custom_call_target="tpu_custom_call" | custom-call | bytes 57800000 | tf_op jit(solution)/shard_map/cond/branch_1_fun/attend_forward/pallas_call | solution.py:200
  178.6 17.1 %ffn_forward.5 = (f32[512,768]{1,0:T(8,128)}, bf16[512,768]{1,0:T(8,128)(2,1)}, bf16[512,3072]{1,0:T(8,128)(2,1)S(1)}, bf16[512,3072]{1,0:T(8,128)(2,1)}, f32[51...) custom-call(bf16[512,768]{1,0:T(8,128)(2,1)S(1)} %copy-done.7, ...), custom_call_target="tpu_custom_call" | custom-call | bytes 51000000 | tf_op jit(solution)/shard_map/ffn_forward/pallas_call | solution.py:451
  197.4 14.2 %conditional.41 = (bf16[512,768]{1,0:T(8,128)(2,1)}, bf16[512,1536]{1,0:T(8,128)(2,1)}, bf16[512,384]{1,0:T(8,128)(2,1)}, bf16[512,768]{1,0:T(8,128)(2,1)S(1)}, f32[512,768]{1,0:T(8,128)S(1)}) conditional(s32[]{:T(128)} %bitcast.34, () %tuple.277, (bf16[512,768]{1,0:T(8,128)(2,1)}, bf16[512,3072]{1,0:T(8,128)(2,1)S(1)}, ...), branch_computations={%region_24.25_spmd, %region_25.26_spmd} | conditional | bytes 65942368 | solution.py:789
  211.7 26.6 %attend_backward.3 = (bf16[512,768]{1,0:T(8,128)(2,1)}, f32[512,768]{1,0:T(8,128)}, f32[512,768]{1,0:T(8,128)}, bf16[512,768]{1,0:T(8,128)(2,1)}, bf16[512,768]{1,0:T(8,128)(2,1)}) custom-call(s32[3]{0:T(128)} %get-tuple-element.1158.refs_0_, bf16[512,768]{1,0:T(8,128)(2,1)} %get-tuple-element.1173.refs_1_, ...), custom_call_target="tpu_custom_call" | custom-call | bytes 102000000 | tf_op jit(solution)/shard_map/attend_backward/pallas_call | solution.py:309
  238.3 32.6 %conditional.42 = (bf16[512,768]{1,0:T(8,128)(2,1)}) conditional(s32[]{:T(128)} %bitcast.34, () %tuple.279, (bf16[512,768]{1,0:T(8,128)(2,1)}, bf16[512,768]{1,0:T(8,128)(2,1)}, bf16[512,768]{1,0:T(8,128)(2,1)}, f32[512,768]{1,0:T(8,128)}, f32[512,768]{1,0:T(8,128)}, /*index=5*/f32[512,768]{1,0:T(8,128)S(1)}, bf16[3,384,768]{2,1,0:T(8,128)(2,1)}, ...), branch_computations={%region_26.27_spmd, %region_27.28_spmd} | conditional | bytes 29837312 | solution.py:789
  250.4 20.5 %collective-permute-done.11 = bf16[512,768]{1,0:T(8,128)(2,1)} collective-permute-done((bf16[512,768]{1,0:T(8,128)(2,1)S(1)}, bf16[512,768]{1,0:T(8,128)(2,1)}, u32[]{:S(2)}, u32[]{:S(2)}) %collective-permute-start.11) | collective-permute-done | bytes 786464 | tf_op jit(solution)/shard_map/cond/branch_1_fun/ppermute | solution.py:861
  282.9 28.9 %conditional.44 = (bf16[768,768]{1,0:T(8,128)(2,1)}, bf16[512,768]{1,0:T(8,128)(2,1)}, f32[512,768]{1,0:T(8,128)}, bf16[512,768]{1,0:T(8,128)(2,1)}, bf16[512,30...) conditional(s32[]{:T(128)} %bitcast.34, () %tuple.260, ...), branch_computations={%region_30.31_spmd, %region_31.34_spmd} | conditional | flops 2 | bytes 69318880 | solution.py:789
  284.5 18.7 %conditional.3 = (bf16[512,768]{1,0:T(8,128)(2,1)}, f32[512,768]{1,0:T(8,128)}, bf16[512,768]{1,0:T(8,128)(2,1)}, bf16[512,3072]{1,0:T(8,128)(2,1)}, f32[4,1,768...) conditional(s32[]{:T(128)} %bitcast.12, () %tuple.176, (f32[512,768]{1,0:T(8,128)}, ...), branch_computations={%region_32.32_spmd, %region_33.33_spmd} | conditional | bytes 64600056 | solution.py:789
  284.5 14.4 %ffn_backward.3 = (bf16[512,3072]{1,0:T(8,128)(2,1)}, f32[512,768]{1,0:T(8,128)}, bf16[512,768]{1,0:T(8,128)(2,1)}, bf16[512,768]{1,0:T(8,128)(2,1)}, f32[8,768]{1,0:T(8,128)}, /*index=5*/f32[4,1,768]{2,1,0:T(1,128)}) custom-call(f32[512,768]{1,0:T(8,128)} %get-tuple-element.774.refs_0_, bf16[512,768]{1,0:T(8,128)(2,1)S(1)} %get-tuple-element.775.refs_1_.r_ref, ...), custom_call_target="tpu_custom_call" | custom-call | bytes 51000000 | tf_op jit(solution)/shard_map/cond/branch_1_fun/cond/branch_1_fun/ffn_backward/pallas_call | solution.py:571
  311.8 59.0 %conditional.45 = (bf16[768,768]{1,0:T(8,128)(2,1)}, bf16[512,768]{1,0:T(8,128)(2,1)}, f32[512,768]{1,0:T(8,128)}, f32[512,768]{1,0:T(8,128)}, bf16[512,768]{1,0...) conditional(s32[]{:T(128)} %bitcast.34, () %tuple.259, ...), branch_computations={%region_34.35_spmd, %region_35.47_spmd} | conditional | flops 1916934 | bytes 176666656 | solution.py:789
  314.8 54.8 %conditional.8 = (bf16[512,768]{1,0:T(8,128)(2,1)}, f32[512,768]{1,0:T(8,128)}, f32[512,768]{1,0:T(8,128)}, bf16[512,768]{1,0:T(8,128)(2,1)}, bf16[512,768]{1,0:...) conditional(s32[]{:T(128)} %bitcast.15, () %tuple.198, ...), branch_computations={%region_37.37_spmd, %region_38.46_spmd} | conditional | flops 737284 | bytes 166049600 | solution.py:789
  328.3 36.5 %conditional.7 = (bf16[768,768]{1,0:T(8,128)(2,1)}, bf16[192,768]{1,0:T(8,128)(2,1)}, bf16[512,768]{1,0:T(8,128)(2,1)}, f32[512,768]{1,0:T(8,128)}, f32[512,768]...) conditional(s32[]{:T(128)} %bitcast.14, () %tuple.191, ...), branch_computations={%region_43.42_spmd, %region_44.45_spmd} | conditional | flops 2 | bytes 121498552 | solution.py:789
  330.5 34.3 %conditional.4 = (bf16[512,768]{1,0:T(8,128)(2,1)}, f32[512,768]{1,0:T(8,128)}, f32[512,768]{1,0:T(8,128)}, bf16[512,768]{1,0:T(8,128)(2,1)}, bf16[512,768]{1,0:...) conditional(s32[]{:T(128)} %bitcast.13, () %tuple.188, (s32[3]{0:T(128)}, ...), branch_computations={%region_45.43_spmd, %region_46.44_spmd} | conditional | bytes 115600056 | solution.py:789
  335.2 29.6 %attend_backward.2 = (bf16[512,768]{1,0:T(8,128)(2,1)}, f32[512,768]{1,0:T(8,128)}, f32[512,768]{1,0:T(8,128)}, bf16[512,768]{1,0:T(8,128)(2,1)}, bf16[512,768]{...) custom-call(s32[3]{0:T(128)} %get-tuple-element.829.refs_0_, bf16[512,768]{1,0:T(8,128)(2,1)} %get-tuple-element.830.refs_1_, ...), custom_call_target="tpu_custom_call" | custom-call | bytes 102000000 | tf_op jit(solution)/shard_map/cond/branch_1_fun/cond/branch_1_fun/cond/branch_1_fun/cond/branch_1_fun/attend_backward/pallas_call | solution.py:309
  370.8 122.5 %conditional.46 = (f32[1,768,768]{2,1,0:T(8,128)}, f32[1,3,192,768]{3,2,1,0:T(8,128)}, f32[1,2,256,768]{3,2,1,0:T(8,128)}, f32[1,2,192]{2,1,0:T(2,128)}, f32[1,7...) conditional(s32[]{:T(128)} %bitcast.34, () %tuple.258, ...), branch_computations={%region_47.48_spmd, %region_48.67_spmd} | conditional | flops 25134160 | bytes 116259976 | solution.py:789
  371.6 116.2 %conditional.16 = (f32[1,768,768]{2,1,0:T(8,128)}, f32[1,3,192,768]{3,2,1,0:T(8,128)}, f32[1,2,256,768]{3,2,1,0:T(8,128)}, f32[1,2,192]{2,1,0:T(2,128)}, f32[1,7...) conditional(s32[]{:T(128)} %bitcast.31, () %tuple.226, ...), branch_computations={%region_49.49_spmd, %region_50.64_spmd} | conditional | flops 23659598 | bytes 102987088 | solution.py:789
  371.6 18.4 %conditional.11 = (bf16[576,768]{1,0:T(8,128)(2,1)S(1)}, bf16[576,768]{1,0:T(8,128)(2,1)S(1)}, f32[512,768]{1,0:T(8,128)}, bf16[512,768]{1,0:T(8,128)(2,1)}, f32[6,1,384]{2,1,0:T(1,128)S(1)}) conditional(s32[]{:T(128)} %bitcast.29, () %tuple.218, (bf16[512,768]{1,0:T(8,128)(2,1)}, bf16[512,768]{1,0:T(8,128)(2,1)}, bf16[512,768]{1,0:T(8,128)(2,1)}, ...), branch_computations={%region_51.50_spmd, %region_52.51_spmd} | conditional | bytes 45010208 | solution.py:789
  392.0 25.0 %conditional.12 = (bf16[576,768]{1,0:T(8,128)(2,1)}, f32[2,2496]{1,0:T(2,128)}, f32[1,768,768]{2,1,0:T(8,128)}) conditional(s32[]{:T(128)} %bitcast.29, () %tuple.217, (bf16[576,768]{1,0:T(8,128)(2,1)S(1)}, s32[2]{0:T(128)S(1)}, f32[6,2,2,8,1792]{4,3,2,1,0:T(8,128)}, f32[1792,32]{1,0:T(8,128)S(1)}, f32[6,1,384]{2,1,0:T(1,128)S(1)}, ...), branch_computations={%region_53.52_spmd, %region_54.55_spmd} | conditional | flops 17513090 | bytes 11425746 | solution.py:789
  393.6 23.5 %conditional.9 = (f32[2,2496]{1,0:T(2,128)}, f32[1,768,768]{2,1,0:T(8,128)}) conditional(s32[]{:T(128)} %bitcast.20, () %tuple.208, (f32[6,2,2,8,1792]{4,3,2,1,0:T(8,128)}, f32[1792,32]{1,0:T(8,128)S(1)}, f32[6,1,384]{2,1,0:T(1,128)S(1)}, f32[4,1,768]{2,0,1:T(4,128)S(1)}, f32[8,768]{1,0:T(8,128)}, /*index=5*/f32[8,768]{1,0:T(8,128)S(1)}, ...), branch_computations={%region_55.53_spmd, %region_56.54_spmd} | conditional | flops 17513088 | bytes 7886660 | solution.py:789
  419.7 28.7 %conditional.13 = (bf16[288,768]{1,0:T(8,128)(2,1)}, f32[1,2,256,768]{3,2,1,0:T(8,128)}, f32[1,2,192]{2,1,0:T(2,128)}, f32[1,768]{1,0:T(1,128)}, f32[1,2,192]{2,...) conditional(s32[]{:T(128)} %bitcast.29, () %tuple.221, (pred[]{:T(512)}, ...), branch_computations={%region_57.56_spmd, %region_58.59_spmd} | conditional | flops 2386378 | bytes 19377796 | solution.py:789
  422.0 15.3 %conditional.10 = (f32[1,2,256,768]{3,2,1,0:T(8,128)}, f32[1,2,192]{2,1,0:T(2,128)}, f32[1,768]{1,0:T(1,128)}, f32[1,2,192]{2,1,0:T(2,128)}, f32[1,4,192]{2,1,0:T(4,128)}, /*index=5*/f32[1,3,64]{2,1,0:T(4,128)}) conditional(s32[]{:T(128)} %bitcast.28, () %tuple.214, (s32[]{:T(128)}, pred[]{:T(512)}, f32[512,768]{1,0:T(8,128)}, ...), branch_computations={%region_59.57_spmd, %region_60.58_spmd} | conditional | flops 2165192 | bytes 16281060 | solution.py:789
  449.5 22.2 %conditional.14 = (bf16[288,768]{1,0:T(8,128)(2,1)}) conditional(s32[]{:T(128)} %bitcast.29, () %tuple.223, bf16[288,768]{1,0:T(8,128)(2,1)S(1)} %select_add_fusion), branch_computations={%region_61.60_spmd, %region_62.61_spmd} | conditional | bytes 1769520 | solution.py:789
  450.1 21.6 %collective-permute-done.21 = bf16[288,768]{1,0:T(8,128)(2,1)} collective-permute-done((bf16[288,768]{1,0:T(8,128)(2,1)S(1)}, bf16[288,768]{1,0:T(8,128)(2,1)}, u32[]{:S(2)}, u32[]{:S(2)}) %collective-permute-start.21) | collective-permute-done | bytes 442400 | tf_op jit(solution)/shard_map/cond/branch_1_fun/cond/branch_1_fun/cond/branch_1_fun/ppermute | solution.py:977
  (287 shorter events, 381.4 us)
Async XLA Ops:
  11.2 21.9 %collective-permute-start.25 = (bf16[3,96,768]{2,1,0:T(8,128)(2,1)S(1)}, bf16[3,96,768]{2,1,0:T(8,128)(2,1)}, u32[]{:S(2)}, u32[]{:S(2)}) collective-permute-start(bf16[3,96,768]{2,1,0:T(8,128)(2,1)S(1)} %get-tuple-element.649), channel_id=1, source_target_pairs={{0,2},{2,0},{1,3},{3,1},{4,6},{6,4},{5,7},{7,5},{8,10},{10,8},{9,1... | collective-permute-start | bytes 1327112 | tf_op jit(solution)/shard_map/cond/branch_1_fun/ppermute | solution.py:38
  15.4 17.8 %collective-permute-start.24 = (bf16[256,768]{1,0:T(8,128)(2,1)S(1)}, bf16[256,768]{1,0:T(8,128)(2,1)}, u32[]{:S(2)}, u32[]{:S(2)}) collective-permute-start(bf16[256,768]{1,0:T(8,128)(2,1)S(1)} %dynamic-slice_bitcast_fusion.2), channel_id=1, source_target_pairs={{0,2},{2,0},{1,3},{3,1},{4,6},{6,4},{5,7},{7,5},{8,10},{10,8},{9,1... | collective-permute-start | bytes 1179656 | tf_op jit(solution)/shard_map/cond/branch_1_fun/ppermute | solution.py:38
  15.4 17.7 %collective-permute-start.23 = (f32[1344]{0:T(1024)S(1)}, f32[1344]{0:T(1024)}, u32[]{:S(2)}, u32[]{:S(2)}) collective-permute-start(f32[1344]{0:T(1024)S(1)} %get-tuple-element.646), channel_id=1, source_target_pairs={{0,2},{2,0},{1,3},{3,1},{4,6},{6,4},{5,7},{7,5},{8,10},{10,8},{9,1... | collective-permute-start | bytes 16136 | tf_op jit(solution)/shard_map/cond/branch_1_fun/ppermute | solution.py:38
  33.2 17.9 %collective-permute-start.37 = (bf16[384,768]{1,0:T(8,128)(2,1)S(1)}, bf16[384,768]{1,0:T(8,128)(2,1)}, u32[]{:S(2)}, u32[]{:S(2)}) collective-permute-start(bf16[384,768]{1,0:T(8,128)(2,1)S(1)} %get-tuple-element.665), channel_id=1, source_target_pairs={{0,2},{2,0},{1,3},{3,1},{4,6},{6,4},{5,7},{7,5},{8,10},{10,8},{9,1... | collective-permute-start | bytes 1769480 | tf_op jit(solution)/shard_map/cond/branch_1_fun/ppermute | solution.py:38
  35.0 16.0 %collective-permute-start.35 = (bf16[3,96,768]{2,1,0:T(8,128)(2,1)}, bf16[3,96,768]{2,1,0:T(8,128)(2,1)}, u32[]{:S(2)}, u32[]{:S(2)}) collective-permute-start(bf16[3,96,768]{2,1,0:T(8,128)(2,1)} %get-tuple-element.663), channel_id=1, source_target_pairs={{0,4},{4,0},{8,12},{12,8},{1,5},{5,1},{9,13},{13,9},{2,6},{6,2},{1... | collective-permute-start | bytes 1327112 | tf_op jit(solution)/shard_map/cond/branch_1_fun/ppermute | solution.py:767
  36.6 14.5 %collective-permute-start.36 = (bf16[96,768]{1,0:T(8,128)(2,1)S(1)}, bf16[96,768]{1,0:T(8,128)(2,1)}, u32[]{:S(2)}, u32[]{:S(2)}) collective-permute-start(bf16[96,768]{1,0:T(8,128)(2,1)S(1)} %get-tuple-element.664), channel_id=1, source_target_pairs={{0,2},{2,0},{1,3},{3,1},{4,6},{6,4},{5,7},{7,5},{8,10},{10,8},{9,1... | collective-permute-start | bytes 442376 | tf_op jit(solution)/shard_map/cond/branch_1_fun/ppermute | solution.py:38
  37.9 6.1 %collective-permute-start.34 = (f32[2,1344]{1,0:T(2,128)S(1)}, f32[2,1344]{1,0:T(2,128)S(1)}, u32[]{:S(2)}, u32[]{:S(2)}) collective-permute-start(f32[2,1344]{1,0:T(2,128)S(1)} %pad_maximum_fusion.8), channel_id=1, source_target_pairs={{0,1},{1,0},{2,3},{3,2},{4,5},{5,4},{6,7},{7,6},{8,9},{9,8},{10,11... | collective-permute-start | bytes 32264 | tf_op jit(solution)/shard_map/cond/branch_1_fun/cond/branch_1_fun/ppermute | solution.py:42
  52.1 19.9 %collective-permute-start.30 = (bf16[384,768]{1,0:T(8,128)(2,1)}, bf16[384,768]{1,0:T(8,128)(2,1)}, u32[]{:S(2)}, u32[]{:S(2)}) collective-permute-start(bf16[384,768]{1,0:T(8,128)(2,1)} %get-tuple-element.703), channel_id=1, source_target_pairs={{0,4},{4,0},{8,12},{12,8},{1,5},{5,1},{9,13},{13,9},{2,6},{6,2},{1... | collective-permute-start | bytes 1769480 | tf_op jit(solution)/shard_map/cond/branch_1_fun/ppermute | solution.py:767
  53.7 18.4 %collective-permute-start.28 = (bf16[384,768]{1,0:T(8,128)(2,1)S(1)}, bf16[384,768]{1,0:T(8,128)(2,1)}, u32[]{:S(2)}, u32[]{:S(2)}) collective-permute-start(bf16[384,768]{1,0:T(8,128)(2,1)S(1)} %get-tuple-element.701), channel_id=1, source_target_pairs={{0,2},{2,0},{1,3},{3,1},{4,6},{6,4},{5,7},{7,5},{8,10},{10,8},{9,1... | collective-permute-start | bytes 1769480 | tf_op jit(solution)/shard_map/cond/branch_1_fun/ppermute | solution.py:38
  55.2 16.9 %collective-permute-start.29 = (bf16[96,768]{1,0:T(8,128)(2,1)}, bf16[96,768]{1,0:T(8,128)(2,1)}, u32[]{:S(2)}, u32[]{:S(2)}) collective-permute-start(bf16[96,768]{1,0:T(8,128)(2,1)} %get-tuple-element.702), channel_id=1, source_target_pairs={{0,4},{4,0},{8,12},{12,8},{1,5},{5,1},{9,13},{13,9},{2,6},{6,2},{1... | collective-permute-start | bytes 442376 | tf_op jit(solution)/shard_map/cond/branch_1_fun/ppermute | solution.py:767
  77.4 21.3 %collective-permute-start.2 = (bf16[2,768,768]{2,1,0:T(8,128)(2,1)}, bf16[2,768,768]{2,1,0:T(8,128)(2,1)}, u32[]{:S(2)}, u32[]{:S(2)}) collective-permute-start(bf16[2,768,768]{2,1,0:T(8,128)(2,1)} %get-tuple-element.712), channel_id=1, source_target_pairs={{0,1},{1,0},{2,3},{3,2},{4,5},{5,4},{6,7},{7,6},{8,9},{9,8},{10,11... | collective-permute-start | bytes 7077896 | tf_op jit(solution)/shard_map/cond/branch_1_fun/ppermute | solution.py:42
  77.5 21.2 %collective-permute-start.1 = (bf16[384,768]{1,0:T(8,128)(2,1)S(1)}, bf16[384,768]{1,0:T(8,128)(2,1)}, u32[]{:S(2)}, u32[]{:S(2)}) collective-permute-start(bf16[384,768]{1,0:T(8,128)(2,1)S(1)} %get-tuple-element.711), channel_id=1, source_target_pairs={{0,1},{1,0},{2,3},{3,2},{4,5},{5,4},{6,7},{7,6},{8,9},{9,8},{10,11... | collective-permute-start | bytes 1769480 | tf_op jit(solution)/shard_map/cond/branch_1_fun/ppermute | solution.py:42
  77.9 20.8 %collective-permute-start = (bf16[384,768]{1,0:T(8,128)(2,1)}, bf16[384,768]{1,0:T(8,128)(2,1)}, u32[]{:S(2)}, u32[]{:S(2)}) collective-permute-start(bf16[384,768]{1,0:T(8,128)(2,1)} %get-tuple-element.710), channel_id=1, source_target_pairs={{0,4},{4,0},{8,12},{12,8},{1,5},{5,1},{9,13},{13,9},{2,6},{6,2},{1... | collective-permute-start | bytes 1769480 | tf_op jit(solution)/shard_map/cond/branch_1_fun/ppermute | solution.py:767
  118.9 14.2 %collective-permute-start.4 = (bf16[256,768]{1,0:T(8,128)(2,1)S(1)}, bf16[256,768]{1,0:T(8,128)(2,1)}, u32[]{:S(2)}, u32[]{:S(2)}) collective-permute-start(bf16[256,768]{1,0:T(8,128)(2,1)S(1)} %get-tuple-element.719), channel_id=1, source_target_pairs={{0,16},{1,17},{2,18},{3,19},{4,20},{5,21},{6,22},{7,23},{8,24},{9,... | collective-permute-start | bytes 1179656 | tf_op jit(solution)/shard_map/cond/branch_1_fun/ppermute | solution.py:858
  133.1 10.2 %collective-permute-start.5 = (bf16[256,768]{1,0:T(8,128)(2,1)S(1)}, bf16[256,768]{1,0:T(8,128)(2,1)}, u32[]{:S(2)}, u32[]{:S(2)}) collective-permute-start(bf16[256,768]{1,0:T(8,128)(2,1)S(1)} %param.19), channel_id=1, source_target_pairs={{0,16},{1,17},{2,18},{3,19},{4,20},{5,21},{6,22},{7,23},{8,24},{9,... | collective-permute-start | bytes 1179656 | tf_op jit(solution)/shard_map/cond/branch_1_fun/ppermute | solution.py:858
  156.3 19.9 %collective-permute-start.33 = (bf16[512,768]{1,0:T(8,128)(2,1)}, bf16[512,768]{1,0:T(8,128)(2,1)}, u32[]{:S(2)}, u32[]{:S(2)}) collective-permute-start(bf16[512,768]{1,0:T(8,128)(2,1)} %get-tuple-element.741), channel_id=1, source_target_pairs={{0,1},{1,0},{2,3},{3,2},{4,5},{5,4},{6,7},{7,6},{8,9},{9,8},{10,11... | collective-permute-start | bytes 2359304 | tf_op jit(solution)/shard_map/cond/branch_1_fun/ppermute | solution.py:42
  156.5 19.7 %collective-permute-start.32 = (bf16[256,768]{1,0:T(8,128)(2,1)S(1)}, bf16[256,768]{1,0:T(8,128)(2,1)}, u32[]{:S(2)}, u32[]{:S(2)}) collective-permute-start(bf16[256,768]{1,0:T(8,128)(2,1)S(1)} %dynamic-slice_bitcast_fusion.3), channel_id=1, source_target_pairs={{0,2},{2,0},{1,3},{3,1},{4,6},{6,4},{5,7},{7,5},{8,10},{10,8},{9,1... | collective-permute-start | bytes 1179656 | tf_op jit(solution)/shard_map/cond/branch_1_fun/ppermute | solution.py:38
  197.5 13.9 %collective-permute-start.7 = (bf16[512,1536]{1,0:T(8,128)(2,1)S(1)}, bf16[512,1536]{1,0:T(8,128)(2,1)}, u32[]{:S(2)}, u32[]{:S(2)}) collective-permute-start(bf16[512,1536]{1,0:T(8,128)(2,1)S(1)} %slice.114), channel_id=1, source_target_pairs={{0,1},{1,0},{2,3},{3,2},{4,5},{5,4},{6,7},{7,6},{8,9},{9,8},{10,11... | collective-permute-start | bytes 4718600 | tf_op jit(solution)/shard_map/cond/branch_1_fun/ppermute | solution.py:42
  197.7 13.7 %collective-permute-start.6 = (bf16[512,768]{1,0:T(8,128)(2,1)}, bf16[512,768]{1,0:T(8,128)(2,1)}, u32[]{:S(2)}, u32[]{:S(2)}) collective-permute-start(bf16[512,768]{1,0:T(8,128)(2,1)} %get-tuple-element.749), channel_id=1, source_target_pairs={{0,1},{1,0},{2,3},{3,2},{4,5},{5,4},{6,7},{7,6},{8,9},{9,8},{10,11... | collective-permute-start | bytes 2359304 | tf_op jit(solution)/shard_map/cond/branch_1_fun/ppermute | solution.py:42
  198.1 13.3 %collective-permute-start.8 = (bf16[512,384]{1,0:T(8,128)(2,1)S(1)}, bf16[512,384]{1,0:T(8,128)(2,1)}, u32[]{:S(2)}, u32[]{:S(2)}) collective-permute-start(bf16[512,384]{1,0:T(8,128)(2,1)S(1)} %slice.138), channel_id=1, source_target_pairs={{0,1},{1,0},{2,3},{3,2},{4,5},{5,4},{6,7},{7,6},{8,9},{9,8},{10,11... | collective-permute-start | bytes 1179656 | tf_op jit(solution)/shard_map/cond/branch_1_fun/ppermute | solution.py:42
  249.1 21.8 %collective-permute-start.11 = (bf16[512,768]{1,0:T(8,128)(2,1)S(1)}, bf16[512,768]{1,0:T(8,128)(2,1)}, u32[]{:S(2)}, u32[]{:S(2)}) collective-permute-start(bf16[512,768]{1,0:T(8,128)(2,1)S(1)} %get-tuple-element.773), channel_id=1, source_target_pairs={{16,0},{17,1},{18,2},{19,3},{20,4},{21,5},{22,6},{23,7},{24,8},{25... | collective-permute-start | bytes 2359304 | tf_op jit(solution)/shard_map/cond/branch_1_fun/ppermute | solution.py:861
  282.9 28.4 %collective-permute-start.13 = (bf16[768,768]{1,0:T(8,128)(2,1)}, bf16[768,768]{1,0:T(8,128)(2,1)}, u32[]{:S(2)}, u32[]{:S(2)}) collective-permute-start(bf16[768,768]{1,0:T(8,128)(2,1)} %get-tuple-element.794), channel_id=1, source_target_pairs={{0,2},{2,0},{1,3},{3,1},{4,6},{6,4},{5,7},{7,5},{8,10},{10,8},{9,1... | collective-permute-start | bytes 3538952 | tf_op jit(solution)/shard_map/cond/branch_1_fun/ppermute | solution.py:38
  311.8 59.0 %all-reduce.6.cloned.1.call-start = ((), (), s32[]{:S(2)}) async-start(), calls=%async_computation | async-start | bytes 2359296 | tf_op jit(solution)/shard_map/cond/branch_1_fun/psum | solution.py:1039
  328.3 36.5 %collective-permute-start.16 = (bf16[768,768]{1,0:T(8,128)(2,1)S(1)}, bf16[768,768]{1,0:T(8,128)(2,1)}, u32[]{:S(2)}, u32[]{:S(2)}) collective-permute-start(bf16[768,768]{1,0:T(8,128)(2,1)S(1)} %get-tuple-element.846), channel_id=1, source_target_pairs={{0,2},{2,0},{1,3},{3,1},{4,6},{6,4},{5,7},{7,5},{8,10},{10,8},{9,1... | collective-permute-start | bytes 3538952 | tf_op jit(solution)/shard_map/cond/branch_1_fun/cond/branch_1_fun/cond/branch_1_fun/ppermute | solution.py:38
  329.9 34.9 %collective-permute-start.17 = (bf16[192,768]{1,0:T(8,128)(2,1)S(1)}, bf16[192,768]{1,0:T(8,128)(2,1)}, u32[]{:S(2)}, u32[]{:S(2)}) collective-permute-start(bf16[192,768]{1,0:T(8,128)(2,1)S(1)} %get-tuple-element.847), channel_id=1, source_target_pairs={{0,2},{2,0},{1,3},{3,1},{4,6},{6,4},{5,7},{7,5},{8,10},{10,8},{9,1... | collective-permute-start | bytes 884744 | tf_op jit(solution)/shard_map/cond/branch_1_fun/cond/branch_1_fun/cond/branch_1_fun/ppermute | solution.py:38
  370.8 117.7 %all-reduce.8.cloned.1.call-start = ((), (), s32[]{:S(2)}) async-start(), calls=%async_computation.1 | async-start | bytes 2949120 | tf_op jit(solution)/shard_map/cond/branch_1_fun/psum | solution.py:1042
  392.0 25.0 %collective-permute-start.44 = (bf16[576,768]{1,0:T(8,128)(2,1)S(1)}, bf16[576,768]{1,0:T(8,128)(2,1)}, u32[]{:S(2)}, u32[]{:S(2)}) collective-permute-start(bf16[576,768]{1,0:T(8,128)(2,1)S(1)} %get-tuple-element.944), channel_id=1, source_target_pairs={{0,2},{2,0},{1,3},{3,1},{4,6},{6,4},{5,7},{7,5},{8,10},{10,8},{9,1... | collective-permute-start | bytes 2654216 | tf_op jit(solution)/shard_map/cond/branch_1_fun/cond/branch_1_fun/cond/branch_1_fun/ppermute | solution.py:38
  420.5 27.9 %collective-permute-start.40 = (bf16[288,768]{1,0:T(8,128)(2,1)}, bf16[288,768]{1,0:T(8,128)(2,1)}, u32[]{:S(2)}, u32[]{:S(2)}) collective-permute-start(bf16[288,768]{1,0:T(8,128)(2,1)} %broadcast_select_fusion.3), channel_id=1, source_target_pairs={{0,4},{4,0},{8,12},{12,8},{1,5},{5,1},{9,13},{13,9},{2,6},{6,2},{1... | collective-permute-start | bytes 1327112 | tf_op jit(solution)/shard_map/cond/branch_1_fun/cond/branch_1_fun/cond/branch_1_fun/ppermute | solution.py:767
  422.2 12.6 %collective-permute-start.38 = (bf16[256,768]{1,0:T(8,128)(2,1)S(1)}, bf16[256,768]{1,0:T(8,128)(2,1)S(1)}, u32[]{:S(2)}, u32[]{:S(2)}) collective-permute-start(bf16[256,768]{1,0:T(8,128)(2,1)S(1)} %dynamic-slice_bitcast_fusion.4), channel_id=1, source_target_pairs={{0,2},{2,0},{1,3},{3,1},{4,6},{6,4},{5,7},{7,5},{8,10},{10,8},{9,1... | collective-permute-start | bytes 1179656 | tf_op jit(solution)/shard_map/cond/branch_1_fun/cond/branch_1_fun/cond/branch_1_fun/cond/branch_1_fun/ppermute | solution.py:38
  423.4 7.9 %collective-permute-start.39 = (f32[2496]{0:T(1024)S(1)}, f32[2496]{0:T(1024)S(1)}, u32[]{:S(2)}, u32[]{:S(2)}) collective-permute-start(f32[2496]{0:T(1024)S(1)} %get-tuple-element.1445), channel_id=1, source_target_pairs={{0,2},{2,0},{1,3},{3,1},{4,6},{6,4},{5,7},{7,5},{8,10},{10,8},{9,1... | collective-permute-start | bytes 29960 | tf_op jit(solution)/shard_map/cond/branch_1_fun/cond/branch_1_fun/cond/branch_1_fun/cond/branch_1_fun/ppermute | solution.py:38
  449.6 22.1 %collective-permute-start.21 = (bf16[288,768]{1,0:T(8,128)(2,1)S(1)}, bf16[288,768]{1,0:T(8,128)(2,1)}, u32[]{:S(2)}, u32[]{:S(2)}) collective-permute-start(bf16[288,768]{1,0:T(8,128)(2,1)S(1)} %param.59), channel_id=1, source_target_pairs={{0,8},{8,0},{4,12},{12,4},{1,9},{9,1},{5,13},{13,5},{2,10},{10,2},... | collective-permute-start | bytes 1327112 | tf_op jit(solution)/shard_map/cond/branch_1_fun/cond/branch_1_fun/cond/branch_1_fun/ppermute | solution.py:977
  472.8 12.3 %collective-permute-start.22 = (bf16[288,768]{1,0:T(8,128)(2,1)S(1)}, bf16[288,768]{1,0:T(8,128)(2,1)}, u32[]{:S(2)}, u32[]{:S(2)}) collective-permute-start(bf16[288,768]{1,0:T(8,128)(2,1)S(1)} %param.61), channel_id=1, source_target_pairs={{0,4},{4,0},{8,12},{12,8},{1,5},{5,1},{9,13},{13,9},{2,6},{6,2},{1... | collective-permute-start | bytes 1327112 | tf_op jit(solution)/shard_map/cond/branch_1_fun/cond/branch_1_fun/cond/branch_1_fun/ppermute | solution.py:767
  (41 other events, 291.7 us)
Sparse Core Ops, SparseCore 0:
  315.6 55.1 all-reduce.5
  374.1 72.7 all-reduce.7
